TPU v7x, 32 devices: a whole 2x2x4 slice. The times are simulated.
32 devices in a mesh: dp: 8 (over z, x), expert: 4 (over y, core).
Axes of the slice: x: 2, y: 2, z: 4, core: 2. Of those that a mesh axis runs over, the one named last changes fastest.
Arguments:
- text_embed: bfloat16 [2048, 2048], P(('dp', 'expert')), may hold values from -6 to 6
- image_feats: bfloat16 [1024, 4608], P(('dp', 'expert')), may hold values from -6 to 6
- tile_pos: int32 [1024], P(('dp', 'expert')), may hold values from 0 to 2047, as said below
- proj_in: bfloat16 [4608, 2048], P(None, 'expert'), may hold values from -0.09375 to 0.09375
- proj_out: bfloat16 [2048, 2048], P('expert'), may hold values from -0.125 to 0.125
- norm_gain: float32 [2048], replicated, may hold values from 0.1 to 1.9
- shared_gate: bfloat16 [2048, 2816], P(None, 'expert'), may hold values from -0.125 to 0.125
- shared_up: bfloat16 [2048, 2816], P(None, 'expert'), may hold values from -0.125 to 0.125
- shared_down: bfloat16 [2816, 2048], P('expert'), may hold values from -0.109375 to 0.109375
- expert_gate: bfloat16 [8, 2048, 1408], P('dp', None, 'expert'), may hold values from -0.125 to 0.125
- expert_up: bfloat16 [8, 2048, 1408], P('dp', None, 'expert'), may hold values from -0.125 to 0.125
- expert_down: bfloat16 [8, 1408, 2048], P('dp', 'expert'), may hold values from -0.15625 to 0.15625
- route_ids: int32 [2048, 2], P(('dp', 'expert')), may hold values from 0 to 7, all different within a row; in each aligned block of 256 rows (0 to 255, 256 to 511, ...) at most 96 rows name the same one
- route_wts: int32 [2048, 2], P(('dp', 'expert')), may hold values from 1 to 65535
Outputs:
- block_out: bfloat16 [2048, 2048], P(('dp', 'expert'))
Inputs may be any that keep to these rules, and one draw needn't show every extreme that they name: `tile_pos`: positions are distinct. The 32 image tokens of one device go 4 to each index of dp, always to rows held by the devices with the sender's own index of expert. `route_ids`: in each aligned block of 256 rows no expert is named by more than 96 rows, a bound that some block reaches.
All inputs are finite; a program needn't handle non-finite values.
Results may differ from a plain program's by a relative error of at most 0.018.
Values may be sent and summed in bfloat16 or wider, within the bound.
No kernel may reach another device: no remote copies, remote signals or barrier semaphores. Data moves between devices by JAX's collectives and lax.ppermute only.
A program may use at most 128 MiB of HBM per device.

v0:
```python
import jax
import jax.numpy as jnp
from jax import lax
from jax.sharding import PartitionSpec as P


def normalize(rows, norm_gain):
    rows_f = rows.astype(jnp.float32)
    meansq = jnp.mean(rows_f * rows_f, axis=-1, keepdims=True) + 1e-06
    return (rows_f * lax.rsqrt(meansq) * norm_gain).astype(jnp.bfloat16)


def project_part(feats, proj_in, proj_out):
    vis_hidden = jax.nn.gelu(
        jnp.dot(feats, proj_in, preferred_element_type=jnp.float32), approximate=True
    ).astype(jnp.bfloat16)
    return jnp.dot(vis_hidden, proj_out, preferred_element_type=jnp.float32)


def shards(
    text_embed,
    image_feats,
    tile_pos,
    proj_in,
    proj_out,
    norm_gain,
    shared_gate,
    shared_up,
    shared_down,
    expert_gate,
    expert_up,
    expert_down,
    route_ids,
    route_wts,
):
    tok_dev = text_embed.shape[0]
    img_dev = image_feats.shape[0]
    width_model = text_embed.shape[1]
    n_data = lax.axis_size("dp")
    n_group = lax.axis_size("expert")
    peer = img_dev // n_data
    my_place = lax.axis_index("expert")
    owner = tile_pos // tok_dev
    dest_index = owner // n_group
    order = jnp.argsort(dest_index, stable=True)
    sorted_feats = image_feats[order].reshape(n_data, peer, image_feats.shape[1])
    sorted_offs = (tile_pos[order] % tok_dev).reshape(n_data, peer)
    moved_feats, moved_offs = (
        lax.all_to_all(sorted_feats, "dp", split_axis=0, concat_axis=0, tiled=True),
        lax.all_to_all(sorted_offs, "dp", split_axis=0, concat_axis=0, tiled=True),
    )
    moved_feats = moved_feats.reshape(img_dev, image_feats.shape[1])
    moved_offs = moved_offs.reshape(img_dev)
    texts, feats, offsets, ids, weights = (
        lax.all_gather(text_embed, "expert", axis=0, tiled=True),
        lax.all_gather(moved_feats, "expert", axis=0, tiled=True),
        lax.all_gather(moved_offs, "expert", axis=0, tiled=True),
        lax.all_gather(route_ids, "expert", axis=0, tiled=True),
        lax.all_gather(route_wts, "expert", axis=0, tiled=True),
    )
    partial_value = project_part(feats, proj_in, proj_out)
    projected = lax.psum(partial_value.astype(jnp.bfloat16), "expert")
    block_start = jnp.arange(offsets.shape[0], dtype=jnp.int32) // img_dev * tok_dev
    embed_group = texts.at[offsets + block_start].set(projected)
    normed = normalize(embed_group, norm_gain)
    own_rows = lax.dynamic_slice_in_dim(embed_group, my_place * tok_dev, tok_dev, 0)
    gate_s = jnp.dot(normed, shared_gate, preferred_element_type=jnp.float32)
    up_s = jnp.dot(normed, shared_up, preferred_element_type=jnp.float32)
    shared_hidden = (jax.nn.silu(gate_s) * up_s).astype(jnp.bfloat16)
    group_rows = normed.shape[0]
    top_count = ids.shape[1]
    capacity = 3 * group_rows * top_count // (2 * n_data)
    share = capacity // n_group
    flat_ids = ids.reshape(-1)
    onehot = (flat_ids[:, None] == jnp.arange(n_data, dtype=jnp.int32)[None, :]).astype(jnp.int32)
    rank = jnp.sum(jnp.cumsum(onehot, axis=0) * onehot, axis=1) - 1
    pair_token = jnp.arange(group_rows * top_count, dtype=jnp.int32) // top_count
    send = (
        jnp.zeros((n_data, capacity, width_model), jnp.bfloat16)
        .at[flat_ids, rank]
        .set(normed[pair_token])
    )
    slots = lax.all_to_all(send, "dp", split_axis=0, concat_axis=0, tiled=True)
    gate_e = jnp.einsum("ncd,df->ncf", slots, expert_gate[0], preferred_element_type=jnp.float32)
    up_e = jnp.einsum("ncd,df->ncf", slots, expert_up[0], preferred_element_type=jnp.float32)
    hidden_e = (jax.nn.silu(gate_e) * up_e).astype(jnp.bfloat16)
    partial_out = jnp.einsum(
        "ncf,fd->ncd", hidden_e, expert_down[0], preferred_element_type=jnp.float32
    )
    summed = lax.psum_scatter(
        partial_out.astype(jnp.bfloat16), "expert", scatter_dimension=1, tiled=True
    )
    returned = lax.all_to_all(summed, "dp", split_axis=0, concat_axis=0, tiled=True)
    inside = rank // share == my_place
    local_slot = jnp.where(inside, rank - my_place * share, 0)
    picked = returned.reshape(n_data * share, width_model)[flat_ids * share + local_slot]
    weights_f = weights.astype(jnp.float32)
    weights_n = weights_f / jnp.sum(weights_f, axis=1, keepdims=True)
    coef = jnp.where(inside, weights_n.reshape(-1), 0.0)
    combined = jnp.sum(
        (picked.astype(jnp.float32) * coef[:, None]).reshape(group_rows, top_count, width_model),
        axis=1,
    )
    total = lax.psum_scatter(
        (jnp.dot(shared_hidden, shared_down, preferred_element_type=jnp.float32) + combined).astype(
            jnp.bfloat16
        ),
        "expert",
        scatter_dimension=0,
        tiled=True,
    ).astype(jnp.float32)
    return (own_rows.astype(jnp.float32) + total).astype(jnp.bfloat16)


def solution(mesh):
    return jax.shard_map(
        shards,
        mesh=mesh,
        in_specs=(
            P(("dp", "expert"), None),
            P(("dp", "expert"), None),
            P(("dp", "expert")),
            P(None, "expert"),
            P("expert", None),
            P(),
            P(None, "expert"),
            P(None, "expert"),
            P("expert", None),
            P("dp", None, "expert"),
            P("dp", None, "expert"),
            P("dp", "expert", None),
            P(("dp", "expert"), None),
            P(("dp", "expert"), None),
        ),
        out_specs=P(("dp", "expert"), None),
        check_vma=False,
    )
```

profile of v0, /device:TPU:0, one launch (start us, length us, event | category | flops | bytes accessed | tf_op | source)
XLA Modules:
  0.0 426.1 jit_solution(16760553065638043584)
XLA Ops:
  6.5 0.8 and_select_fusion.3
  7.4 1.6 sort.17
  9.0 2.0 gather_fusion.1
  11.0 0.1 reshape.279
  11.1 17.4 %all_to_all.21 = bf16[8,4,4608]{2,1,0:T(4,128)(2,1)S(1)} all-to-all(bf16[8,4,4608]{2,1,0:T(4,128)(2,1)S(1)} %reshape.279), channel_id=1, replica_groups=mesh['dp'=8,'expert'=4] {'dp'}, dimensions={0} | all-to-all | bytes 589824 | tf_op jit(solution)/shard_map/all_to_all | solution.py:49
  28.5 0.8 reshape.280
  29.3 0.0 all-gather.5.cloned.1.call-start
  29.4 0.7 all-gather.5.cloned.1.call-update
  30.1 0.7 gather_fusion
  30.8 0.1 gather.15
  30.9 0.6 add_select_fusion.1
  31.5 3.3 all-to-all-start
  34.8 0.0 all-reduce.3.cloned.1.call-start
  34.9 5.1 %all-gather = s32[4,64,2]{1,2,0:T(2,128)S(1)} all-gather(s32[1,64,2]{1,2,0:T(2,128)S(1)} %bitcast.71), channel_id=1, replica_groups=mesh['dp'=8,'expert'=4] {'expert'}, dimensions={0}, use_global_device_ids=true | all-gather | bytes 2560 | tf_op jit(solution)/shard_map/all_gather | solution.py:58
  39.9 0.1 copy.22
  40.0 0.1 copy.24
  40.2 0.1 eq.47
  40.3 0.1 reshape.281
  40.5 0.1 copy.25
  40.5 1.2 reduce-window.6
  41.7 0.2 slice_reduce_fusion
  42.0 0.1 fusion.35
  42.1 3.2 all-gather.7.cloned.1.call-done
  45.3 5.4 %convolution_convert_fusion.1 = bf16[128,2048]{1,0:T(8,128)(2,1)} fusion(bf16[512,2048]{1,0:T(8,128)(2,1)} %param.18, bf16[128,4608]{1,0:T(8,128)(2,1)} %all-gather.7.cloned.1.call-done, bf16[4608,512]{1,0:T(8,128)(2,1)} %param.17), kind=kOutput, calls=%fused_computation.12 | convolution fusion | flops 873267200 | bytes 8519680 | tf_op jit(solution)/shard_map/dot_general | solution.py:17
  50.7 0.0 all-reduce.3.cloned.1.call-update
  50.7 0.0 reduce-scatter.7.cloned.1.call-start
  50.8 0.7 dynamic-slice
  52.2 0.5 broadcast.402
  52.7 0.7 reduce.7
  53.3 0.1 reshape.334
  53.4 0.2 dynamic-update-slice
  53.6 4.3 all-reduce
  57.9 5.8 %all-gather.5.cloned.1.call-done = bf16[256,2048]{1,0:T(8,128)(2,1)} async-done(((bf16[64,2048]{1,0:T(8,128)(2,1)}), bf16[256,2048]{1,0:T(8,128)(2,1)}) %all-gather.5.cloned.1.call-update) | async-done | bytes 1048592 | tf_op jit(solution)/shard_map/all_gather | solution.py:55
  63.7 35.6 %all-reduce.3.cloned.1.call-done = bf16[128,2048]{1,0:T(8,128)(2,1)} async-done(((bf16[128,2048]{1,0:T(8,128)(2,1)}), bf16[128,2048]{1,0:T(8,128)(2,1)}) %all-reduce.3.cloned.1.call-update) | async-done | bytes 524304 | tf_op jit(solution)/shard_map/psum | solution.py:62
  99.3 4.2 scatter_fusion
  103.5 1.5 fusion.1
  105.0 2.5 fusion.3
  107.6 6.6 %gather_fusion.2 = bf16[512,2048]{1,0:T(8,128)(2,1)} fusion(bf16[256,2048]{1,0:T(8,128)(2,1)} %fusion.3, s32[1024]{0:T(1024)S(1)} %pad_clamp_fusion.1), kind=kCustom, calls=%fused_computation.2 | custom fusion | bytes 4196352 | tf_op jit(solution)/shard_map/gather | solution.py:81
  114.2 2.1 broadcast_in_dim.13
  116.2 91.8 %scatter_fusion.1 = bf16[8,96,2048]{2,1,0:T(8,128)(2,1)} fusion(bf16[8,96,2048]{2,1,0:T(8,128)(2,1)} %broadcast_in_dim.13, s32[512]{0:T(512)S(1)} %bitcast.62, bf16[512,2048]{1,0:T(8,128)(2,1)} %gather_fusion.2), kind=kCustom, calls=%fused_computation.5 | custom fusion | bytes 6295552 | tf_op jit(solution)/shard_map/scatter | solution.py:81
  208.0 75.7 %all_to_all.22 = bf16[8,96,2048]{2,1,0:T(8,128)(2,1)S(1)} all-to-all(bf16[8,96,2048]{2,1,0:T(8,128)(2,1)} %scatter_fusion.1), channel_id=1, replica_groups=mesh['dp'=8,'expert'=4] {'dp'}, dimensions={0} | all-to-all | bytes 6291456 | tf_op jit(solution)/shard_map/all_to_all | solution.py:83
  283.8 1.7 copy-done.2
  285.5 2.8 fusion.7
  288.3 8.2 %fusion.49 = bf16[12,8,8,2048]{3,1,0,2:T(8,128)(2,1)} fusion(bf16[1,352,2048]{2,1,0:T(8,128)(2,1)} %param.25, bf16[8,96,2048]{2,1,0:T(8,128)(2,1)} %copy-done.2, bf16[1,2048,352]{1,2,0:T(8,128)(2,1)} %param.24, f32[8,96,352]{2,1,0:T(8,128)} %fusion.7), kind=kOutput, calls=%fused_computation.103 | convolution fusion | flops 2217787392 | bytes 10256384 | tf_op jit(solution)/shard_map/ncf,fd->ncd/dot_general | solution.py:87
  296.5 4.0 copy.32
  300.5 36.1 %reduce-scatter.7.cloned.1.call-done = bf16[24,16384]{1,0:T(8,128)(2,1)} async-done(((bf16[96,16384]{1,0:T(8,128)(2,1)}), bf16[24,16384]{1,0:T(8,128)(2,1)}) %reduce-scatter.7.cloned.1.call-update) | async-done | bytes 786448
  336.6 1.6 copy.33
  338.2 1.3 copy.30
  339.5 5.5 %all-to-all-start.3 = ((bf16[8,24,2048]{2,1,0:T(8,128)(2,1)}), bf16[8,24,2048]{2,1,0:T(8,128)(2,1)}, u32[]{:S(2)}, u32[]{:S(2)}) async-start(bf16[8,24,2048]{2,1,0:T(8,128)(2,1)} %copy.30), calls=%async_computation.3 | async-start | bytes 1572864 | tf_op jit(solution)/shard_map/all_to_all | solution.py:93
  345.0 0.0 reduce-scatter.5.cloned.1.call-start
  345.1 0.1 div.94
  345.2 0.2 and.78
  345.4 5.1 %all-gather.1 = s32[4,64,2]{1,2,0:T(2,128)S(1)} all-gather(s32[1,64,2]{1,2,0:T(2,128)S(1)} %bitcast.72), channel_id=1, replica_groups=mesh['dp'=8,'expert'=4] {'expert'}, dimensions={0}, use_global_device_ids=true | all-gather | bytes 2560 | tf_op jit(solution)/shard_map/all_gather | solution.py:59
  350.5 0.1 copy.28
  350.6 0.1 reshape.347
  350.7 0.1 fusion.30
  350.8 4.0 fusion.56
  354.8 10.5 %all-to-all-done.3 = bf16[8,24,2048]{2,1,0:T(8,128)(2,1)} async-done(((bf16[8,24,2048]{2,1,0:T(8,128)(2,1)}), bf16[8,24,2048]{2,1,0:T(8,128)(2,1)}, u32[]{:S(2)}, u32[]{:S(2)}) %all-to-all-start.3) | async-done | bytes 786464 | tf_op jit(solution)/shard_map/all_to_all | solution.py:93
  365.3 6.5 %gather_fusion.3 = bf16[512,2048]{1,0:T(8,128)(2,1)} fusion(bf16[192,2048]{1,0:T(8,128)(2,1)} %bitcast.16, s32[1024]{0:T(1024)S(1)} %pad_clamp_fusion), kind=kCustom, calls=%fused_computation.3 | custom fusion | bytes 4196352 | tf_op jit(solution)/shard_map/gather | solution.py:96
  371.8 5.4 %reshape.284 = f32[256,2,2048]{2,1,0:T(2,128)} reshape(bf16[512,2048]{1,0:T(8,128)(2,1)} %gather_fusion.3) | data formatting | bytes 6291456 | tf_op jit(solution)/shard_map/convert_element_type | solution.py:101
  377.3 10.1 %multiply_reduce_fusion = f32[256,2048]{1,0:T(8,128)} fusion(f32[256,2,2048]{2,1,0:T(2,128)} %reshape.284, f32[256,2]{1,0:T(8,128)S(1)} %fusion.30), kind=kLoop, calls=%fused_computation.6 | loop fusion | flops 1572864 | bytes 6293504 | tf_op jit(solution)/shard_map/reduce_sum | solution.py:100
  387.4 7.3 %fusion = bf16[256,2048]{1,0:T(8,128)(2,1)} fusion(f32[256,2048]{1,0:T(8,128)} %multiply_reduce_fusion, bf16[704,2048]{1,0:T(8,128)(2,1)S(1)} %copy-done, bf16[256,2048]{1,0:T(8,128)(2,1)} %fusion.3, bf16[2048,704]{0,1:T(8,128)(2,1)} %param.21, f32[256,704]{0,1:T(8,128)} %fusion.56), kind=kOutput, calls=%fused_computation.11 | convolution fusion | flops 1478524928 | bytes 10682368 | tf_op jit(solution)/shard_map/dot_general | solution.py:105
  394.7 23.1 %reduce-scatter.5.cloned.1.call-done = bf16[64,2048]{1,0:T(8,128)(2,1)} async-done(((bf16[256,2048]{1,0:T(8,128)(2,1)}), bf16[64,2048]{1,0:T(8,128)(2,1)}) %reduce-scatter.5.cloned.1.call-update) | async-done | bytes 262160 | tf_op jit(solution)/shard_map/reduce_scatter | solution.py:104
  417.8 1.8 add_convert_fusion
  (37 shorter events, 0.3 us)
Async XLA Ops:
  6.5 380.8 %copy-start = (bf16[704,2048]{1,0:T(8,128)(2,1)S(1)}, bf16[704,2048]{1,0:T(8,128)(2,1)}, u32[]{:S(2)}) copy-start(bf16[704,2048]{1,0:T(8,128)(2,1)} %param.22) | copy-start | bytes 8650756
  6.5 38.7 %all-gather.7.cloned.1.call-start = ((), (), s32[]{:S(2)}) async-start(), calls=%async_computation.7 | async-start | bytes 1474560 | tf_op jit(solution)/shard_map/all_gather | solution.py:56
  9.0 21.1 %copy-start.1 = (s32[32]{0:T(128)S(1)}, s32[32]{0:T(128)}, u32[]{:S(2)}) copy-start(s32[32]{0:T(128)} %param.16) | copy-start | bytes 388
  11.0 23.8 %copy-start.4 = (s32[64,2]{0,1:T(2,128)S(1)}, s32[64,2]{0,1:T(2,128)}, u32[]{:S(2)}) copy-start(s32[64,2]{0,1:T(2,128)} %param.26) | copy-start | bytes 1540
  29.3 34.4 %all-gather.5.cloned.1.call-start = ((), (), s32[]{:S(2)}) async-start(), calls=%async_computation.6 | async-start | bytes 1310720 | tf_op jit(solution)/shard_map/all_gather | solution.py:55
  31.5 20.7 %all-to-all-start = ((s32[8,1,4]{2,1,0:T(1,128)}), s32[8,1,4]{2,1,0:T(1,128)S(1)}, u32[]{:S(2)}, u32[]{:S(2)}) async-start(s32[8,1,4]{2,1,0:T(1,128)} %bitcast), calls=%async_computation | async-start | bytes 8192 | tf_op jit(solution)/shard_map/all_to_all | solution.py:50
  34.8 64.5 %all-reduce.3.cloned.1.call-start = ((), (), s32[]{:S(2)}) async-start(), calls=%async_computation.8 | async-start | bytes 1048576 | tf_op jit(solution)/shard_map/psum | solution.py:62
  42.1 8.7 %copy-start.7 = (u32[32]{0:T(128)S(1)}, u32[32]{0:T(128)}, u32[]{:S(2)}) copy-start(u32[32]{0:T(128)} %constant.144) | copy-start | bytes 388
  50.7 285.9 %reduce-scatter.7.cloned.1.call-start = ((), (), s32[]{:S(2)}) async-start(), calls=%async_computation.10 | async-start | bytes 3932160
  57.9 47.1 %copy-start.3 = (f32[2048]{0:T(1024)S(1)}, f32[2048]{0:T(1024)}, u32[]{:S(2)}) copy-start(f32[2048]{0:T(1024)} %param.19) | copy-start | bytes 24580
  208.0 77.5 %copy-start.6 = (bf16[1,2048,352]{1,2,0:T(8,128)(2,1)S(1)}, bf16[1,2048,352]{1,2,0:T(8,128)(2,1)}, u32[]{:S(2)}) copy-start(bf16[1,2048,352]{1,2,0:T(8,128)(2,1)} %param.23) | copy-start | bytes 4325380
  283.8 1.7 copy-start.2
  336.6 8.8 %copy-start.5 = (s32[64,2]{0,1:T(2,128)S(1)}, s32[64,2]{0,1:T(2,128)}, u32[]{:S(2)}) copy-start(s32[64,2]{0,1:T(2,128)} %param.27) | copy-start | bytes 1540
  339.5 25.8 %all-to-all-start.3 = ((bf16[8,24,2048]{2,1,0:T(8,128)(2,1)}), bf16[8,24,2048]{2,1,0:T(8,128)(2,1)}, u32[]{:S(2)}, u32[]{:S(2)}) async-start(bf16[8,24,2048]{2,1,0:T(8,128)(2,1)} %copy.30), calls=%async_computation.3 | async-start | bytes 1572864 | tf_op jit(solution)/shard_map/all_to_all | solution.py:93
  345.0 72.8 %reduce-scatter.5.cloned.1.call-start = ((), (), s32[]{:S(2)}) async-start(), calls=%async_computation.9 | async-start | bytes 1310720 | tf_op jit(solution)/shard_map/reduce_scatter | solution.py:104
Sparse Core Ops, SparseCore 0:
  29.4 15.7 all-gather.6
  46.8 16.8 all-gather.4
  66.0 33.1 all-reduce.2
  300.6 35.9 reduce-scatter.6
  394.8 22.9 reduce-scatter.4
where the time goes:
time: 429 us; the launch traced here: 426 us
  local copies, waits for them, and re-layouts  132 us (31%)
  waiting for transfers between devices  115 us (27%)
  blocking collectives  108 us (25%)
  matrix products  27.7 us (6%)
  other arithmetic  21.2 us (5%)
  between operations  14.1 us (3%)
  starting transfers between devices  8.98 us (2%)
    scatter x1, local copies, waits for them, and re-layouts, shards(): send = jnp.zeros((n_data, capacity, width_model), jnp.bfloat16).at[flat_i...  91.8 us
    all_to_all x1, blocking collectives, shards(): slots = lax.all_to_all(send, 'dp', split_axis=0, concat_axis=0, tiled=True)  75.7 us
    unnamed x6, waiting for transfers between devices  36.8 us
    psum x1, waiting for transfers between devices, shards(): projected = lax.psum(partial_value.astype(jnp.bfloat16), 'expert')  35.6 us
    reduce_scatter x1, waiting for transfers between devices, shards(): lax.psum_scatter((jnp.dot(shared_hidden, shared_down, preferred_element_t...  23.1 us
    all_to_all x1, blocking collectives, shards(): lax.all_to_all(sorted_feats, 'dp', split_axis=0, concat_axis=0, tiled=True)  17.4 us
    all_to_all x1, waiting for transfers between devices, shards(): lax.all_to_all(summed, 'dp', split_axis=0, concat_axis=0, tiled=True)  10.5 us
    reduce_sum x1, other arithmetic, shards(): jnp.sum((picked.astype(jnp.float32) * coef[:, None]).reshape(group_rows,...  10.1 us
  transfers between devices with their start and end apart: 7, of which 6 were waited for; matrix products, arithmetic and copies ran while one was open for 4% of the time, Pallas kernels for 0%

commit v1 on v0

v1 whole, which is shorter than its diff:
```python
import jax
import jax.numpy as jnp
from jax import lax
from jax.sharding import PartitionSpec as P

BF = jnp.bfloat16
F32 = jnp.float32


def dot(a, b):
    return jnp.dot(a, b, preferred_element_type=F32)


def swap(rows, axis, mask):
    count = lax.axis_size(axis)
    return lax.ppermute(rows, axis, [(i, i ^ mask) for i in range(count)])


def gather_blocks(block, axis):
    count = lax.axis_size(axis)
    me = lax.axis_index(axis)
    held = block[None]
    mask = count // 2
    while mask:
        other = swap(held, axis, mask)
        low = (me & mask) == 0
        first = jnp.where(low, held, other)
        second = jnp.where(low, other, held)
        held = jnp.stack([first, second], axis=1).reshape((-1,) + block.shape)
        mask //= 2
    return held


def scatter_sum(parts, axis):
    count = lax.axis_size(axis)
    me = lax.axis_index(axis)
    held = parts
    mask = 1
    while mask < count:
        pairs = held.reshape((held.shape[0] // 2, 2) + held.shape[1:])
        bit = (me // mask) & 1
        keep = lax.dynamic_index_in_dim(pairs, bit, 1, keepdims=False)
        give = lax.dynamic_index_in_dim(pairs, 1 - bit, 1, keepdims=False)
        held = (keep.astype(F32) + swap(give, axis, mask).astype(F32)).astype(BF)
        mask *= 2
    return held[0]


def one_hot(places, count):
    return places[None, :] == jnp.arange(count, dtype=jnp.int32)[:, None]


def shards(
    text_embed,
    image_feats,
    tile_pos,
    proj_in,
    proj_out,
    norm_gain,
    shared_gate,
    shared_up,
    shared_down,
    expert_gate,
    expert_up,
    expert_down,
    route_ids,
    route_wts,
):
    tok_dev, width = text_embed.shape
    img_dev = image_feats.shape[0]
    n_data = lax.axis_size("dp")
    n_group = lax.axis_size("expert")
    peer = img_dev // n_data
    my_place = lax.axis_index("expert")
    top = route_ids.shape[1]
    group_rows = tok_dev * n_group
    capacity = 3 * group_rows * top // (2 * n_data)
    share = capacity // n_group

    feats = gather_blocks(image_feats, "expert").reshape(n_group * img_dev, -1)
    vis_hidden = jax.nn.gelu(dot(feats, proj_in), approximate=True).astype(BF)
    part = dot(vis_hidden, proj_out).astype(BF)
    projected = scatter_sum(part.reshape(n_group, img_dev, width), "expert")

    owner = tile_pos // tok_dev // n_group
    earlier = jnp.arange(img_dev)[None, :] < jnp.arange(img_dev)[:, None]
    rank_img = jnp.sum(((owner[:, None] == owner[None, :]) & earlier).astype(jnp.int32), axis=1)
    place = one_hot(owner * peer + rank_img, img_dev).astype(BF)
    offsets = jnp.broadcast_to((tile_pos % tok_dev).astype(BF)[:, None], (img_dev, 128))
    leaving = dot(place, jnp.concatenate([projected, offsets], axis=1)).astype(BF)
    arrived = lax.all_to_all(
        leaving.reshape(n_data, peer, width + 128), "dp", split_axis=0, concat_axis=0, tiled=True
    ).reshape(img_dev, width + 128)
    spots = one_hot(arrived[:, width].astype(jnp.int32), tok_dev)
    image_rows = dot(spots.astype(BF), arrived[:, :width]).astype(BF)
    embed = jnp.where(jnp.any(spots, axis=1, keepdims=True), image_rows, text_embed)

    embed_f = embed.astype(F32)
    meansq = jnp.mean(embed_f * embed_f, axis=-1, keepdims=True) + 1e-06
    normed_own = (embed_f * lax.rsqrt(meansq) * norm_gain).astype(BF)
    normed = gather_blocks(normed_own, "expert").reshape(group_rows, width)

    routes = gather_blocks(jnp.concatenate([route_ids, route_wts], axis=1), "expert")
    routes = routes.reshape(group_rows, 2 * top)
    ids, weights = routes[:, :top], routes[:, top:].astype(F32)
    weights = weights / jnp.sum(weights, axis=1, keepdims=True)
    named = ids[:, :, None] == jnp.arange(n_data, dtype=jnp.int32)[None, None, :]
    before = jnp.arange(group_rows)[None, :] < jnp.arange(group_rows)[:, None]
    counts = dot(before.astype(BF), jnp.any(named, axis=1).astype(BF))
    rank = jnp.sum(jnp.where(named, counts[:, None, :], 0.0), axis=2).astype(jnp.int32)
    slot = jnp.where(rank // share == my_place, ids * share + rank % share, -1)
    hits = [one_hot(slot[:, k], n_data * share) for k in range(top)]
    picks = sum(hit.astype(BF) for hit in hits)
    coef = sum(jnp.where(hit, weights[:, k][None, :], 0.0) for k, hit in enumerate(hits))

    send = dot(picks, normed).astype(BF).reshape(n_data, share, width)
    slots = lax.all_to_all(send, "dp", split_axis=0, concat_axis=0, tiled=True)
    rows = gather_blocks(slots.reshape(n_data * share, width), "expert").reshape(-1, width)
    gate_e, up_e = dot(rows, expert_gate[0]), dot(rows, expert_up[0])
    hidden_e = (jax.nn.silu(gate_e) * up_e).astype(BF)
    part_e = dot(hidden_e, expert_down[0]).astype(BF)
    summed = scatter_sum(part_e.reshape(n_group, n_data * share, width), "expert")
    returned = lax.all_to_all(
        summed.reshape(n_data, share, width), "dp", split_axis=0, concat_axis=0, tiled=True
    ).reshape(n_data * share, width)

    gate_s, up_s = dot(normed, shared_gate), dot(normed, shared_up)
    shared_hidden = (jax.nn.silu(gate_s) * up_s).astype(BF)
    coef_hi = coef.astype(BF)
    coef_lo = (coef - coef_hi.astype(F32)).astype(BF)
    total = dot(shared_hidden, shared_down) + dot(coef_hi.T, returned) + dot(coef_lo.T, returned)
    total = scatter_sum(total.astype(BF).reshape(n_group, tok_dev, width), "expert")
    return (embed_f + total.astype(F32)).astype(BF)


def solution(mesh):
    return jax.shard_map(
        shards,
        mesh=mesh,
        in_specs=(
            P(("dp", "expert"), None),
            P(("dp", "expert"), None),
            P(("dp", "expert")),
            P(None, "expert"),
            P("expert", None),
            P(),
            P(None, "expert"),
            P(None, "expert"),
            P("expert", None),
            P("dp", None, "expert"),
            P("dp", None, "expert"),
            P("dp", "expert", None),
            P(("dp", "expert"), None),
            P(("dp", "expert"), None),
        ),
        out_specs=P(("dp", "expert"), None),
        check_vma=False,
    )
```

time: 429 us -> 192 us (0.45)
  local copies, waits for them, and re-layouts: 132 us -> 5.22 us
  blocking collectives: 108 us -> 23.1 us
  waiting for transfers between devices: 115 us -> 93.3 us
  starting transfers between devices: 8.98 us -> 23.9 us
  between operations: 14.1 us -> 0.35 us
  other arithmetic: 21.2 us -> 11.3 us
  matrix products: 27.7 us -> 34.4 us
    scatter x2 -> x0, local copies, waits for them, and re-layouts: 96 us -> none  [the longest x1 91.8 us: shards(): send = jnp.zeros((n_data, capacity, width_model), jnp.bfloat16).at[flat_i...]
    ppermute x0 -> x14, waiting for transfers between devices: none -> 70.3 us  [swap(): return lax.ppermute(rows, axis, [(i, i ^ mask) for i in range(count)])]
    all_to_all x1, blocking collectives: 75.7 us -> 23.1 us  [shards(): slots = lax.all_to_all(send, 'dp', split_axis=0, concat_axis=0, tiled=True)]
    unnamed x6 -> x0, waiting for transfers between devices: 36.8 us -> none
    psum x1 -> x0, waiting for transfers between devices: 35.6 us -> none  [shards(): projected = lax.psum(partial_value.astype(jnp.bfloat16), 'expert')]
    reduce_scatter x1 -> x0, waiting for transfers between devices: 23.1 us -> none  [shards(): lax.psum_scatter((jnp.dot(shared_hidden, shared_down, preferred_element_t...]
    all_to_all x1 -> x0, blocking collectives: 17.4 us -> none  [shards(): lax.all_to_all(sorted_feats, 'dp', split_axis=0, concat_axis=0, tiled=True)]
    gather x5 -> x0, local copies, waits for them, and re-layouts: 15.9 us -> none  [the longest x1 6.59 us: shards(): normed[pair_token]]
  transfers between devices with their start and end apart: 7 -> 16, of which waited for: 6 -> 14; matrix products, arithmetic and copies ran while one was open for 4% -> 7% of each run, Pallas kernels for 0% -> 0%
where the time goes in v1:
time: 192 us
  waiting for transfers between devices  93.3 us (49%)
  matrix products  34.4 us (18%)
  starting transfers between devices  23.9 us (12%)
  blocking collectives  23.1 us (12%)
  other arithmetic  11.3 us (6%)
  local copies, waits for them, and re-layouts  5.22 us (3%)
    ppermute x14, waiting for transfers between devices, swap(): return lax.ppermute(rows, axis, [(i, i ^ mask) for i in range(count)])  70.3 us
    dot_general x11, matrix products, dot(): return jnp.dot(a, b, preferred_element_type=F32)  34.4 us
    all_to_all x1, blocking collectives, shards(): slots = lax.all_to_all(send, 'dp', split_axis=0, concat_axis=0, tiled=True)  23.1 us
    all_to_all x1, waiting for transfers between devices, shards(): lax.all_to_all(summed.reshape(n_data, share, width), 'dp', split_axis=0,...  15.7 us
    ppermute x14, starting transfers between devices, swap(): return lax.ppermute(rows, axis, [(i, i ^ mask) for i in range(count)])  13.5 us
    all_to_all x1, waiting for transfers between devices, shards(): lax.all_to_all(leaving.reshape(n_data, peer, width + 128), 'dp', split_ax...  7.26 us
    all_to_all x1, starting transfers between devices, shards(): lax.all_to_all(leaving.reshape(n_data, peer, width + 128), 'dp', split_ax...  6.03 us
    another operation x12, other arithmetic, gather_blocks(): held = jnp.stack([first, second], axis=1).reshape((-1,) + block.shape)  5.07 us
  transfers between devices with their start and end apart: 16, of which 14 were waited for; matrix products, arithmetic and copies ran while one was open for 7% of the time, Pallas kernels for 0%

profile of v1, /device:TPU:0, one launch (start us, length us, event | category | flops | bytes accessed | tf_op | source)
XLA Modules:
  0.0 191.6 jit_solution(6775737611441441448)
XLA Ops:
  0.0 3.0 %collective-permute-start = (bf16[1,32,4608]{2,1,0:T(8,128)(2,1)}, bf16[1,32,4608]{2,1,0:T(8,128)(2,1)}, u32[]{:S(2)}, u32[]{:S(2)}) collective-permute-start(bf16[1,32,4608]{2,1,0:T(8,128)(2,1)} %bitcast.159), channel_id=1, source_target_pairs={{0,2},{1,3},{2,0},{3,1},{4,6},{5,7},{6,4},{7,5},{8,10},{9,11},{10,... | collective-permute-start | bytes 884744 | tf_op jit(solution)/shard_map/ppermute | solution.py:16
  3.1 7.3 %collective-permute-done = bf16[1,32,4608]{2,1,0:T(8,128)(2,1)} collective-permute-done((bf16[1,32,4608]{2,1,0:T(8,128)(2,1)}, bf16[1,32,4608]{2,1,0:T(8,128)(2,1)}, u32[]{:S(2)}, u32[]{:S(2)}) %collective-permute-start) | collective-permute-done | bytes 294944 | tf_op jit(solution)/shard_map/ppermute | solution.py:16
  10.4 1.1 select_bitcast_fusion.9
  11.5 0.9 maximum_bitcast_fusion.1
  12.4 1.8 collective-permute-start.6
  14.2 0.5 collective-permute-done.1
  14.7 1.1 select_bitcast_fusion.5
  15.8 1.1 pad_maximum_fusion.1
  17.0 4.6 %convolution_convert_fusion.3 = bf16[128,2048]{1,0:T(8,128)(2,1)S(1)} fusion(bf16[512,2048]{1,0:T(8,128)(2,1)} %param.18, bf16[128,4608]{1,0:T(8,128)(2,1)} %bitcast.143, bf16[4608,512]{1,0:T(8,128)(2,1)} %param.17), kind=kOutput, calls=%fused_computation.9 | convolution fusion | flops 873267200 | bytes 8519680 | tf_op jit(solution)/shard_map/dot_general | solution.py:11
  21.6 0.7 dynamic-slice_bitcast_fusion.2
  22.3 0.1 collective-permute-start.2
  22.5 0.2 convert_reduce_fusion.1
  22.7 1.5 collective-permute-done.2
  24.2 1.0 fusion.17
  25.3 1.8 collective-permute-start.3
  27.2 3.7 %collective-permute-done.3 = bf16[1,32,2048]{2,1,0:T(8,128)(2,1)S(1)} collective-permute-done((bf16[1,32,2048]{2,1,0:T(8,128)(2,1)S(1)}, bf16[1,32,2048]{2,1,0:T(8,128)(2,1)S(1)}, u32[]{:S(2)}, u32[]{:S(2)}) %collective-permute-start.3) | collective-permute-done | bytes 131104 | tf_op jit(solution)/shard_map/ppermute | solution.py:16
  30.9 0.1 broadcast_in_dim.79
  31.0 0.2 convolution_convert_fusion.1
  31.1 0.7 reshape.82
  31.8 6.0 %all-to-all-start = ((bf16[8,4,2176]{2,1,0:T(4,128)(2,1)}), bf16[8,4,2176]{2,1,0:T(4,128)(2,1)S(1)}, u32[]{:S(2)}, u32[]{:S(2)}) async-start(bf16[8,4,2176]{2,1,0:T(4,128)(2,1)} %reshape.82), calls=%async_computation | async-start | bytes 278528 | tf_op jit(solution)/shard_map/all_to_all | solution.py:91
  37.9 0.1 reshape_reshape.24
  38.0 7.3 %all-to-all-done = bf16[8,4,2176]{2,1,0:T(4,128)(2,1)S(1)} async-done(((bf16[8,4,2176]{2,1,0:T(4,128)(2,1)}), bf16[8,4,2176]{2,1,0:T(4,128)(2,1)S(1)}, u32[]{:S(2)}, u32[]{:S(2)}) %all-to-all-start) | async-done | bytes 139296 | tf_op jit(solution)/shard_map/all_to_all | solution.py:91
  45.3 0.1 convert_reduce_fusion
  45.4 0.1 fusion.57
  45.5 1.4 multiply_reduce_fusion
  46.9 0.8 fusion.27
  47.8 1.6 collective-permute-start.4
  49.4 0.2 fusion.29
  49.5 4.7 %collective-permute-done.4 = bf16[1,64,2048]{2,1,0:T(8,128)(2,1)S(1)} collective-permute-done((bf16[1,64,2048]{2,1,0:T(8,128)(2,1)S(1)}, bf16[1,64,2048]{2,1,0:T(8,128)(2,1)S(1)}, u32[]{:S(2)}, u32[]{:S(2)}) %collective-permute-start.4) | collective-permute-done | bytes 262176 | tf_op jit(solution)/shard_map/ppermute | solution.py:16
  54.2 0.9 select_bitcast_fusion.11
  55.3 1.8 collective-permute-done.5
  57.1 0.1 select_bitcast_fusion.7
  57.2 0.1 pad_maximum_fusion.2
  57.3 0.1 copy.32
  57.4 0.4 convolution_convert_fusion.2
  57.8 23.1 %all_to_all.15 = bf16[8,24,2048]{2,1,0:T(8,128)(2,1)S(1)} all-to-all(bf16[8,24,2048]{2,1,0:T(8,128)(2,1)S(1)} %bitcast.154), channel_id=1, replica_groups=mesh['dp'=8,'expert'=4] {'dp'}, dimensions={0} | all-to-all | bytes 1572864 | tf_op jit(solution)/shard_map/all_to_all | solution.py:117
  80.9 1.5 collective-permute-start.8
  82.4 17.2 %collective-permute-done.8 = bf16[1,192,2048]{2,1,0:T(8,128)(2,1)S(1)} collective-permute-done((bf16[1,192,2048]{2,1,0:T(8,128)(2,1)S(1)}, bf16[1,192,2048]{2,1,0:T(8,128)(2,1)S(1)}, u32[]{:S(2)}, u32[]{:S(2)}) %collective-permute-start.8) | collective-permute-done | bytes 786464 | tf_op jit(solution)/shard_map/ppermute | solution.py:16
  99.7 0.1 select_bitcast_fusion.3
  99.8 0.1 maximum_bitcast_fusion
  100.0 3.4 %collective-permute-done.9 = bf16[2,192,2048]{2,1,0:T(8,128)(2,1)S(1)} collective-permute-done((bf16[2,192,2048]{2,1,0:T(8,128)(2,1)S(1)}, bf16[2,192,2048]{2,1,0:T(8,128)(2,1)S(1)}, u32[]{:S(2)}, u32[]{:S(2)}) %collective-permute-start.9) | collective-permute-done | bytes 1572896 | tf_op jit(solution)/shard_map/ppermute | solution.py:16
  103.4 0.2 select_bitcast_fusion.1
  103.6 0.3 pad_maximum_fusion
  103.9 1.6 copy-done.3
  105.6 2.3 %fusion.5 = f32[768,352]{0,1:T(8,128)} fusion(bf16[768,2048]{1,0:T(8,128)(2,1)S(1)} %bitcast.152, bf16[1,2048,352]{1,2,0:T(8,128)(2,1)S(1)} %copy-done.6), kind=kOutput, calls=%fused_computation.19 | convolution fusion | flops 1107296256 | bytes 5668864 | tf_op jit(solution)/shard_map/dot_general | solution.py:11
  107.9 8.5 %convolution_convert_fusion = bf16[768,2048]{1,0:T(8,128)(2,1)} fusion(bf16[1,352,2048]{2,1,0:T(8,128)(2,1)} %param.25, f32[768,352]{0,1:T(8,128)} %fusion.5, bf16[768,2048]{1,0:T(8,128)(2,1)} %bitcast.153, bf16[1,2048,352]{1,2,0:T(8,128)(2,1)} %param.23), kind=kOutput, calls=%fused_computation | convolution fusion | flops 2217787392 | bytes 10256384 | tf_op jit(solution)/shard_map/dot_general | solution.py:11
  116.4 1.7 dynamic-slice_bitcast_fusion
  118.1 0.2 collective-permute-start.10
  118.3 3.3 %collective-permute-done.10 = bf16[2,192,2048]{2,1,0:T(8,128)(2,1)S(1)} collective-permute-done((bf16[2,192,2048]{2,1,0:T(8,128)(2,1)S(1)}, bf16[2,192,2048]{2,1,0:T(8,128)(2,1)S(1)}, u32[]{:S(2)}, u32[]{:S(2)}) %collective-permute-start.10) | collective-permute-done | bytes 1572896 | tf_op jit(solution)/shard_map/ppermute | solution.py:16
  121.6 0.7 fusion
  122.3 1.6 collective-permute-start.11
  123.9 18.1 %collective-permute-done.11 = bf16[1,192,2048]{2,1,0:T(8,128)(2,1)S(1)} collective-permute-done((bf16[1,192,2048]{2,1,0:T(8,128)(2,1)S(1)}, bf16[1,192,2048]{2,1,0:T(8,128)(2,1)S(1)}, u32[]{:S(2)}, u32[]{:S(2)}) %collective-permute-start.11) | collective-permute-done | bytes 786464 | tf_op jit(solution)/shard_map/ppermute | solution.py:16
  142.0 1.2 add_convert_fusion
  143.1 4.4 %all-to-all-start.2 = ((bf16[8,24,2048]{2,1,0:T(8,128)(2,1)}), bf16[8,24,2048]{2,1,0:T(8,128)(2,1)}, u32[]{:S(2)}, u32[]{:S(2)}) async-start(bf16[8,24,2048]{2,1,0:T(8,128)(2,1)} %bitcast.149), calls=%async_computation.2 | async-start | bytes 1572864 | tf_op jit(solution)/shard_map/all_to_all | solution.py:123
  147.6 4.0 %fusion.78 = f32[256,704]{0,1:T(8,128)} fusion(bf16[256,2048]{1,0:T(8,128)(2,1)} %bitcast.147, bf16[2048,704]{0,1:T(8,128)(2,1)} %param.20), kind=kOutput, calls=%fused_computation.145 | convolution fusion | flops 738197504 | bytes 4653056 | tf_op jit(solution)/shard_map/dot_general | solution.py:11
  151.5 15.7 %all-to-all-done.2 = bf16[8,24,2048]{2,1,0:T(8,128)(2,1)} async-done(((bf16[8,24,2048]{2,1,0:T(8,128)(2,1)}), bf16[8,24,2048]{2,1,0:T(8,128)(2,1)}, u32[]{:S(2)}, u32[]{:S(2)}) %all-to-all-start.2) | async-done | bytes 786464 | tf_op jit(solution)/shard_map/all_to_all | solution.py:123
  167.3 2.9 %fusion.54 = f32[256,2048]{1,0:T(8,128)} fusion(bf16[192,2048]{1,0:T(8,128)(2,1)} %bitcast.45, f32[256]{0:T(256)S(1)} %bitcast.168, s32[256]{0:T(256)S(1)} %bitcast.164, f32[256]{0:T(256)S(1)} %bitcast.166, s32[256]{0:T(256)S(1)} %bitcast.161), kind=kOutput, calls=%fused_computation.91 | convolution fusion | flops 201621504 | bytes 2887680 | tf_op jit(solution)/shard_map/dot_general | solution.py:11
  170.2 7.6 %convolution_add_fusion = f32[256,2048]{1,0:T(8,128)} fusion(f32[256,2048]{1,0:T(8,128)} %fusion.54, bf16[704,2048]{1,0:T(8,128)(2,1)S(1)} %copy-done, bf16[256,2048]{1,0:T(8,128)(2,1)} %bitcast.148, bf16[2048,704]{0,1:T(8,128)(2,1)} %param.21, f32[256,704]{0,1:T(8,128)} %fusion.78), kind=kOutput, calls=%fused_computation.5 | convolution fusion | flops 1478000640 | bytes 11730944 | tf_op jit(solution)/shard_map/dot_general | solution.py:11
  177.9 2.3 %fusion.1 = bf16[256,2048]{1,0:T(8,128)(2,1)S(1)} fusion(f32[256,2048]{1,0:T(8,128)} %convolution_add_fusion, bf16[192,2048]{1,0:T(8,128)(2,1)} %bitcast.45, f32[256]{0:T(256)S(1)} %bitcast.169, s32[256]{0:T(256)S(1)} %bitcast.165, f32[256]{0:T(256)S(1)} %bitcast.167, s32[256]{0:T(256)S(1)} %bitcast.162), kind=kOutput, calls=%fused_computation.7 | convolution fusion | flops 202817536 | bytes 3936256 | tf_op jit(solution)/shard_map/dot_general | solution.py:11
  180.3 1.9 collective-permute-done.12
  182.2 0.1 fusion.10
  182.4 1.6 collective-permute-start.13
  184.0 6.8 %collective-permute-done.13 = bf16[1,64,2048]{2,1,0:T(8,128)(2,1)S(1)} collective-permute-done((bf16[1,64,2048]{2,1,0:T(8,128)(2,1)S(1)}, bf16[1,64,2048]{2,1,0:T(8,128)(2,1)S(1)}, u32[]{:S(2)}, u32[]{:S(2)}) %collective-permute-start.13) | collective-permute-done | bytes 262176 | tf_op jit(solution)/shard_map/ppermute | solution.py:16
  190.8 0.8 fusion.16
  (46 shorter events, 0.8 us)
Async XLA Ops:
  0.0 170.2 %copy-start = (bf16[704,2048]{1,0:T(8,128)(2,1)S(1)}, bf16[704,2048]{1,0:T(8,128)(2,1)}, u32[]{:S(2)}) copy-start(bf16[704,2048]{1,0:T(8,128)(2,1)} %param.22) | copy-start | bytes 8650756
  0.0 12.4 %copy-start.5 = (s32[64,2]{0,1:T(2,128)S(1)}, s32[64,2]{0,1:T(2,128)}, u32[]{:S(2)}) copy-start(s32[64,2]{0,1:T(2,128)} %param.26) | copy-start | bytes 1540
  0.0 12.4 %copy-start.4 = (s32[64,2]{0,1:T(2,128)S(1)}, s32[64,2]{0,1:T(2,128)}, u32[]{:S(2)}) copy-start(s32[64,2]{0,1:T(2,128)} %param.27) | copy-start | bytes 1540
  0.0 14.2 %copy-start.7 = (s32[32]{0:T(128)S(1)}, s32[32]{0:T(128)}, u32[]{:S(2)}) copy-start(s32[32]{0:T(128)} %param.16) | copy-start | bytes 388
  0.0 10.4 %collective-permute-start = (bf16[1,32,4608]{2,1,0:T(8,128)(2,1)}, bf16[1,32,4608]{2,1,0:T(8,128)(2,1)}, u32[]{:S(2)}, u32[]{:S(2)}) collective-permute-start(bf16[1,32,4608]{2,1,0:T(8,128)(2,1)} %bitcast.159), channel_id=1, source_target_pairs={{0,2},{1,3},{2,0},{3,1},{4,6},{5,7},{6,4},{7,5},{8,10},{9,11},{10,... | collective-permute-start | bytes 884744 | tf_op jit(solution)/shard_map/ppermute | solution.py:16
  12.4 2.3 %collective-permute-start.1 = (bf16[2,32,4608]{2,1,0:T(8,128)(2,1)}, bf16[2,32,4608]{2,1,0:T(8,128)(2,1)}, u32[]{:S(2)}, u32[]{:S(2)}) collective-permute-start(bf16[2,32,4608]{2,1,0:T(8,128)(2,1)} %maximum_bitcast_fusion.1), channel_id=1, source_target_pairs={{0,1},{1,0},{2,3},{3,2},{4,5},{5,4},{6,7},{7,6},{8,9},{9,8},{10,11... | collective-permute-start | bytes 1769480 | tf_op jit(solution)/shard_map/ppermute | solution.py:16
  12.4 14.7 %collective-permute-start.6 = (s32[1,64,4]{1,2,0:T(4,128)S(1)}, s32[1,64,4]{1,2,0:T(4,128)S(1)}, u32[]{:S(2)}, u32[]{:S(2)}) collective-permute-start(s32[1,64,4]{1,2,0:T(4,128)S(1)} %add_bitcast_fusion.1), channel_id=1, source_target_pairs={{0,2},{1,3},{2,0},{3,1},{4,6},{5,7},{6,4},{7,5},{8,10},{9,11},{10,... | collective-permute-start | bytes 3080 | tf_op jit(solution)/shard_map/ppermute | solution.py:16
  22.3 1.9 collective-permute-start.2
  25.3 5.6 %collective-permute-start.3 = (bf16[1,32,2048]{2,1,0:T(8,128)(2,1)S(1)}, bf16[1,32,2048]{2,1,0:T(8,128)(2,1)S(1)}, u32[]{:S(2)}, u32[]{:S(2)}) collective-permute-start(bf16[1,32,2048]{2,1,0:T(8,128)(2,1)S(1)} %constant_dynamic-slice_fusion.2), channel_id=1, source_target_pairs={{0,2},{1,3},{2,0},{3,1},{4,6},{5,7},{6,4},{7,5},{8,10},{9,11},{10,... | collective-permute-start | bytes 393224 | tf_op jit(solution)/shard_map/ppermute | solution.py:16
  27.1 10.8 %collective-permute-start.7 = (s32[2,64,4]{1,2,0:T(4,128)S(1)}, s32[2,64,4]{1,2,0:T(4,128)S(1)}, u32[]{:S(2)}, u32[]{:S(2)}) collective-permute-start(s32[2,64,4]{1,2,0:T(4,128)S(1)} %add_bitcast_fusion), channel_id=1, source_target_pairs={{0,1},{1,0},{2,3},{3,2},{4,5},{5,4},{6,7},{7,6},{8,9},{9,8},{10,11... | collective-permute-start | bytes 6152 | tf_op jit(solution)/shard_map/ppermute | solution.py:16
  31.8 13.4 %all-to-all-start = ((bf16[8,4,2176]{2,1,0:T(4,128)(2,1)}), bf16[8,4,2176]{2,1,0:T(4,128)(2,1)S(1)}, u32[]{:S(2)}, u32[]{:S(2)}) async-start(bf16[8,4,2176]{2,1,0:T(4,128)(2,1)} %reshape.82), calls=%async_computation | async-start | bytes 278528 | tf_op jit(solution)/shard_map/all_to_all | solution.py:91
  47.8 6.4 %collective-permute-start.4 = (bf16[1,64,2048]{2,1,0:T(8,128)(2,1)S(1)}, bf16[1,64,2048]{2,1,0:T(8,128)(2,1)S(1)}, u32[]{:S(2)}, u32[]{:S(2)}) collective-permute-start(bf16[1,64,2048]{2,1,0:T(8,128)(2,1)S(1)} %fusion.27), channel_id=1, source_target_pairs={{0,2},{1,3},{2,0},{3,1},{4,6},{5,7},{6,4},{7,5},{8,10},{9,11},{10,... | collective-permute-start | bytes 786440 | tf_op jit(solution)/shard_map/ppermute | solution.py:16
  55.1 2.0 %collective-permute-start.5 = (bf16[2,64,2048]{2,1,0:T(8,128)(2,1)S(1)}, bf16[2,64,2048]{2,1,0:T(8,128)(2,1)S(1)}, u32[]{:S(2)}, u32[]{:S(2)}) collective-permute-start(bf16[2,64,2048]{2,1,0:T(8,128)(2,1)S(1)} %maximum_bitcast_fusion.2), channel_id=1, source_target_pairs={{0,1},{1,0},{2,3},{3,2},{4,5},{5,4},{6,7},{7,6},{8,9},{9,8},{10,11... | collective-permute-start | bytes 1572872 | tf_op jit(solution)/shard_map/ppermute | solution.py:16
  57.4 23.5 %copy-start.1 = (bf16[2,2,64,2048]{3,2,1,0:T(8,128)(2,1)}, bf16[2,2,64,2048]{3,2,1,0:T(8,128)(2,1)S(1)}, u32[]{:S(2)}) copy-start(bf16[2,2,64,2048]{3,2,1,0:T(8,128)(2,1)S(1)} %copy.32) | copy-start | bytes 3145732
  80.9 18.8 %collective-permute-start.8 = (bf16[1,192,2048]{2,1,0:T(8,128)(2,1)S(1)}, bf16[1,192,2048]{2,1,0:T(8,128)(2,1)S(1)}, u32[]{:S(2)}, u32[]{:S(2)}) collective-permute-start(bf16[1,192,2048]{2,1,0:T(8,128)(2,1)S(1)} %bitcast.155), channel_id=1, source_target_pairs={{0,2},{1,3},{2,0},{3,1},{4,6},{5,7},{6,4},{7,5},{8,10},{9,11},{10,... | collective-permute-start | bytes 2359304 | tf_op jit(solution)/shard_map/ppermute | solution.py:16
  99.9 3.5 %collective-permute-start.9 = (bf16[2,192,2048]{2,1,0:T(8,128)(2,1)S(1)}, bf16[2,192,2048]{2,1,0:T(8,128)(2,1)S(1)}, u32[]{:S(2)}, u32[]{:S(2)}) collective-permute-start(bf16[2,192,2048]{2,1,0:T(8,128)(2,1)S(1)} %maximum_bitcast_fusion), channel_id=1, source_target_pairs={{0,1},{1,0},{2,3},{3,2},{4,5},{5,4},{6,7},{7,6},{8,9},{9,8},{10,11... | collective-permute-start | bytes 4718600 | tf_op jit(solution)/shard_map/ppermute | solution.py:16
  103.6 2.0 %copy-start.6 = (bf16[1,2048,352]{1,2,0:T(8,128)(2,1)S(1)}, bf16[1,2048,352]{1,2,0:T(8,128)(2,1)}, u32[]{:S(2)}) copy-start(bf16[1,2048,352]{1,2,0:T(8,128)(2,1)} %param.24) | copy-start | bytes 4325380
  103.9 1.7 copy-start.3
  116.4 5.1 %copy-start.2 = (bf16[768,2048]{1,0:T(8,128)(2,1)S(1)}, bf16[768,2048]{1,0:T(8,128)(2,1)}, u32[]{:S(2)}) copy-start(bf16[768,2048]{1,0:T(8,128)(2,1)} %convolution_convert_fusion) | copy-start | bytes 9437188
  118.1 3.5 %collective-permute-start.10 = (bf16[2,192,2048]{2,1,0:T(8,128)(2,1)S(1)}, bf16[2,192,2048]{2,1,0:T(8,128)(2,1)S(1)}, u32[]{:S(2)}, u32[]{:S(2)}) collective-permute-start(bf16[2,192,2048]{2,1,0:T(8,128)(2,1)S(1)} %dynamic-slice_bitcast_fusion), channel_id=1, source_target_pairs={{0,1},{1,0},{2,3},{3,2},{4,5},{5,4},{6,7},{7,6},{8,9},{9,8},{10,11... | collective-permute-start | bytes 4718600 | tf_op jit(solution)/shard_map/ppermute | solution.py:16
  122.3 19.6 %collective-permute-start.11 = (bf16[1,192,2048]{2,1,0:T(8,128)(2,1)S(1)}, bf16[1,192,2048]{2,1,0:T(8,128)(2,1)S(1)}, u32[]{:S(2)}, u32[]{:S(2)}) collective-permute-start(bf16[1,192,2048]{2,1,0:T(8,128)(2,1)S(1)} %constant_dynamic-slice_fusion.1), channel_id=1, source_target_pairs={{0,2},{1,3},{2,0},{3,1},{4,6},{5,7},{6,4},{7,5},{8,10},{9,11},{10,... | collective-permute-start | bytes 2359304 | tf_op jit(solution)/shard_map/ppermute | solution.py:16
  143.1 24.1 %all-to-all-start.2 = ((bf16[8,24,2048]{2,1,0:T(8,128)(2,1)}), bf16[8,24,2048]{2,1,0:T(8,128)(2,1)}, u32[]{:S(2)}, u32[]{:S(2)}) async-start(bf16[8,24,2048]{2,1,0:T(8,128)(2,1)} %bitcast.149), calls=%async_computation.2 | async-start | bytes 1572864 | tf_op jit(solution)/shard_map/all_to_all | solution.py:123
  180.2 2.0 %collective-permute-start.12 = (bf16[2,64,2048]{2,1,0:T(8,128)(2,1)S(1)}, bf16[2,64,2048]{2,1,0:T(8,128)(2,1)S(1)}, u32[]{:S(2)}, u32[]{:S(2)}) collective-permute-start(bf16[2,64,2048]{2,1,0:T(8,128)(2,1)S(1)} %dynamic-slice_bitcast_fusion.1), channel_id=1, source_target_pairs={{0,1},{1,0},{2,3},{3,2},{4,5},{5,4},{6,7},{7,6},{8,9},{9,8},{10,11... | collective-permute-start | bytes 1572872 | tf_op jit(solution)/shard_map/ppermute | solution.py:16
  182.4 8.4 %collective-permute-start.13 = (bf16[1,64,2048]{2,1,0:T(8,128)(2,1)S(1)}, bf16[1,64,2048]{2,1,0:T(8,128)(2,1)S(1)}, u32[]{:S(2)}, u32[]{:S(2)}) collective-permute-start(bf16[1,64,2048]{2,1,0:T(8,128)(2,1)S(1)} %constant_dynamic-slice_fusion), channel_id=1, source_target_pairs={{0,2},{1,3},{2,0},{3,1},{4,6},{5,7},{6,4},{7,5},{8,10},{9,11},{10,... | collective-permute-start | bytes 786440 | tf_op jit(solution)/shard_map/ppermute | solution.py:16

commit v2 on v1

v2 whole, which is shorter than its diff:
```python
import jax
import jax.numpy as jnp
from jax import lax
from jax.experimental import pallas as pl
from jax.experimental.pallas import tpu as pltpu
from jax.sharding import PartitionSpec as P

BF = jnp.bfloat16
F32 = jnp.float32


def dot(a, b):
    return jnp.dot(a, b, preferred_element_type=F32)


def dot_t(a, b):
    return lax.dot_general(a, b, (((1,), (1,)), ((), ())), preferred_element_type=F32)


def swap(rows, axis, mask):
    count = lax.axis_size(axis)
    return lax.ppermute(rows, axis, [(i, i ^ mask) for i in range(count)])


def gather(piece, axis):
    mask = lax.axis_size(axis) // 2
    pieces = [piece]
    while mask:
        pieces = pieces + [swap(p, axis, mask) for p in pieces]
        mask //= 2
    return pieces


def add(rows, other):
    return (rows.astype(F32) + other.astype(F32)).astype(BF)


def scatter_sum(keep, give, axis, last=None):
    rows, mask = add(keep, swap(give, axis, 1)), 2
    while mask < (last or lax.axis_size(axis)):
        half = rows.shape[0] // 2
        rows = add(rows[:half], swap(rows[half:], axis, mask))
        mask *= 2
    return rows


def reversed_bits(places, count):
    turned, mask, low = jnp.zeros_like(places), count // 2, 1
    while mask:
        turned += jnp.where((places & low) != 0, mask, 0)
        mask, low = mask // 2, low * 2
    return turned


def local_kernel(body, outs, args, scratch=(), macs=0):
    moved = sum(x.size * x.dtype.itemsize for x in args) + sum(
        o.size * o.dtype.itemsize for o in outs
    )
    return pl.pallas_call(
        body,
        out_shape=list(outs),
        in_specs=[pl.BlockSpec(memory_space=pltpu.VMEM)] * len(args),
        out_specs=[pl.BlockSpec(memory_space=pltpu.VMEM)] * len(outs),
        scratch_shapes=list(scratch),
        compiler_params=pltpu.CompilerParams(vmem_limit_bytes=48 * 2**20),
        cost_estimate=pl.CostEstimate(flops=2 * macs, bytes_accessed=moved, transcendentals=0),
    )(*args)


def put_together(refs, whole):
    at = 0
    for ref in refs:
        whole[at : at + ref.shape[0]] = ref[...]
        at += ref.shape[0]


def out(rows, columns, dtype=BF):
    return jax.ShapeDtypeStruct((rows, columns), dtype)


def steps_of(size, step):
    return size // step if size % step == 0 else 1


def gated(rows, gate, up):
    value = dot_t(rows, gate)
    return (value / (1.0 + jnp.exp(-value)) * dot_t(rows, up)).astype(BF)


def fits(pieces):
    return all(p.shape[0] % 16 == 0 for p in pieces)


def expert_rows(pieces, gate, up, down):
    count = sum(p.shape[0] for p in pieces)
    units, width = gate.shape
    if not fits(pieces) or count % 32:
        part = dot(gated(jnp.concatenate(pieces, axis=0), gate, up), down).astype(BF)
        return part[: count // 2], part[count // 2 :]

    def body(*refs):
        n = len(pieces)
        gate_ref, up_ref, down_ref, keep, give, whole = refs[n:]
        put_together(refs[:n], whole)
        for rows, result in ((slice(count // 2, count), give), (slice(0, count // 2), keep)):
            hidden = gated(whole[rows], gate_ref[...], up_ref[...])
            result[...] = dot(hidden, down_ref[...]).astype(BF)

    return local_kernel(
        body,
        [out(count // 2, width)] * 2,
        [*pieces, gate, up, down],
        [pltpu.VMEM((count, width), BF)],
        3 * count * width * units,
    )


def shared_rows(pieces, gate, up, down):
    count = sum(p.shape[0] for p in pieces)
    units, width = gate.shape
    if not fits(pieces):
        part = dot(gated(jnp.concatenate(pieces, axis=0), gate, up), down)
        return part[: count // 2], part[count // 2 :]

    def body(*refs):
        n = len(pieces)
        gate_ref, up_ref, down_ref, keep, give, whole = refs[n:]
        put_together(refs[:n], whole)
        part = dot(gated(whole[...], gate_ref[...], up_ref[...]), down_ref[...])
        keep[...] = part[: count // 2]
        give[...] = part[count // 2 :]

    return local_kernel(
        body,
        [out(count // 2, width, F32)] * 2,
        [*pieces, gate, up, down],
        [pltpu.VMEM((count, width), BF)],
        3 * count * width * units,
    )


def image_rows(pieces, proj_in, proj_out):
    count = sum(p.shape[0] for p in pieces)
    depth, units = proj_in.shape
    width = proj_out.shape[1]

    def body(*refs):
        n = len(pieces)
        in_ref, out_ref, keep, give, whole = refs[n:]
        put_together(refs[:n], whole)
        hidden = jax.nn.gelu(dot(whole[...], in_ref[...]), approximate=True).astype(BF)
        part = dot(hidden, out_ref[...])
        keep[...] = part[: count // 2].astype(BF)
        give[...] = part[count // 2 :].astype(BF)

    return local_kernel(
        body,
        [out(count // 2, width)] * 2,
        [*pieces, proj_in, proj_out],
        [pltpu.VMEM((count, depth), BF)],
        count * units * (depth + width),
    )


def place_rows(mine, other, place, offsets, n_data):
    count, width = mine.shape
    peer = count // n_data
    wide = width + offsets.shape[1]
    if count % 16:
        rows = jnp.concatenate([add(mine, other), offsets], axis=1)
        return dot(place, rows).astype(BF).reshape(n_data, peer, wide)

    def body(mine_ref, other_ref, place_ref, offsets_ref, result):
        rows = add(mine_ref[...], other_ref[...])
        moved = dot(place_ref[...], rows).astype(BF)
        beside = dot(place_ref[...], offsets_ref[...]).astype(BF)
        for d in range(n_data):
            result[d, :, :width] = moved[d * peer : (d + 1) * peer]
            result[d, :, width:] = beside[d * peer : (d + 1) * peer]

    return local_kernel(
        body,
        [jax.ShapeDtypeStruct((n_data, peer, wide), BF)],
        [mine, other, place, offsets],
        (),
        count * count * wide,
    )[0]


def embed_rows(arrived, text, gain):
    n_data, peer, wide = arrived.shape
    count, width = text.shape

    def math(rows, offsets, text_rows, gain_row):
        spots = lax.broadcasted_iota(jnp.int32, (1, count), 1).astype(F32) == offsets
        spots = spots.astype(F32)
        turned = (((0,), (0,)), ((), ()))
        placed = lax.dot_general(spots.astype(BF), rows, turned, preferred_element_type=F32)
        named = lax.dot_general(spots, jnp.ones_like(offsets), turned, preferred_element_type=F32)
        embed = jnp.where(named > 0.5, placed, text_rows.astype(F32))
        meansq = jnp.mean(embed * embed, axis=-1, keepdims=True) + 1e-06
        return embed, (embed * lax.rsqrt(meansq) * gain_row).astype(BF)

    gain = gain.reshape(1, width)
    if n_data * peer % 16 or peer % 4:
        rows = arrived.reshape(n_data * peer, wide)
        return math(rows[:, :width], rows[:, width : width + 1].astype(F32), text, gain)

    def body(arrived_ref, text_ref, gain_ref, embed_ref, normed_ref):
        rows = jnp.concatenate([arrived_ref[d].astype(F32) for d in range(n_data)], axis=0)
        embed, normed = math(
            rows[:, :width].astype(BF), rows[:, width : width + 1], text_ref[...], gain_ref[...]
        )
        embed_ref[...] = embed
        normed_ref[...] = normed

    return local_kernel(
        body, [out(count, width, F32), out(count, width)], [arrived, text, gain], (), count * n_data * peer * width
    )


def pick_rows(picks, pieces, starts, sizes):
    count, width = sum(p.shape[0] for p in pieces), pieces[0].shape[1]
    if not fits(pieces) or any(n % 8 for n in (*starts, *sizes)):
        rows = dot(picks, jnp.concatenate(pieces, axis=0)).astype(BF)
        return [rows[at : at + size] for at, size in zip(starts, sizes)]

    def body(*refs):
        n = len(pieces)
        whole = refs[-1]
        put_together(refs[1 : n + 1], whole)
        rows = dot(refs[0][...], whole[...])
        for ref, at, size in zip(refs[n + 1 : -1], starts, sizes):
            ref[...] = rows[at : at + size].astype(BF)

    return local_kernel(
        body,
        [out(size, width) for size in sizes],
        [picks, *pieces],
        [pltpu.VMEM((count, width), BF)],
        picks.shape[0] * count * width,
    )


def combine_rows(total, coef, backs, starts):
    count, width = total.shape
    slots = coef.shape[2]
    ends = list(starts[1:]) + [slots]
    if any(n % 16 for n in (slots, *starts)):
        whole = jnp.concatenate(
            [jnp.pad(b, ((0, e - s - b.shape[0]), (0, 0))) for b, s, e in zip(backs, starts, ends)],
            axis=0,
        )
        return (total + dot(coef[0], whole) + dot(coef[1], whole)).astype(BF)

    def body(*refs):
        total_ref, coef_ref, result, whole = refs[0], refs[1], refs[-2], refs[-1]
        for ref, at, end in zip(refs[2:-2], starts, ends):
            size = ref.shape[0]
            if size != end - at:
                whole[end - 16 : end] = jnp.zeros((16, width), BF)
            whole[at : at + size] = ref[...]
        rows = whole[...]
        value = total_ref[...] + dot(coef_ref[0], rows)
        result[...] = (value + dot(coef_ref[1], rows)).astype(BF)

    return local_kernel(
        body,
        [out(count, width)],
        [total, coef, *backs],
        [pltpu.VMEM((slots, width), BF)],
        2 * count * width * slots,
    )[0]


def one_hot(places, count):
    return places[None, :] == jnp.arange(count, dtype=jnp.int32)[:, None]


def shards(
    text_embed,
    image_feats,
    tile_pos,
    proj_in,
    proj_out,
    norm_gain,
    shared_gate,
    shared_up,
    shared_down,
    expert_gate,
    expert_up,
    expert_down,
    route_ids,
    route_wts,
):
    tok_dev, width = text_embed.shape
    img_dev = image_feats.shape[0]
    n_data = lax.axis_size("dp")
    n_group = lax.axis_size("expert")
    peer = img_dev // n_data
    my_place = lax.axis_index("expert")
    top = route_ids.shape[1]
    group_rows = tok_dev * n_group
    capacity = 3 * group_rows * top // (2 * n_data)
    share = capacity // n_group

    keep, give = image_rows(gather(image_feats, "expert"), proj_in, proj_out)
    rows, mask = add(keep, swap(give, "expert", 1)), 2
    while 2 * mask < n_group:
        half = rows.shape[0] // 2
        rows = add(rows[:half], swap(rows[half:], "expert", mask))
        mask *= 2
    other = swap(rows[img_dev:], "expert", mask)

    owner = tile_pos // tok_dev // n_group
    earlier = jnp.arange(img_dev)[None, :] < jnp.arange(img_dev)[:, None]
    rank_img = jnp.sum(((owner[:, None] == owner[None, :]) & earlier).astype(jnp.int32), axis=1)
    place = one_hot(owner * peer + rank_img, img_dev).astype(BF)
    offsets = jnp.broadcast_to((tile_pos % tok_dev).astype(BF)[:, None], (img_dev, 128))
    leaving = place_rows(rows[:img_dev], other, place, offsets, n_data)
    arrived = lax.all_to_all(leaving, "dp", split_axis=0, concat_axis=0, tiled=True)
    embed_f, normed = embed_rows(arrived, text_embed, norm_gain)
    normed = gather(normed, "expert")

    routes = jnp.concatenate([route_ids, route_wts], axis=1)
    routes = jnp.concatenate(gather(routes, "expert"), axis=0)
    ids, weights = routes[:, :top], routes[:, top:].astype(F32)
    weights = weights / jnp.sum(weights, axis=1, keepdims=True)
    rows_at = jnp.arange(group_rows, dtype=jnp.int32)
    token = (my_place ^ reversed_bits(rows_at // tok_dev, n_group)) * tok_dev + rows_at % tok_dev
    named = ids[:, :, None] == jnp.arange(n_data, dtype=jnp.int32)[None, None, :]
    before = token[None, :] < token[:, None]
    counts = dot(before.astype(BF), jnp.any(named, axis=1).astype(BF))
    rank = jnp.sum(jnp.where(named, counts[:, None, :], 0.0), axis=2).astype(jnp.int32)
    distance = ids ^ lax.axis_index("dp")

    half = n_data // 2
    wide = 2 * capacity // 4
    core = my_place % 2
    near_slot = jnp.where((distance < half) & (rank // wide == core), distance * wide + rank % wide, -1)
    apart = -(-share // 16) * 16
    far_slot = jnp.where(
        (distance >= half) & (rank // share == my_place),
        (distance - half) * apart + rank % share + half * wide,
        -1,
    )
    slot = jnp.maximum(near_slot, far_slot)
    sizes = [wide] * half + [share] * (n_data - half)
    starts = [m * wide if m < half else half * wide + (m - half) * apart for m in range(n_data)]
    slots = half * wide + (n_data - half) * apart
    hits = [one_hot(slot[:, k], slots) for k in range(top)]
    picks = sum(hit.astype(BF) for hit in hits)
    coef = sum(jnp.where(hit, weights[:, k][None, :], 0.0) for k, hit in enumerate(hits)).T
    coef_hi = coef.astype(BF)
    coef = jnp.stack([coef_hi, (coef - coef_hi.astype(F32)).astype(BF)])

    send = pick_rows(picks, normed, starts, sizes)
    got = [None] * n_data
    got[0] = send[0]
    quarter = n_data // 4
    near, far_one, far_two = range(half), range(half, half + quarter), range(half + quarter, n_data)
    for m in (*near[1:], *far_one):
        got[m] = swap(send[m], "dp", m)
    for i, m in enumerate(far_two):
        late, got[i + 1] = lax.optimization_barrier((send[m], got[i + 1]))
        got[m] = swap(late, "dp", m)

    shared = shared_rows(normed, shared_gate.T, shared_up.T, shared_down)
    experts = (expert_gate[0].T, expert_up[0].T, expert_down[0])

    def join(stage):
        return jnp.concatenate([got[m] for m in stage], axis=0)

    far = join(far_one)
    far, shared = lax.optimization_barrier((far, shared))
    far_pieces = gather(far, "expert")
    mine = [got[m] for m in near]
    keep, give = expert_rows(mine + [swap(p, "expert", 1) for p in mine], *experts)
    far_pieces, keep, give = lax.optimization_barrier((far_pieces, keep, give))
    back = [None] * n_data

    def send_back(stage, rows):
        size = sizes[stage[0]]
        for i, m in enumerate(stage):
            part = rows[i * size : (i + 1) * size]
            back[m] = swap(part, "dp", m) if m else part

    send_back(near, scatter_sum(keep, give, "expert", last=2))
    send_back(far_one, scatter_sum(*expert_rows(far_pieces, *experts), "expert"))
    pieces = gather(join(far_two), "expert")
    send_back(far_two, scatter_sum(*expert_rows(pieces, *experts), "expert"))

    middle = group_rows // 2
    give = combine_rows(shared[1], coef[:, middle:], back, starts)
    keep = combine_rows(shared[0], coef[:, :middle], back, starts)
    total = scatter_sum(keep, give, "expert")
    return (embed_f + total.astype(F32)).astype(BF)


def solution(mesh):
    return jax.shard_map(
        shards,
        mesh=mesh,
        in_specs=(
            P(("dp", "expert"), None),
            P(("dp", "expert"), None),
            P(("dp", "expert")),
            P(None, "expert"),
            P("expert", None),
            P(),
            P(None, "expert"),
            P(None, "expert"),
            P("expert", None),
            P("dp", None, "expert"),
            P("dp", None, "expert"),
            P("dp", "expert", None),
            P(("dp", "expert"), None),
            P(("dp", "expert"), None),
        ),
        out_specs=P(("dp", "expert"), None),
        check_vma=False,
    )
```

time: 192 us -> 135 us (0.70)
  matrix products: 34.4 us -> 0.23 us
  waiting for transfers between devices: 93.3 us -> 66.8 us
  blocking collectives: 23.1 us -> 0 us
  Pallas kernels: 0 us -> 22 us
  starting transfers between devices: 23.9 us -> 38.6 us
  other arithmetic: 11.3 us -> 3.6 us
  local copies, waits for them, and re-layouts: 5.22 us -> 2.86 us
    dot_general x11 -> x1, matrix products: 34.4 us -> 0.23 us  [dot(): return jnp.dot(a, b, preferred_element_type=F32)]
    all_to_all x1 -> x0, blocking collectives: 23.1 us -> none  [shards(): slots = lax.all_to_all(send, 'dp', split_axis=0, concat_axis=0, tiled=True)]
    pallas_call x0 -> x10, Pallas kernels: none -> 22 us  [local_kernel(): pl.pallas_call(body, out_shape=list(outs), in_specs=[pl.BlockSpec(memory_...]
    ppermute x14 -> x42, starting transfers between devices: 13.5 us -> 32.8 us  [swap(): return lax.ppermute(rows, axis, [(i, i ^ mask) for i in range(count)])]
    all_to_all x2 -> x1, waiting for transfers between devices: 23 us -> 7.16 us  [shards(): lax.all_to_all(leaving, 'dp', split_axis=0, concat_axis=0, tiled=True)]
    ppermute x14 -> x42, waiting for transfers between devices: 70.3 us -> 59.6 us  [swap(): return lax.ppermute(rows, axis, [(i, i ^ mask) for i in range(count)])]
    another operation x12 -> x1, other arithmetic: 5.07 us -> 0.05 us  [shards(): coef = jnp.stack([coef_hi, (coef - coef_hi.astype(F32)).astype(BF)])]
    all_to_all x2 -> x1, starting transfers between devices: 10.4 us -> 5.81 us  [shards(): lax.all_to_all(leaving, 'dp', split_axis=0, concat_axis=0, tiled=True)]
  transfers between devices with their start and end apart: 16 -> 43, of which waited for: 14 -> 21; matrix products, arithmetic and copies ran while one was open for 7% -> 2% of each run, Pallas kernels for 0% -> 14%
where the time goes in v2:
time: 135 us
  waiting for transfers between devices  66.8 us (49%)
  starting transfers between devices  38.6 us (29%)
  Pallas kernels  22 us (16%)
  other arithmetic  3.6 us (3%)
  local copies, waits for them, and re-layouts  2.86 us (2%)
    ppermute x42, waiting for transfers between devices, swap(): return lax.ppermute(rows, axis, [(i, i ^ mask) for i in range(count)])  59.6 us
    ppermute x42, starting transfers between devices, swap(): return lax.ppermute(rows, axis, [(i, i ^ mask) for i in range(count)])  32.8 us
    pallas_call x10, Pallas kernels, local_kernel(): pl.pallas_call(body, out_shape=list(outs), in_specs=[pl.BlockSpec(memory_...  22 us
    all_to_all x1, waiting for transfers between devices, shards(): lax.all_to_all(leaving, 'dp', split_axis=0, concat_axis=0, tiled=True)  7.16 us
    all_to_all x1, starting transfers between devices, shards(): lax.all_to_all(leaving, 'dp', split_axis=0, concat_axis=0, tiled=True)  5.81 us
  transfers between devices with their start and end apart: 43, of which 21 were waited for; matrix products, arithmetic and copies ran while one was open for 2% of the time, Pallas kernels for 14%

profile of v2, /device:TPU:0, one launch (start us, length us, event | category | flops | bytes accessed | tf_op | source)
XLA Modules:
  0.0 134.5 jit_solution(3210752313262772546)
XLA Ops:
  0.0 0.7 pad_add_fusion.1
  0.7 3.0 %collective-permute-start.5 = (s32[64,4]{0,1:T(4,128)S(1)}, s32[64,4]{0,1:T(4,128)S(1)}, u32[]{:S(2)}, u32[]{:S(2)}) collective-permute-start(s32[64,4]{0,1:T(4,128)S(1)} %pad_add_fusion.1), channel_id=1, source_target_pairs={{0,2},{1,3},{2,0},{3,1},{4,6},{5,7},{6,4},{7,5},{8,10},{9,11},{10,... | collective-permute-start | bytes 3080 | tf_op jit(solution)/shard_map/ppermute | solution.py:22
  3.8 0.4 collective-permute-start.1
  4.2 0.7 fusion.23
  5.0 8.3 %collective-permute-done.refs_1_ = bf16[32,4608]{1,0:T(8,128)(2,1)S(1)} collective-permute-done((bf16[32,4608]{1,0:T(8,128)(2,1)}, bf16[32,4608]{1,0:T(8,128)(2,1)S(1)}, u32[]{:S(2)}, u32[]{:S(2)}) %collective-permute-start) | collective-permute-done | bytes 294944 | tf_op jit(solution)/shard_map/ppermute | solution.py:22
  13.4 1.5 %collective-permute-done.2.refs_3_ = bf16[32,4608]{1,0:T(8,128)(2,1)S(1)} collective-permute-done((bf16[32,4608]{1,0:T(8,128)(2,1)S(1)}, bf16[32,4608]{1,0:T(8,128)(2,1)S(1)}, u32[]{:S(2)}, u32[]{:S(2)}) %collective-permute-start.2) | collective-permute-done | bytes 294944 | tf_op jit(solution)/shard_map/ppermute | solution.py:22
  14.9 1.6 %copy-done.4 = bf16[512,2048]{1,0:T(8,128)(2,1)S(1)} copy-done((bf16[512,2048]{1,0:T(8,128)(2,1)S(1)}, bf16[512,2048]{1,0:T(8,128)(2,1)}, u32[]{:S(2)}) %copy-start.4) | copy-done | bytes 2097176
  16.5 1.0 copy-done.5
  17.4 3.5 %shard_map.136 = (bf16[64,2048]{1,0:T(8,128)(2,1)S(1)}, bf16[64,2048]{1,0:T(8,128)(2,1)S(1)}) custom-call(bf16[32,4608]{1,0:T(8,128)(2,1)S(1)} %copy-done.5, bf16[32,4608]{1,0:T(8,128)(2,1)S(1)} %collective-permute-done.refs_1_, bf16[32,4608]{1,0:T(8,128)(2,1)S(1)} %collective-permute-done.1.refs_2_, bf16[32,4608]{1,0:T(8,128)(2,1)S(1)} %collective-permute-done.2.refs_3_, ...), custom_call_target="tpu_custom_call" | custom-call | flops 872415232 | bytes 8519680 | tf_op jit(solution)/shard_map/pallas_call | solution.py:59
  21.2 0.4 collective-permute-start.7
  21.7 0.9 collective-permute-done.7
  22.8 0.3 collective-permute-start.4
  23.2 5.3 %collective-permute-done.4.other_ref = bf16[32,2048]{1,0:T(8,128)(2,1)S(1)} collective-permute-done((bf16[32,2048]{1,0:T(8,128)(2,1)S(1)}, bf16[32,2048]{1,0:T(8,128)(2,1)S(1)}, u32[]{:S(2)}, u32[]{:S(2)}) %collective-permute-start.4) | collective-permute-done | bytes 131104 | tf_op jit(solution)/shard_map/ppermute | solution.py:22
  28.6 0.8 shard_map.137
  29.4 5.8 %all-to-all-start = ((bf16[8,4,2176]{2,1,0:T(4,128)(2,1)}), bf16[8,4,2176]{2,1,0:T(4,128)(2,1)S(1)}, u32[]{:S(2)}, u32[]{:S(2)}) async-start(bf16[8,4,2176]{2,1,0:T(4,128)(2,1)} %shard_map.137), calls=%async_computation | async-start | bytes 278528 | tf_op jit(solution)/shard_map/all_to_all | solution.py:321
  35.5 7.2 %all-to-all-done.arrived_ref = bf16[8,4,2176]{2,1,0:T(4,128)(2,1)S(1)} async-done(((bf16[8,4,2176]{2,1,0:T(4,128)(2,1)}), bf16[8,4,2176]{2,1,0:T(4,128)(2,1)S(1)}, u32[]{:S(2)}, u32[]{:S(2)}) %all-to-all-start) | async-done | bytes 139296 | tf_op jit(solution)/shard_map/all_to_all | solution.py:321
  42.6 0.6 shard_map.138
  43.2 0.6 collective-permute-start.8
  43.9 5.7 %collective-permute-done.8.refs_2_.refs_1_ = bf16[64,2048]{1,0:T(8,128)(2,1)S(1)} collective-permute-done((bf16[64,2048]{1,0:T(8,128)(2,1)S(1)}, bf16[64,2048]{1,0:T(8,128)(2,1)S(1)}, u32[]{:S(2)}, u32[]{:S(2)}) %collective-permute-start.8) | collective-permute-done | bytes 262176 | tf_op jit(solution)/shard_map/ppermute | solution.py:22
  49.8 1.4 %collective-permute-done.10.refs_4_.refs_3_ = bf16[64,2048]{1,0:T(8,128)(2,1)S(1)} collective-permute-done((bf16[64,2048]{1,0:T(8,128)(2,1)S(1)}, bf16[64,2048]{1,0:T(8,128)(2,1)S(1)}, u32[]{:S(2)}, u32[]{:S(2)}) %collective-permute-start.10) | collective-permute-done | bytes 262176 | tf_op jit(solution)/shard_map/ppermute | solution.py:22
  51.2 0.5 shard_map.139
  51.8 1.4 %collective-permute-start.16 = (bf16[48,2048]{1,0:T(8,128)(2,1)S(1)}, bf16[48,2048]{1,0:T(8,128)(2,1)S(1)}, u32[]{:S(2)}, u32[]{:S(2)}) collective-permute-start(bf16[48,2048]{1,0:T(8,128)(2,1)S(1)} %get-tuple-element.50), channel_id=1, source_target_pairs={{0,4},{4,0},{8,12},{12,8},{16,20},{20,16},{24,28},{28,24},{1,5},{5... | collective-permute-start | bytes 589832 | tf_op jit(solution)/shard_map/ppermute | solution.py:22
  53.2 2.1 %collective-permute-start.18 = (bf16[48,2048]{1,0:T(8,128)(2,1)S(1)}, bf16[48,2048]{1,0:T(8,128)(2,1)S(1)}, u32[]{:S(2)}, u32[]{:S(2)}) collective-permute-start(bf16[48,2048]{1,0:T(8,128)(2,1)S(1)} %get-tuple-element.55), channel_id=1, source_target_pairs={{0,12},{4,8},{8,4},{12,0},{16,28},{20,24},{24,20},{28,16},{1,13},{... | collective-permute-start | bytes 589832 | tf_op jit(solution)/shard_map/ppermute | solution.py:22
  55.3 0.5 collective-permute-start.11
  55.7 2.1 %collective-permute-start.12 = (bf16[24,2048]{1,0:T(8,128)(2,1)S(1)}, bf16[24,2048]{1,0:T(8,128)(2,1)S(1)}, u32[]{:S(2)}, u32[]{:S(2)}) collective-permute-start(bf16[24,2048]{1,0:T(8,128)(2,1)S(1)} %get-tuple-element.43), channel_id=1, source_target_pairs={{0,20},{4,16},{8,28},{12,24},{16,4},{20,0},{24,12},{28,8},{1,21},{... | collective-permute-start | bytes 294920 | tf_op jit(solution)/shard_map/ppermute | solution.py:22
  57.8 5.5 %shard_map.140 = (f32[128,2048]{1,0:T(8,128)S(1)}, f32[128,2048]{1,0:T(8,128)S(1)}) custom-call(bf16[64,2048]{1,0:T(8,128)(2,1)S(1)} %get-tuple-element.41.refs_1_.refs_0_, bf16[64,2048]{1,0:T(8,128)(2,1)S(1)} %collective-permute-done.8.refs_2_.refs_1_, bf16[64,2048]{1,0:T(8,128)(2,1)S(1)} %collective-permute-done.9.refs_3_.refs_2_, ...), custom_call_target="tpu_custom_call" | custom-call | flops 2214592512 | bytes 11796480 | tf_op jit(solution)/shard_map/pallas_call | solution.py:59
  63.4 1.9 %collective-permute-start.31 = (bf16[24,2048]{1,0:T(8,128)(2,1)S(1)}, bf16[24,2048]{1,0:T(8,128)(2,1)S(1)}, u32[]{:S(2)}, u32[]{:S(2)}) collective-permute-start(bf16[24,2048]{1,0:T(8,128)(2,1)S(1)} %get-tuple-element.66), channel_id=1, source_target_pairs={{0,24},{4,28},{8,16},{12,20},{16,8},{20,12},{24,0},{28,4},{1,25},{... | collective-permute-start | bytes 294920 | tf_op jit(solution)/shard_map/ppermute | solution.py:22
  65.4 0.6 collective-permute-start.13
  65.9 4.6 %collective-permute-done.31 = bf16[24,2048]{1,0:T(8,128)(2,1)S(1)} collective-permute-done((bf16[24,2048]{1,0:T(8,128)(2,1)S(1)}, bf16[24,2048]{1,0:T(8,128)(2,1)S(1)}, u32[]{:S(2)}, u32[]{:S(2)}) %collective-permute-start.31) | collective-permute-done | bytes 98336 | tf_op jit(solution)/shard_map/ppermute | solution.py:22
  70.5 1.9 %collective-permute-start.32 = (bf16[24,2048]{1,0:T(8,128)(2,1)S(1)}, bf16[24,2048]{1,0:T(8,128)(2,1)S(1)}, u32[]{:S(2)}, u32[]{:S(2)}) collective-permute-start(bf16[24,2048]{1,0:T(8,128)(2,1)S(1)} %get-tuple-element.67), channel_id=1, source_target_pairs={{0,28},{4,24},{8,20},{12,16},{16,12},{20,8},{24,4},{28,0},{1,29},{... | collective-permute-start | bytes 294920 | tf_op jit(solution)/shard_map/ppermute | solution.py:22
  72.5 0.5 collective-permute-start.20
  73.0 4.8 %collective-permute-done.32 = bf16[24,2048]{1,0:T(8,128)(2,1)S(1)} collective-permute-done((bf16[24,2048]{1,0:T(8,128)(2,1)S(1)}, bf16[24,2048]{1,0:T(8,128)(2,1)S(1)}, u32[]{:S(2)}, u32[]{:S(2)}) %collective-permute-start.32) | collective-permute-done | bytes 98336 | tf_op jit(solution)/shard_map/ppermute | solution.py:22
  77.8 0.5 collective-permute-start.15
  78.3 0.6 collective-permute-start.33
  78.9 0.3 collective-permute-done.22.refs_7_
  79.3 4.6 %shard_map.141 = (bf16[192,2048]{1,0:T(8,128)(2,1)S(1)}, bf16[192,2048]{1,0:T(8,128)(2,1)S(1)}) custom-call(bf16[48,2048]{1,0:T(8,128)(2,1)S(1)} %get-tuple-element.48.refs_0_, bf16[48,2048]{1,0:T(8,128)(2,1)S(1)} %collective-permute-done.16.refs_1_, bf16[48,2048]{1,0:T(8,128)(2,1)S(1)} %collective-permute-done.17.refs_2_, ...), custom_call_target="tpu_custom_call" | custom-call | flops 1660944384 | bytes 7471104 | tf_op jit(solution)/shard_map/pallas_call | solution.py:59
  83.9 2.5 %shard_map.142 = (bf16[96,2048]{1,0:T(8,128)(2,1)S(1)}, bf16[96,2048]{1,0:T(8,128)(2,1)S(1)}) custom-call(bf16[48,2048]{1,0:T(8,128)(2,1)S(1)} %pad_maximum_fusion.1.refs_0_, bf16[48,2048]{1,0:T(8,128)(2,1)S(1)} %collective-permute-done.13.refs_1_, bf16[48,2048]{1,0:T(8,128)(2,1)S(1)} %collective-permute-done.14.refs_2_, ...), custom_call_target="tpu_custom_call" | custom-call | flops 830472192 | bytes 5898240 | tf_op jit(solution)/shard_map/pallas_call | solution.py:59
  86.7 0.4 collective-permute-start.34
  87.4 0.4 collective-permute-start.23
  87.8 0.7 collective-permute-done.34.refs_2_
  88.5 0.3 collective-permute-done.35.refs_3_
  88.8 2.5 %shard_map.143 = (bf16[96,2048]{1,0:T(8,128)(2,1)S(1)}, bf16[96,2048]{1,0:T(8,128)(2,1)S(1)}) custom-call(bf16[48,2048]{1,0:T(8,128)(2,1)S(1)} %constant_dynamic-update-slice_fusion.refs_0_, bf16[48,2048]{1,0:T(8,128)(2,1)S(1)} %collective-permute-done.33.refs_1_, bf16[48,2048]{1,0:T(8,128)(2,1)S(1)} %collective-permute-done.34.refs_2_, ...), custom_call_target="tpu_custom_call" | custom-call | flops 830472192 | bytes 5898240 | tf_op jit(solution)/shard_map/pallas_call | solution.py:59
  91.7 1.3 collective-permute-start.28
  93.3 1.3 collective-permute-start.37
  94.5 4.9 %collective-permute-done.28 = bf16[48,2048]{1,0:T(8,128)(2,1)S(1)} collective-permute-done((bf16[48,2048]{1,0:T(8,128)(2,1)S(1)}, bf16[48,2048]{1,0:T(8,128)(2,1)S(1)}, u32[]{:S(2)}, u32[]{:S(2)}) %collective-permute-start.28) | collective-permute-done | bytes 196640 | tf_op jit(solution)/shard_map/ppermute | solution.py:22
  99.6 2.1 %collective-permute-start.29 = (bf16[24,2048]{1,0:T(8,128)(2,1)S(1)}, bf16[24,2048]{1,0:T(8,128)(2,1)S(1)}, u32[]{:S(2)}, u32[]{:S(2)}) collective-permute-start(bf16[24,2048]{1,0:T(8,128)(2,1)S(1)} %get-tuple-element.82), channel_id=1, source_target_pairs={{0,16},{4,20},{8,24},{12,28},{16,0},{20,4},{24,8},{28,12},{1,17},{... | collective-permute-start | bytes 294920 | tf_op jit(solution)/shard_map/ppermute | solution.py:22
  101.7 2.1 %collective-permute-start.30 = (bf16[24,2048]{1,0:T(8,128)(2,1)S(1)}, bf16[24,2048]{1,0:T(8,128)(2,1)S(1)}, u32[]{:S(2)}, u32[]{:S(2)}) collective-permute-start(bf16[24,2048]{1,0:T(8,128)(2,1)S(1)} %get-tuple-element.81), channel_id=1, source_target_pairs={{0,20},{4,16},{8,28},{12,24},{16,4},{20,0},{24,12},{28,8},{1,21},{... | collective-permute-start | bytes 294920 | tf_op jit(solution)/shard_map/ppermute | solution.py:22
  103.8 0.3 add_convert_fusion
  104.2 0.3 collective-permute-start.24
  104.4 1.4 %collective-permute-start.25 = (bf16[48,2048]{1,0:T(8,128)(2,1)S(1)}, bf16[48,2048]{1,0:T(8,128)(2,1)S(1)}, u32[]{:S(2)}, u32[]{:S(2)}) collective-permute-start(bf16[48,2048]{1,0:T(8,128)(2,1)S(1)} %get-tuple-element.72), channel_id=1, source_target_pairs={{0,8},{4,12},{8,0},{12,4},{16,24},{20,28},{24,16},{28,20},{1,9},{5... | collective-permute-start | bytes 589832 | tf_op jit(solution)/shard_map/ppermute | solution.py:22
  105.8 1.9 %collective-permute-start.26 = (bf16[48,2048]{1,0:T(8,128)(2,1)S(1)}, bf16[48,2048]{1,0:T(8,128)(2,1)S(1)}, u32[]{:S(2)}, u32[]{:S(2)}) collective-permute-start(bf16[48,2048]{1,0:T(8,128)(2,1)S(1)} %get-tuple-element.71), channel_id=1, source_target_pairs={{0,12},{4,8},{8,4},{12,0},{16,28},{20,24},{24,20},{28,16},{1,13},{... | collective-permute-start | bytes 589832 | tf_op jit(solution)/shard_map/ppermute | solution.py:22
  107.8 1.7 %collective-permute-done.29.refs_6_ = bf16[24,2048]{1,0:T(8,128)(2,1)S(1)} collective-permute-done((bf16[24,2048]{1,0:T(8,128)(2,1)S(1)}, bf16[24,2048]{1,0:T(8,128)(2,1)S(1)}, u32[]{:S(2)}, u32[]{:S(2)}) %collective-permute-start.29) | collective-permute-done | bytes 98336 | tf_op jit(solution)/shard_map/ppermute | solution.py:22
  109.5 0.7 collective-permute-start.38
  110.2 2.5 %collective-permute-done.30.refs_7_ = bf16[24,2048]{1,0:T(8,128)(2,1)S(1)} collective-permute-done((bf16[24,2048]{1,0:T(8,128)(2,1)S(1)}, bf16[24,2048]{1,0:T(8,128)(2,1)S(1)}, u32[]{:S(2)}, u32[]{:S(2)}) %collective-permute-start.30) | collective-permute-done | bytes 98336 | tf_op jit(solution)/shard_map/ppermute | solution.py:22
  112.7 1.8 %collective-permute-start.39 = (bf16[24,2048]{1,0:T(8,128)(2,1)S(1)}, bf16[24,2048]{1,0:T(8,128)(2,1)S(1)}, u32[]{:S(2)}, u32[]{:S(2)}) collective-permute-start(bf16[24,2048]{1,0:T(8,128)(2,1)S(1)} %get-tuple-element.79), channel_id=1, source_target_pairs={{0,28},{4,24},{8,20},{12,16},{16,12},{20,8},{24,4},{28,0},{1,29},{... | collective-permute-start | bytes 294920 | tf_op jit(solution)/shard_map/ppermute | solution.py:22
  114.6 4.5 %collective-permute-done.38.refs_8_ = bf16[24,2048]{1,0:T(8,128)(2,1)S(1)} collective-permute-done((bf16[24,2048]{1,0:T(8,128)(2,1)S(1)}, bf16[24,2048]{1,0:T(8,128)(2,1)S(1)}, u32[]{:S(2)}, u32[]{:S(2)}) %collective-permute-start.38) | collective-permute-done | bytes 98336 | tf_op jit(solution)/shard_map/ppermute | solution.py:22
  119.0 2.1 %collective-permute-done.39.refs_9_ = bf16[24,2048]{1,0:T(8,128)(2,1)S(1)} collective-permute-done((bf16[24,2048]{1,0:T(8,128)(2,1)S(1)}, bf16[24,2048]{1,0:T(8,128)(2,1)S(1)}, u32[]{:S(2)}, u32[]{:S(2)}) %collective-permute-start.39) | collective-permute-done | bytes 98336 | tf_op jit(solution)/shard_map/ppermute | solution.py:22
  121.1 1.4 %collective-permute-done.26.refs_5_ = bf16[48,2048]{1,0:T(8,128)(2,1)S(1)} collective-permute-done((bf16[48,2048]{1,0:T(8,128)(2,1)S(1)}, bf16[48,2048]{1,0:T(8,128)(2,1)S(1)}, u32[]{:S(2)}, u32[]{:S(2)}) %collective-permute-start.26) | collective-permute-done | bytes 196640 | tf_op jit(solution)/shard_map/ppermute | solution.py:22
  122.5 0.7 shard_map.145
  123.3 0.7 shard_map.144
  124.0 1.2 collective-permute-done.40
  125.3 1.3 collective-permute-start.41
  126.6 7.1 %collective-permute-done.41 = bf16[64,2048]{1,0:T(8,128)(2,1)S(1)} collective-permute-done((bf16[64,2048]{1,0:T(8,128)(2,1)S(1)}, bf16[64,2048]{1,0:T(8,128)(2,1)S(1)}, u32[]{:S(2)}, u32[]{:S(2)}) %collective-permute-start.41) | collective-permute-done | bytes 262176 | tf_op jit(solution)/shard_map/ppermute | solution.py:22
  133.7 0.8 add_convert_fusion.4
  (90 shorter events, 3.2 us)
Async XLA Ops:
  0.7 20.5 %collective-permute-start.5 = (s32[64,4]{0,1:T(4,128)S(1)}, s32[64,4]{0,1:T(4,128)S(1)}, u32[]{:S(2)}, u32[]{:S(2)}) collective-permute-start(s32[64,4]{0,1:T(4,128)S(1)} %pad_add_fusion.1), channel_id=1, source_target_pairs={{0,2},{1,3},{2,0},{3,1},{4,6},{5,7},{6,4},{7,5},{8,10},{9,11},{10,... | collective-permute-start | bytes 3080 | tf_op jit(solution)/shard_map/ppermute | solution.py:22
  3.7 18.0 %collective-permute-start.6 = (s32[64,4]{0,1:T(4,128)S(1)}, s32[64,4]{0,1:T(4,128)S(1)}, u32[]{:S(2)}, u32[]{:S(2)}) collective-permute-start(s32[64,4]{0,1:T(4,128)S(1)} %pad_add_fusion.1), channel_id=1, source_target_pairs={{0,1},{1,0},{2,3},{3,2},{4,5},{5,4},{6,7},{7,6},{8,9},{9,8},{10,11... | collective-permute-start | bytes 3080 | tf_op jit(solution)/shard_map/ppermute | solution.py:22
  3.7 9.6 %collective-permute-start = (bf16[32,4608]{1,0:T(8,128)(2,1)}, bf16[32,4608]{1,0:T(8,128)(2,1)S(1)}, u32[]{:S(2)}, u32[]{:S(2)}) collective-permute-start(bf16[32,4608]{1,0:T(8,128)(2,1)} %refs_0_.1), channel_id=1, source_target_pairs={{0,2},{1,3},{2,0},{3,1},{4,6},{5,7},{6,4},{7,5},{8,10},{9,11},{10,... | collective-permute-start | bytes 884744 | tf_op jit(solution)/shard_map/ppermute | solution.py:22
  3.8 9.5 %collective-permute-start.1 = (bf16[32,4608]{1,0:T(8,128)(2,1)}, bf16[32,4608]{1,0:T(8,128)(2,1)S(1)}, u32[]{:S(2)}, u32[]{:S(2)}) collective-permute-start(bf16[32,4608]{1,0:T(8,128)(2,1)} %refs_0_.1), channel_id=1, source_target_pairs={{0,1},{1,0},{2,3},{3,2},{4,5},{5,4},{6,7},{7,6},{8,9},{9,8},{10,11... | collective-permute-start | bytes 884744 | tf_op jit(solution)/shard_map/ppermute | solution.py:22
  13.3 1.6 %collective-permute-start.2 = (bf16[32,4608]{1,0:T(8,128)(2,1)S(1)}, bf16[32,4608]{1,0:T(8,128)(2,1)S(1)}, u32[]{:S(2)}, u32[]{:S(2)}) collective-permute-start(bf16[32,4608]{1,0:T(8,128)(2,1)S(1)} %collective-permute-done.refs_1_), channel_id=1, source_target_pairs={{0,1},{1,0},{2,3},{3,2},{4,5},{5,4},{6,7},{7,6},{8,9},{9,8},{10,11... | collective-permute-start | bytes 884744 | tf_op jit(solution)/shard_map/ppermute | solution.py:22
  13.3 9.3 %copy-start.8 = (s32[64,2]{0,1:T(2,128)S(1)}, s32[64,2]{0,1:T(2,128)}, u32[]{:S(2)}) copy-start(s32[64,2]{0,1:T(2,128)} %param.27) | copy-start | bytes 1540
  13.3 9.3 %copy-start.9 = (s32[64,2]{0,1:T(2,128)S(1)}, s32[64,2]{0,1:T(2,128)}, u32[]{:S(2)}) copy-start(s32[64,2]{0,1:T(2,128)} %param.26) | copy-start | bytes 1540
  14.9 1.6 %copy-start.4 = (bf16[512,2048]{1,0:T(8,128)(2,1)S(1)}, bf16[512,2048]{1,0:T(8,128)(2,1)}, u32[]{:S(2)}) copy-start(bf16[512,2048]{1,0:T(8,128)(2,1)} %refs_5_.1) | copy-start | bytes 6291460
  16.5 1.0 copy-start.5
  21.0 21.6 %copy-start.6 = (bf16[64,2048]{1,0:T(8,128)(2,1)S(1)}, bf16[64,2048]{1,0:T(8,128)(2,1)}, u32[]{:S(2)}) copy-start(bf16[64,2048]{1,0:T(8,128)(2,1)} %text_ref.1) | copy-start | bytes 786436
  21.0 21.6 %copy-start.7 = (f32[2048]{0:T(1024)S(1)}, f32[2048]{0:T(1024)}, u32[]{:S(2)}) copy-start(f32[2048]{0:T(1024)} %param.19) | copy-start | bytes 24580
  21.0 1.7 %collective-permute-start.3 = (bf16[64,2048]{1,0:T(8,128)(2,1)S(1)}, bf16[64,2048]{1,0:T(8,128)(2,1)S(1)}, u32[]{:S(2)}, u32[]{:S(2)}) collective-permute-start(bf16[64,2048]{1,0:T(8,128)(2,1)S(1)} %get-tuple-element.39), channel_id=1, source_target_pairs={{0,1},{1,0},{2,3},{3,2},{4,5},{5,4},{6,7},{7,6},{8,9},{9,8},{10,11... | collective-permute-start | bytes 786440 | tf_op jit(solution)/shard_map/ppermute | solution.py:22
  21.2 1.4 %collective-permute-start.7 = (s32[64,4]{0,1:T(4,128)S(1)}, s32[64,4]{0,1:T(4,128)S(1)}, u32[]{:S(2)}, u32[]{:S(2)}) collective-permute-start(s32[64,4]{0,1:T(4,128)S(1)} %collective-permute-done.5), channel_id=1, source_target_pairs={{0,1},{1,0},{2,3},{3,2},{4,5},{5,4},{6,7},{7,6},{8,9},{9,8},{10,11... | collective-permute-start | bytes 3080 | tf_op jit(solution)/shard_map/ppermute | solution.py:22
  22.8 35.0 %copy-start.3 = (bf16[2048,704]{0,1:T(8,128)(2,1)S(1)}, bf16[2048,704]{0,1:T(8,128)(2,1)}, u32[]{:S(2)}) copy-start(bf16[2048,704]{0,1:T(8,128)(2,1)} %param.20) | copy-start | bytes 8650756
  22.8 5.7 %collective-permute-start.4 = (bf16[32,2048]{1,0:T(8,128)(2,1)S(1)}, bf16[32,2048]{1,0:T(8,128)(2,1)S(1)}, u32[]{:S(2)}, u32[]{:S(2)}) collective-permute-start(bf16[32,2048]{1,0:T(8,128)(2,1)S(1)} %get-tuple-element.77), channel_id=1, source_target_pairs={{0,2},{1,3},{2,0},{3,1},{4,6},{5,7},{6,4},{7,5},{8,10},{9,11},{10,... | collective-permute-start | bytes 393224 | tf_op jit(solution)/shard_map/ppermute | solution.py:22
  29.4 13.2 %all-to-all-start = ((bf16[8,4,2176]{2,1,0:T(4,128)(2,1)}), bf16[8,4,2176]{2,1,0:T(4,128)(2,1)S(1)}, u32[]{:S(2)}, u32[]{:S(2)}) async-start(bf16[8,4,2176]{2,1,0:T(4,128)(2,1)} %shard_map.137), calls=%async_computation | async-start | bytes 278528 | tf_op jit(solution)/shard_map/all_to_all | solution.py:321
  43.2 6.4 %collective-permute-start.8 = (bf16[64,2048]{1,0:T(8,128)(2,1)S(1)}, bf16[64,2048]{1,0:T(8,128)(2,1)S(1)}, u32[]{:S(2)}, u32[]{:S(2)}) collective-permute-start(bf16[64,2048]{1,0:T(8,128)(2,1)S(1)} %get-tuple-element.41.refs_1_.refs_0_), channel_id=1, source_target_pairs={{0,2},{1,3},{2,0},{3,1},{4,6},{5,7},{6,4},{7,5},{8,10},{9,11},{10,... | collective-permute-start | bytes 786440 | tf_op jit(solution)/shard_map/ppermute | solution.py:22
  43.8 5.9 %collective-permute-start.9 = (bf16[64,2048]{1,0:T(8,128)(2,1)S(1)}, bf16[64,2048]{1,0:T(8,128)(2,1)S(1)}, u32[]{:S(2)}, u32[]{:S(2)}) collective-permute-start(bf16[64,2048]{1,0:T(8,128)(2,1)S(1)} %get-tuple-element.41.refs_1_.refs_0_), channel_id=1, source_target_pairs={{0,1},{1,0},{2,3},{3,2},{4,5},{5,4},{6,7},{7,6},{8,9},{9,8},{10,11... | collective-permute-start | bytes 786440 | tf_op jit(solution)/shard_map/ppermute | solution.py:22
  49.7 1.5 %collective-permute-start.10 = (bf16[64,2048]{1,0:T(8,128)(2,1)S(1)}, bf16[64,2048]{1,0:T(8,128)(2,1)S(1)}, u32[]{:S(2)}, u32[]{:S(2)}) collective-permute-start(bf16[64,2048]{1,0:T(8,128)(2,1)S(1)} %collective-permute-done.8.refs_2_.refs_1_), channel_id=1, source_target_pairs={{0,1},{1,0},{2,3},{3,2},{4,5},{5,4},{6,7},{7,6},{8,9},{9,8},{10,11... | collective-permute-start | bytes 786440 | tf_op jit(solution)/shard_map/ppermute | solution.py:22
  51.7 14.2 %collective-permute-start.17 = (bf16[48,2048]{1,0:T(8,128)(2,1)S(1)}, bf16[48,2048]{1,0:T(8,128)(2,1)S(1)}, u32[]{:S(2)}, u32[]{:S(2)}) collective-permute-start(bf16[48,2048]{1,0:T(8,128)(2,1)S(1)} %get-tuple-element.53), channel_id=1, source_target_pairs={{0,8},{4,12},{8,0},{12,4},{16,24},{20,28},{24,16},{28,20},{1,9},{5... | collective-permute-start | bytes 589832 | tf_op jit(solution)/shard_map/ppermute | solution.py:22
  51.8 11.5 %collective-permute-start.16 = (bf16[48,2048]{1,0:T(8,128)(2,1)S(1)}, bf16[48,2048]{1,0:T(8,128)(2,1)S(1)}, u32[]{:S(2)}, u32[]{:S(2)}) collective-permute-start(bf16[48,2048]{1,0:T(8,128)(2,1)S(1)} %get-tuple-element.50), channel_id=1, source_target_pairs={{0,4},{4,0},{8,12},{12,8},{16,20},{20,16},{24,28},{28,24},{1,5},{5... | collective-permute-start | bytes 589832 | tf_op jit(solution)/shard_map/ppermute | solution.py:22
  53.2 19.2 %collective-permute-start.18 = (bf16[48,2048]{1,0:T(8,128)(2,1)S(1)}, bf16[48,2048]{1,0:T(8,128)(2,1)S(1)}, u32[]{:S(2)}, u32[]{:S(2)}) collective-permute-start(bf16[48,2048]{1,0:T(8,128)(2,1)S(1)} %get-tuple-element.55), channel_id=1, source_target_pairs={{0,12},{4,8},{8,4},{12,0},{16,28},{20,24},{24,20},{28,16},{1,13},{... | collective-permute-start | bytes 589832 | tf_op jit(solution)/shard_map/ppermute | solution.py:22
  55.3 8.1 %collective-permute-start.11 = (bf16[24,2048]{1,0:T(8,128)(2,1)S(1)}, bf16[24,2048]{1,0:T(8,128)(2,1)S(1)}, u32[]{:S(2)}, u32[]{:S(2)}) collective-permute-start(bf16[24,2048]{1,0:T(8,128)(2,1)S(1)} %get-tuple-element.42), channel_id=1, source_target_pairs={{0,16},{4,20},{8,24},{12,28},{16,0},{20,4},{24,8},{28,12},{1,17},{... | collective-permute-start | bytes 294920 | tf_op jit(solution)/shard_map/ppermute | solution.py:22
  55.7 9.6 %collective-permute-start.12 = (bf16[24,2048]{1,0:T(8,128)(2,1)S(1)}, bf16[24,2048]{1,0:T(8,128)(2,1)S(1)}, u32[]{:S(2)}, u32[]{:S(2)}) collective-permute-start(bf16[24,2048]{1,0:T(8,128)(2,1)S(1)} %get-tuple-element.43), channel_id=1, source_target_pairs={{0,20},{4,16},{8,28},{12,24},{16,4},{20,0},{24,12},{28,8},{1,21},{... | collective-permute-start | bytes 294920 | tf_op jit(solution)/shard_map/ppermute | solution.py:22
  57.8 21.4 %copy-start = (bf16[1,2048,352]{1,2,0:T(8,128)(2,1)S(1)}, bf16[1,2048,352]{1,2,0:T(8,128)(2,1)}, u32[]{:S(2)}) copy-start(bf16[1,2048,352]{1,2,0:T(8,128)(2,1)} %param.23) | copy-start | bytes 4325380
  57.8 21.4 %copy-start.1 = (bf16[1,2048,352]{1,2,0:T(8,128)(2,1)S(1)}, bf16[1,2048,352]{1,2,0:T(8,128)(2,1)}, u32[]{:S(2)}) copy-start(bf16[1,2048,352]{1,2,0:T(8,128)(2,1)} %param.24) | copy-start | bytes 4325380
  63.3 9.2 %collective-permute-start.19 = (bf16[48,2048]{1,0:T(8,128)(2,1)S(1)}, bf16[48,2048]{1,0:T(8,128)(2,1)S(1)}, u32[]{:S(2)}, u32[]{:S(2)}) collective-permute-start(bf16[48,2048]{1,0:T(8,128)(2,1)S(1)} %get-tuple-element.48.refs_0_), channel_id=1, source_target_pairs={{0,1},{1,0},{2,3},{3,2},{4,5},{5,4},{6,7},{7,6},{8,9},{9,8},{10,11... | collective-permute-start | bytes 589832 | tf_op jit(solution)/shard_map/ppermute | solution.py:22
  63.4 7.1 %collective-permute-start.31 = (bf16[24,2048]{1,0:T(8,128)(2,1)S(1)}, bf16[24,2048]{1,0:T(8,128)(2,1)S(1)}, u32[]{:S(2)}, u32[]{:S(2)}) collective-permute-start(bf16[24,2048]{1,0:T(8,128)(2,1)S(1)} %get-tuple-element.66), channel_id=1, source_target_pairs={{0,24},{4,28},{8,16},{12,20},{16,8},{20,12},{24,0},{28,4},{1,25},{... | collective-permute-start | bytes 294920 | tf_op jit(solution)/shard_map/ppermute | solution.py:22
  65.4 12.5 %collective-permute-start.13 = (bf16[48,2048]{1,0:T(8,128)(2,1)S(1)}, bf16[48,2048]{1,0:T(8,128)(2,1)S(1)}, u32[]{:S(2)}, u32[]{:S(2)}) collective-permute-start(bf16[48,2048]{1,0:T(8,128)(2,1)S(1)} %pad_maximum_fusion.1.refs_0_), channel_id=1, source_target_pairs={{0,2},{1,3},{2,0},{3,1},{4,6},{5,7},{6,4},{7,5},{8,10},{9,11},{10,... | collective-permute-start | bytes 589832 | tf_op jit(solution)/shard_map/ppermute | solution.py:22
  65.9 18.0 %collective-permute-start.14 = (bf16[48,2048]{1,0:T(8,128)(2,1)S(1)}, bf16[48,2048]{1,0:T(8,128)(2,1)S(1)}, u32[]{:S(2)}, u32[]{:S(2)}) collective-permute-start(bf16[48,2048]{1,0:T(8,128)(2,1)S(1)} %pad_maximum_fusion.1.refs_0_), channel_id=1, source_target_pairs={{0,1},{1,0},{2,3},{3,2},{4,5},{5,4},{6,7},{7,6},{8,9},{9,8},{10,11... | collective-permute-start | bytes 589832 | tf_op jit(solution)/shard_map/ppermute | solution.py:22
  70.5 7.3 %collective-permute-start.32 = (bf16[24,2048]{1,0:T(8,128)(2,1)S(1)}, bf16[24,2048]{1,0:T(8,128)(2,1)S(1)}, u32[]{:S(2)}, u32[]{:S(2)}) collective-permute-start(bf16[24,2048]{1,0:T(8,128)(2,1)S(1)} %get-tuple-element.67), channel_id=1, source_target_pairs={{0,28},{4,24},{8,20},{12,16},{16,12},{20,8},{24,4},{28,0},{1,29},{... | collective-permute-start | bytes 294920 | tf_op jit(solution)/shard_map/ppermute | solution.py:22
  72.4 5.9 %collective-permute-start.21 = (bf16[48,2048]{1,0:T(8,128)(2,1)S(1)}, bf16[48,2048]{1,0:T(8,128)(2,1)S(1)}, u32[]{:S(2)}, u32[]{:S(2)}) collective-permute-start(bf16[48,2048]{1,0:T(8,128)(2,1)S(1)} %collective-permute-done.17.refs_2_), channel_id=1, source_target_pairs={{0,1},{1,0},{2,3},{3,2},{4,5},{5,4},{6,7},{7,6},{8,9},{9,8},{10,11... | collective-permute-start | bytes 589832 | tf_op jit(solution)/shard_map/ppermute | solution.py:22
  72.5 6.4 %collective-permute-start.20 = (bf16[48,2048]{1,0:T(8,128)(2,1)S(1)}, bf16[48,2048]{1,0:T(8,128)(2,1)S(1)}, u32[]{:S(2)}, u32[]{:S(2)}) collective-permute-start(bf16[48,2048]{1,0:T(8,128)(2,1)S(1)} %collective-permute-done.16.refs_1_), channel_id=1, source_target_pairs={{0,1},{1,0},{2,3},{3,2},{4,5},{5,4},{6,7},{7,6},{8,9},{9,8},{10,11... | collective-permute-start | bytes 589832 | tf_op jit(solution)/shard_map/ppermute | solution.py:22
  77.8 1.4 %collective-permute-start.22 = (bf16[48,2048]{1,0:T(8,128)(2,1)S(1)}, bf16[48,2048]{1,0:T(8,128)(2,1)S(1)}, u32[]{:S(2)}, u32[]{:S(2)}) collective-permute-start(bf16[48,2048]{1,0:T(8,128)(2,1)S(1)} %collective-permute-done.18.refs_3_), channel_id=1, source_target_pairs={{0,1},{1,0},{2,3},{3,2},{4,5},{5,4},{6,7},{7,6},{8,9},{9,8},{10,11... | collective-permute-start | bytes 589832 | tf_op jit(solution)/shard_map/ppermute | solution.py:22
  77.8 6.1 %collective-permute-start.15 = (bf16[48,2048]{1,0:T(8,128)(2,1)S(1)}, bf16[48,2048]{1,0:T(8,128)(2,1)S(1)}, u32[]{:S(2)}, u32[]{:S(2)}) collective-permute-start(bf16[48,2048]{1,0:T(8,128)(2,1)S(1)} %collective-permute-done.13.refs_1_), channel_id=1, source_target_pairs={{0,1},{1,0},{2,3},{3,2},{4,5},{5,4},{6,7},{7,6},{8,9},{9,8},{10,11... | collective-permute-start | bytes 589832 | tf_op jit(solution)/shard_map/ppermute | solution.py:22
  78.3 8.7 %collective-permute-start.33 = (bf16[48,2048]{1,0:T(8,128)(2,1)S(1)}, bf16[48,2048]{1,0:T(8,128)(2,1)S(1)}, u32[]{:S(2)}, u32[]{:S(2)}) collective-permute-start(bf16[48,2048]{1,0:T(8,128)(2,1)S(1)} %constant_dynamic-update-slice_fusion.refs_0_), channel_id=1, source_target_pairs={{0,2},{1,3},{2,0},{3,1},{4,6},{5,7},{6,4},{7,5},{8,10},{9,11},{10,... | collective-permute-start | bytes 589832 | tf_op jit(solution)/shard_map/ppermute | solution.py:22
  79.3 4.7 %copy-start.2 = (bf16[1,352,2048]{2,1,0:T(8,128)(2,1)S(1)}, bf16[1,352,2048]{2,1,0:T(8,128)(2,1)}, u32[]{:S(2)}) copy-start(bf16[1,352,2048]{2,1,0:T(8,128)(2,1)} %param.25) | copy-start | bytes 4325380
  86.5 5.1 %collective-permute-start.27 = (bf16[96,2048]{1,0:T(8,128)(2,1)S(1)}, bf16[96,2048]{1,0:T(8,128)(2,1)S(1)}, u32[]{:S(2)}, u32[]{:S(2)}) collective-permute-start(bf16[96,2048]{1,0:T(8,128)(2,1)S(1)} %get-tuple-element.65), channel_id=1, source_target_pairs={{0,1},{1,0},{2,3},{3,2},{4,5},{5,4},{6,7},{7,6},{8,9},{9,8},{10,11... | collective-permute-start | bytes 1179656 | tf_op jit(solution)/shard_map/ppermute | solution.py:22
  86.7 1.9 %collective-permute-start.34 = (bf16[48,2048]{1,0:T(8,128)(2,1)S(1)}, bf16[48,2048]{1,0:T(8,128)(2,1)S(1)}, u32[]{:S(2)}, u32[]{:S(2)}) collective-permute-start(bf16[48,2048]{1,0:T(8,128)(2,1)S(1)} %constant_dynamic-update-slice_fusion.refs_0_), channel_id=1, source_target_pairs={{0,1},{1,0},{2,3},{3,2},{4,5},{5,4},{6,7},{7,6},{8,9},{9,8},{10,11... | collective-permute-start | bytes 589832 | tf_op jit(solution)/shard_map/ppermute | solution.py:22
  87.1 1.8 %collective-permute-start.35 = (bf16[48,2048]{1,0:T(8,128)(2,1)S(1)}, bf16[48,2048]{1,0:T(8,128)(2,1)S(1)}, u32[]{:S(2)}, u32[]{:S(2)}) collective-permute-start(bf16[48,2048]{1,0:T(8,128)(2,1)S(1)} %collective-permute-done.33.refs_1_), channel_id=1, source_target_pairs={{0,1},{1,0},{2,3},{3,2},{4,5},{5,4},{6,7},{7,6},{8,9},{9,8},{10,11... | collective-permute-start | bytes 589832 | tf_op jit(solution)/shard_map/ppermute | solution.py:22
  87.4 16.4 %collective-permute-start.23 = (bf16[192,2048]{1,0:T(8,128)(2,1)S(1)}, bf16[192,2048]{1,0:T(8,128)(2,1)S(1)}, u32[]{:S(2)}, u32[]{:S(2)}) collective-permute-start(bf16[192,2048]{1,0:T(8,128)(2,1)S(1)} %get-tuple-element.59), channel_id=1, source_target_pairs={{0,1},{1,0},{2,3},{3,2},{4,5},{5,4},{6,7},{7,6},{8,9},{9,8},{10,11... | collective-permute-start | bytes 2359304 | tf_op jit(solution)/shard_map/ppermute | solution.py:22
  91.3 1.8 %collective-permute-start.36 = (bf16[96,2048]{1,0:T(8,128)(2,1)S(1)}, bf16[96,2048]{1,0:T(8,128)(2,1)S(1)}, u32[]{:S(2)}, u32[]{:S(2)}) collective-permute-start(bf16[96,2048]{1,0:T(8,128)(2,1)S(1)} %get-tuple-element.69), channel_id=1, source_target_pairs={{0,1},{1,0},{2,3},{3,2},{4,5},{5,4},{6,7},{7,6},{8,9},{9,8},{10,11... | collective-permute-start | bytes 1179656 | tf_op jit(solution)/shard_map/ppermute | solution.py:22
  91.7 7.8 %collective-permute-start.28 = (bf16[48,2048]{1,0:T(8,128)(2,1)S(1)}, bf16[48,2048]{1,0:T(8,128)(2,1)S(1)}, u32[]{:S(2)}, u32[]{:S(2)}) collective-permute-start(bf16[48,2048]{1,0:T(8,128)(2,1)S(1)} %slice.111), channel_id=1, source_target_pairs={{0,2},{1,3},{2,0},{3,1},{4,6},{5,7},{6,4},{7,5},{8,10},{9,11},{10,... | collective-permute-start | bytes 589832 | tf_op jit(solution)/shard_map/ppermute | solution.py:22
  93.3 12.6 %collective-permute-start.37 = (bf16[48,2048]{1,0:T(8,128)(2,1)S(1)}, bf16[48,2048]{1,0:T(8,128)(2,1)S(1)}, u32[]{:S(2)}, u32[]{:S(2)}) collective-permute-start(bf16[48,2048]{1,0:T(8,128)(2,1)S(1)} %slice.115), channel_id=1, source_target_pairs={{0,2},{1,3},{2,0},{3,1},{4,6},{5,7},{6,4},{7,5},{8,10},{9,11},{10,... | collective-permute-start | bytes 589832 | tf_op jit(solution)/shard_map/ppermute | solution.py:22
  99.6 10.0 %collective-permute-start.29 = (bf16[24,2048]{1,0:T(8,128)(2,1)S(1)}, bf16[24,2048]{1,0:T(8,128)(2,1)S(1)}, u32[]{:S(2)}, u32[]{:S(2)}) collective-permute-start(bf16[24,2048]{1,0:T(8,128)(2,1)S(1)} %get-tuple-element.82), channel_id=1, source_target_pairs={{0,16},{4,20},{8,24},{12,28},{16,0},{20,4},{24,8},{28,12},{1,17},{... | collective-permute-start | bytes 294920 | tf_op jit(solution)/shard_map/ppermute | solution.py:22
  101.7 11.1 %collective-permute-start.30 = (bf16[24,2048]{1,0:T(8,128)(2,1)S(1)}, bf16[24,2048]{1,0:T(8,128)(2,1)S(1)}, u32[]{:S(2)}, u32[]{:S(2)}) collective-permute-start(bf16[24,2048]{1,0:T(8,128)(2,1)S(1)} %get-tuple-element.81), channel_id=1, source_target_pairs={{0,20},{4,16},{8,28},{12,24},{16,4},{20,0},{24,12},{28,8},{1,21},{... | collective-permute-start | bytes 294920 | tf_op jit(solution)/shard_map/ppermute | solution.py:22
  104.2 16.9 %collective-permute-start.24 = (bf16[48,2048]{1,0:T(8,128)(2,1)S(1)}, bf16[48,2048]{1,0:T(8,128)(2,1)S(1)}, u32[]{:S(2)}, u32[]{:S(2)}) collective-permute-start(bf16[48,2048]{1,0:T(8,128)(2,1)S(1)} %get-tuple-element.73), channel_id=1, source_target_pairs={{0,4},{4,0},{8,12},{12,8},{16,20},{20,16},{24,28},{28,24},{1,5},{5... | collective-permute-start | bytes 589832 | tf_op jit(solution)/shard_map/ppermute | solution.py:22
  104.4 16.7 %collective-permute-start.25 = (bf16[48,2048]{1,0:T(8,128)(2,1)S(1)}, bf16[48,2048]{1,0:T(8,128)(2,1)S(1)}, u32[]{:S(2)}, u32[]{:S(2)}) collective-permute-start(bf16[48,2048]{1,0:T(8,128)(2,1)S(1)} %get-tuple-element.72), channel_id=1, source_target_pairs={{0,8},{4,12},{8,0},{12,4},{16,24},{20,28},{24,16},{28,20},{1,9},{5... | collective-permute-start | bytes 589832 | tf_op jit(solution)/shard_map/ppermute | solution.py:22
  105.8 16.6 %collective-permute-start.26 = (bf16[48,2048]{1,0:T(8,128)(2,1)S(1)}, bf16[48,2048]{1,0:T(8,128)(2,1)S(1)}, u32[]{:S(2)}, u32[]{:S(2)}) collective-permute-start(bf16[48,2048]{1,0:T(8,128)(2,1)S(1)} %get-tuple-element.71), channel_id=1, source_target_pairs={{0,12},{4,8},{8,4},{12,0},{16,28},{20,24},{24,20},{28,16},{1,13},{... | collective-permute-start | bytes 589832 | tf_op jit(solution)/shard_map/ppermute | solution.py:22
  109.5 9.5 %collective-permute-start.38 = (bf16[24,2048]{1,0:T(8,128)(2,1)S(1)}, bf16[24,2048]{1,0:T(8,128)(2,1)S(1)}, u32[]{:S(2)}, u32[]{:S(2)}) collective-permute-start(bf16[24,2048]{1,0:T(8,128)(2,1)S(1)} %get-tuple-element.80), channel_id=1, source_target_pairs={{0,24},{4,28},{8,16},{12,20},{16,8},{20,12},{24,0},{28,4},{1,25},{... | collective-permute-start | bytes 294920 | tf_op jit(solution)/shard_map/ppermute | solution.py:22
  112.7 8.4 %collective-permute-start.39 = (bf16[24,2048]{1,0:T(8,128)(2,1)S(1)}, bf16[24,2048]{1,0:T(8,128)(2,1)S(1)}, u32[]{:S(2)}, u32[]{:S(2)}) collective-permute-start(bf16[24,2048]{1,0:T(8,128)(2,1)S(1)} %get-tuple-element.79), channel_id=1, source_target_pairs={{0,28},{4,24},{8,20},{12,16},{16,12},{20,8},{24,4},{28,0},{1,29},{... | collective-permute-start | bytes 294920 | tf_op jit(solution)/shard_map/ppermute | solution.py:22
  123.2 2.0 %collective-permute-start.40 = (bf16[128,2048]{1,0:T(8,128)(2,1)S(1)}, bf16[128,2048]{1,0:T(8,128)(2,1)S(1)}, u32[]{:S(2)}, u32[]{:S(2)}) collective-permute-start(bf16[128,2048]{1,0:T(8,128)(2,1)S(1)} %shard_map.145), channel_id=1, source_target_pairs={{0,1},{1,0},{2,3},{3,2},{4,5},{5,4},{6,7},{7,6},{8,9},{9,8},{10,11... | collective-permute-start | bytes 1572872 | tf_op jit(solution)/shard_map/ppermute | solution.py:22
  125.3 8.4 %collective-permute-start.41 = (bf16[64,2048]{1,0:T(8,128)(2,1)S(1)}, bf16[64,2048]{1,0:T(8,128)(2,1)S(1)}, u32[]{:S(2)}, u32[]{:S(2)}) collective-permute-start(bf16[64,2048]{1,0:T(8,128)(2,1)S(1)} %slice.119), channel_id=1, source_target_pairs={{0,2},{1,3},{2,0},{3,1},{4,6},{5,7},{6,4},{7,5},{8,10},{9,11},{10,... | collective-permute-start | bytes 786440 | tf_op jit(solution)/shard_map/ppermute | solution.py:22

commit v3 on v2

--- a/solution.py
+++ b/solution.py
@@ -31,15 +31,24 @@
     return pieces
 
 
+def spread(piece):
+    mask = lax.axis_size("expert") // 2
+    pieces = [piece]
+    while mask > 1:
+        pieces = pieces + [swap(p, "expert", mask) for p in pieces]
+        mask //= 2
+    return pieces
+
+
 def add(rows, other):
     return (rows.astype(F32) + other.astype(F32)).astype(BF)
 
 
-def scatter_sum(keep, give, axis, last=None):
-    rows, mask = add(keep, swap(give, axis, 1)), 2
-    while mask < (last or lax.axis_size(axis)):
+def sum_rest(rows):
+    mask = 2
+    while mask < lax.axis_size("expert"):
         half = rows.shape[0] // 2
-        rows = add(rows[:half], swap(rows[half:], axis, mask))
+        rows = add(rows[:half], swap(rows[half:], "expert", mask))
         mask *= 2
     return rows
 
@@ -62,9 +71,33 @@
         in_specs=[pl.BlockSpec(memory_space=pltpu.VMEM)] * len(args),
         out_specs=[pl.BlockSpec(memory_space=pltpu.VMEM)] * len(outs),
         scratch_shapes=list(scratch),
-        compiler_params=pltpu.CompilerParams(vmem_limit_bytes=48 * 2**20),
+        compiler_params=pltpu.CompilerParams(vmem_limit_bytes=12 * 2**20),
         cost_estimate=pl.CostEstimate(flops=2 * macs, bytes_accessed=moved, transcendentals=0),
     )(*args)
+
+
+def fetch(*arrays):
+    def body(*refs):
+        n = len(arrays)
+        sems = refs[-1]
+        copies = [pltpu.make_async_copy(refs[i], refs[n + i], sems.at[i]) for i in range(n)]
+        for copy in copies:
+            copy.start()
+        for copy in copies:
+            copy.wait()
+
+    return pl.pallas_call(
+        body,
+        out_shape=[jax.ShapeDtypeStruct(x.shape, x.dtype) for x in arrays],
+        in_specs=[pl.BlockSpec(memory_space=pltpu.HBM)] * len(arrays),
+        out_specs=[pl.BlockSpec(memory_space=pltpu.VMEM)] * len(arrays),
+        scratch_shapes=[pltpu.SemaphoreType.DMA((len(arrays),))],
+        compiler_params=pltpu.CompilerParams(vmem_limit_bytes=2**20),
+    )(*arrays)
+
+
+def fence(*values):
+    return lax.optimization_barrier(values)
 
 
 def put_together(refs, whole):
@@ -102,6 +135,11 @@
         n = len(pieces)
         gate_ref, up_ref, down_ref, keep, give, whole = refs[n:]
         put_together(refs[:n], whole)
+        if count <= 256:
+            part = dot(gated(whole[...], gate_ref[...], up_ref[...]), down_ref[...])
+            keep[...] = part[: count // 2].astype(BF)
+            give[...] = part[count // 2 :].astype(BF)
+            return
         for rows, result in ((slice(count // 2, count), give), (slice(0, count // 2), keep)):
             hidden = gated(whole[rows], gate_ref[...], up_ref[...])
             result[...] = dot(hidden, down_ref[...]).astype(BF)
@@ -164,58 +202,82 @@
 
 def place_rows(mine, other, place, offsets, n_data):
     count, width = mine.shape
-    peer = count // n_data
+    blocks, size = place.shape[:2]
+    peer = size // n_data
     wide = width + offsets.shape[1]
-    if count % 16:
-        rows = jnp.concatenate([add(mine, other), offsets], axis=1)
-        return dot(place, rows).astype(BF).reshape(n_data, peer, wide)
+    if size % 16:
+        rows = jnp.concatenate([add(mine, other), offsets], axis=1).reshape(blocks, size, wide)
+        moved = jnp.einsum("bsr,brw->bsw", place, rows, preferred_element_type=F32).astype(BF)
+        return moved.reshape(blocks, n_data, peer, wide).swapaxes(0, 1).reshape(n_data, -1, wide)
 
     def body(mine_ref, other_ref, place_ref, offsets_ref, result):
-        rows = add(mine_ref[...], other_ref[...])
-        moved = dot(place_ref[...], rows).astype(BF)
-        beside = dot(place_ref[...], offsets_ref[...]).astype(BF)
+        moved, beside = [], []
+        for b in range(blocks):
+            span = slice(b * size, (b + 1) * size)
+            moved.append(dot(place_ref[b], add(mine_ref[span], other_ref[span])))
+            beside.append(dot(place_ref[b], offsets_ref[span]))
         for d in range(n_data):
-            result[d, :, :width] = moved[d * peer : (d + 1) * peer]
-            result[d, :, width:] = beside[d * peer : (d + 1) * peer]
-
-    return local_kernel(
-        body,
-        [jax.ShapeDtypeStruct((n_data, peer, wide), BF)],
+            part = slice(d * peer, (d + 1) * peer)
+            result[d, :, :width] = jnp.concatenate([m[part] for m in moved], axis=0).astype(BF)
+            result[d, :, width:] = jnp.concatenate([m[part] for m in beside], axis=0).astype(BF)
+
+    return local_kernel(
+        body,
+        [jax.ShapeDtypeStruct((n_data, blocks * peer, wide), BF)],
         [mine, other, place, offsets],
         (),
-        count * count * wide,
+        count * size * wide,
     )[0]
 
 
-def embed_rows(arrived, text, gain):
-    n_data, peer, wide = arrived.shape
-    count, width = text.shape
-
-    def math(rows, offsets, text_rows, gain_row):
-        spots = lax.broadcasted_iota(jnp.int32, (1, count), 1).astype(F32) == offsets
+def embed_rows(pieces, texts, gain, peer):
+    n_data, stack, wide = pieces[0].shape
+    count, width = texts[0].shape
+    blocks = len(texts)
+    total_rows, total = n_data * stack, blocks * count
+
+    def in_order(piece, p):
+        order = [p ^ b for b in range(blocks)]
+        return piece if p == 0 else jnp.concatenate([piece[o * peer : (o + 1) * peer] for o in order], axis=0)
+
+    def math(parts, text, gain_row):
+        rows = parts[0][:, :width]
+        for part in parts[1:]:
+            rows = rows + part[:, :width]
+        line = lax.broadcasted_iota(jnp.int32, (total_rows, 1), 0)
+        target = parts[0][:, width : width + 1] + (line // peer % blocks * count).astype(F32)
+        spots = lax.broadcasted_iota(jnp.int32, (1, total), 1).astype(F32) == target
         spots = spots.astype(F32)
         turned = (((0,), (0,)), ((), ()))
-        placed = lax.dot_general(spots.astype(BF), rows, turned, preferred_element_type=F32)
-        named = lax.dot_general(spots, jnp.ones_like(offsets), turned, preferred_element_type=F32)
-        embed = jnp.where(named > 0.5, placed, text_rows.astype(F32))
+        placed = lax.dot_general(spots.astype(BF), rows.astype(BF), turned, preferred_element_type=F32)
+        named = lax.dot_general(spots, jnp.ones_like(target), turned, preferred_element_type=F32)
+        embed = jnp.where(named > 0.5, placed, text.astype(F32))
         meansq = jnp.mean(embed * embed, axis=-1, keepdims=True) + 1e-06
-        return embed, (embed * lax.rsqrt(meansq) * gain_row).astype(BF)
+        return embed[:count], (embed * lax.rsqrt(meansq) * gain_row).astype(BF)
 
     gain = gain.reshape(1, width)
-    if n_data * peer % 16 or peer % 4:
-        rows = arrived.reshape(n_data * peer, wide)
-        return math(rows[:, :width], rows[:, width : width + 1].astype(F32), text, gain)
-
-    def body(arrived_ref, text_ref, gain_ref, embed_ref, normed_ref):
-        rows = jnp.concatenate([arrived_ref[d].astype(F32) for d in range(n_data)], axis=0)
-        embed, normed = math(
-            rows[:, :width].astype(BF), rows[:, width : width + 1], text_ref[...], gain_ref[...]
-        )
-        embed_ref[...] = embed
-        normed_ref[...] = normed
-
-    return local_kernel(
-        body, [out(count, width, F32), out(count, width)], [arrived, text, gain], (), count * n_data * peer * width
+    if stack % 8:
+        parts = [
+            jnp.concatenate([in_order(piece[d], p) for d in range(n_data)], axis=0).astype(F32)
+            for p, piece in enumerate(pieces)
+        ]
+        return math(parts, jnp.concatenate(texts, axis=0), gain)
+
+    def body(*refs):
+        gain_ref, embed_ref, normed_ref = refs[2 * blocks :]
+        parts = [
+            jnp.concatenate([in_order(ref[d].astype(F32), p) for d in range(n_data)], axis=0)
+            for p, ref in enumerate(refs[:blocks])
+        ]
+        text = jnp.concatenate([ref[...].astype(F32) for ref in refs[blocks : 2 * blocks]], axis=0)
+        embed_ref[...], normed_ref[...] = math(parts, text, gain_ref[...])
+
+    return local_kernel(
+        body,
+        [out(count, width, F32), out(total, width)],
+        [*pieces, *texts, gain],
+        (),
+        total * total_rows * width,
     )
 
 
@@ -242,7 +304,7 @@
     )
 
 
-def combine_rows(total, coef, backs, starts):
+def combine_rows(total, coef, backs, starts, dtype):
     count, width = total.shape
     slots = coef.shape[2]
     ends = list(starts[1:]) + [slots]
@@ -251,7 +313,7 @@
             [jnp.pad(b, ((0, e - s - b.shape[0]), (0, 0))) for b, s, e in zip(backs, starts, ends)],
             axis=0,
         )
-        return (total + dot(coef[0], whole) + dot(coef[1], whole)).astype(BF)
+        return (total + dot(coef[0], whole) + dot(coef[1], whole)).astype(dtype)
 
     def body(*refs):
         total_ref, coef_ref, result, whole = refs[0], refs[1], refs[-2], refs[-1]
@@ -262,11 +324,11 @@
             whole[at : at + size] = ref[...]
         rows = whole[...]
         value = total_ref[...] + dot(coef_ref[0], rows)
-        result[...] = (value + dot(coef_ref[1], rows)).astype(BF)
-
-    return local_kernel(
-        body,
-        [out(count, width)],
+        result[...] = (value + dot(coef_ref[1], rows)).astype(dtype)
+
+    return local_kernel(
+        body,
+        [out(count, width, dtype)],
         [total, coef, *backs],
         [pltpu.VMEM((slots, width), BF)],
         2 * count * width * slots,
@@ -304,26 +366,32 @@
     capacity = 3 * group_rows * top // (2 * n_data)
     share = capacity // n_group
 
-    keep, give = image_rows(gather(image_feats, "expert"), proj_in, proj_out)
-    rows, mask = add(keep, swap(give, "expert", 1)), 2
-    while 2 * mask < n_group:
-        half = rows.shape[0] // 2
-        rows = add(rows[:half], swap(rows[half:], "expert", mask))
-        mask *= 2
-    other = swap(rows[img_dev:], "expert", mask)
-
-    owner = tile_pos // tok_dev // n_group
+    weights_in, weights_out, own_feats = fetch(proj_in, proj_out, image_feats)
+    routes = spread(jnp.concatenate([route_ids, route_wts], axis=1))
+    spots, feats = spread(tile_pos), spread(image_feats)
+    partner = [swap(image_feats, "expert", 1)]
+    feats, partner, spots, routes, own_feats = fence(feats, partner, spots, routes, own_feats)
+    feats = feats + partner + [swap(p, "expert", 1) for p in feats[1:]]
+    keep, give = image_rows([own_feats, *feats[1:]], weights_in, weights_out)
+
+    spots, keep, give = fence(spots, keep, give)
+    spots = jnp.stack(spots)
+    owner = spots // tok_dev // n_group
     earlier = jnp.arange(img_dev)[None, :] < jnp.arange(img_dev)[:, None]
-    rank_img = jnp.sum(((owner[:, None] == owner[None, :]) & earlier).astype(jnp.int32), axis=1)
-    place = one_hot(owner * peer + rank_img, img_dev).astype(BF)
-    offsets = jnp.broadcast_to((tile_pos % tok_dev).astype(BF)[:, None], (img_dev, 128))
-    leaving = place_rows(rows[:img_dev], other, place, offsets, n_data)
+    rank_img = jnp.sum(((owner[:, :, None] == owner[:, None, :]) & earlier).astype(jnp.int32), axis=2)
+    seat = owner * peer + rank_img
+    place = (seat[:, None, :] == jnp.arange(img_dev, dtype=jnp.int32)[None, :, None]).astype(BF)
+    offsets = jnp.broadcast_to((spots % tok_dev).astype(BF).reshape(-1, 1), (spots.size, 128))
+    leaving = place_rows(keep, swap(give, "expert", 1), place, offsets, n_data)
+    texts, routes, leaving = fence(text_embed, routes, leaving)
+    texts = spread(texts)
+    routes = routes + [swap(p, "expert", 1) for p in routes]
     arrived = lax.all_to_all(leaving, "dp", split_axis=0, concat_axis=0, tiled=True)
-    embed_f, normed = embed_rows(arrived, text_embed, norm_gain)
-    normed = gather(normed, "expert")
-
-    routes = jnp.concatenate([route_ids, route_wts], axis=1)
-    routes = jnp.concatenate(gather(routes, "expert"), axis=0)
+    texts, routes, arrived = fence(texts, routes, arrived)
+    embed_f, normed = embed_rows(spread(arrived), texts, norm_gain, peer)
+    normed = [normed, swap(normed, "expert", 1)]
+
+    routes = jnp.concatenate(routes, axis=0)
     ids, weights = routes[:, :top], routes[:, top:].astype(F32)
     weights = weights / jnp.sum(weights, axis=1, keepdims=True)
     rows_at = jnp.arange(group_rows, dtype=jnp.int32)
@@ -366,6 +434,9 @@
         got[m] = swap(late, "dp", m)
 
     shared = shared_rows(normed, shared_gate.T, shared_up.T, shared_down)
+    def total_of(keep, give):
+        return sum_rest(add(keep, swap(give, "expert", 1)))
+
     experts = (expert_gate[0].T, expert_up[0].T, expert_down[0])
 
     def join(stage):
@@ -385,15 +456,17 @@
             part = rows[i * size : (i + 1) * size]
             back[m] = swap(part, "dp", m) if m else part
 
-    send_back(near, scatter_sum(keep, give, "expert", last=2))
-    send_back(far_one, scatter_sum(*expert_rows(far_pieces, *experts), "expert"))
+    send_back(near, add(keep, swap(give, "expert", 1)))
+    send_back(far_one, total_of(*expert_rows(far_pieces, *experts)))
     pieces = gather(join(far_two), "expert")
-    send_back(far_two, scatter_sum(*expert_rows(pieces, *experts), "expert"))
+    send_back(far_two, total_of(*expert_rows(pieces, *experts)))
 
     middle = group_rows // 2
-    give = combine_rows(shared[1], coef[:, middle:], back, starts)
-    keep = combine_rows(shared[0], coef[:, :middle], back, starts)
-    total = scatter_sum(keep, give, "expert")
+    keep, give = [
+        combine_rows(part, coef[:, rows], back, starts, BF)
+        for part, rows in zip(shared, (slice(0, middle), slice(middle, None)))
+    ]
+    total = sum_rest(add(keep, swap(give, "expert", 1)))
     return (embed_f + total.astype(F32)).astype(BF)
 
 

time: 135 us -> 125 us (0.926)
  waiting for transfers between devices: 66.8 us -> 52.9 us
  local copies, waits for them, and re-layouts: 2.86 us -> 9.82 us
  Pallas kernels: 22 us -> 15.1 us
  starting transfers between devices: 38.6 us -> 43 us
    ppermute x42, waiting for transfers between devices: 59.6 us -> 51.7 us  [swap(): return lax.ppermute(rows, axis, [(i, i ^ mask) for i in range(count)])]
    pallas_call x10, Pallas kernels: 22 us -> 14.6 us  [local_kernel(): pl.pallas_call(body, out_shape=list(outs), in_specs=[pl.BlockSpec(memory_...]
    unnamed x21 -> x25, local copies, waits for them, and re-layouts: 2.6 us -> 9.5 us
    all_to_all x1, waiting for transfers between devices: 7.16 us -> 1.24 us  [shards(): lax.all_to_all(leaving, 'dp', split_axis=0, concat_axis=0, tiled=True)]
    ppermute x42, starting transfers between devices: 32.8 us -> 37.2 us  [swap(): return lax.ppermute(rows, axis, [(i, i ^ mask) for i in range(count)])]
  transfers between devices with their start and end apart: 43 -> 43, of which waited for: 21 -> 19; matrix products, arithmetic and copies ran while one was open for 2% -> 2% of each run, Pallas kernels for 14% -> 8%
where the time goes in v3:
time: 125 us; the launch traced here: 124 us
  waiting for transfers between devices  52.9 us (42%)
  starting transfers between devices  43 us (34%)
  Pallas kernels  15.1 us (12%)
  local copies, waits for them, and re-layouts  9.82 us (8%)
  other arithmetic  2.95 us (2%)
    ppermute x42, waiting for transfers between devices, swap(): return lax.ppermute(rows, axis, [(i, i ^ mask) for i in range(count)])  51.7 us
    ppermute x42, starting transfers between devices, swap(): return lax.ppermute(rows, axis, [(i, i ^ mask) for i in range(count)])  37.2 us
    pallas_call x10, Pallas kernels, local_kernel(): pl.pallas_call(body, out_shape=list(outs), in_specs=[pl.BlockSpec(memory_...  14.6 us
    unnamed x25, local copies, waits for them, and re-layouts  9.5 us
    all_to_all x1, starting transfers between devices, shards(): lax.all_to_all(leaving, 'dp', split_axis=0, concat_axis=0, tiled=True)  5.81 us
  transfers between devices with their start and end apart: 43, of which 19 were waited for; matrix products, arithmetic and copies ran while one was open for 2% of the time, Pallas kernels for 8%

profile of v3, /device:TPU:0, one launch (start us, length us, event | category | flops | bytes accessed | tf_op | source)
XLA Modules:
  0.0 124.5 jit_solution(13132195602504191538)
XLA Ops:
  0.0 3.0 %collective-permute-start = (bf16[32,4608]{1,0:T(8,128)(2,1)}, bf16[32,4608]{1,0:T(8,128)(2,1)S(1)}, u32[]{:S(2)}, u32[]{:S(2)}) collective-permute-start(bf16[32,4608]{1,0:T(8,128)(2,1)} %refs_2_.1), channel_id=1, source_target_pairs={{0,2},{1,3},{2,0},{3,1},{4,6},{5,7},{6,4},{7,5},{8,10},{9,11},{10,... | collective-permute-start | bytes 884744 | tf_op jit(solution)/shard_map/ppermute | solution.py:22
  3.0 0.7 pad_add_fusion.1
  3.7 2.0 %collective-permute-start.2 = (s32[32]{0:T(128)}, s32[32]{0:T(128)S(1)}, u32[]{:S(2)}, u32[]{:S(2)}) collective-permute-start(s32[32]{0:T(128)} %param.16), channel_id=1, source_target_pairs={{0,2},{1,3},{2,0},{3,1},{4,6},{5,7},{6,4},{7,5},{8,10},{9,11},{10,... | collective-permute-start | bytes 392 | tf_op jit(solution)/shard_map/ppermute | solution.py:22
  5.7 2.3 %copy-done.3 = bf16[4608,512]{1,0:T(8,128)(2,1)S(1)} copy-done((bf16[4608,512]{1,0:T(8,128)(2,1)S(1)}, bf16[4608,512]{1,0:T(8,128)(2,1)}, u32[]{:S(2)}) %copy-start.3) | copy-done | bytes 4718616
  8.0 1.6 %copy-done.7 = bf16[512,2048]{1,0:T(8,128)(2,1)S(1)} copy-done((bf16[512,2048]{1,0:T(8,128)(2,1)S(1)}, bf16[512,2048]{1,0:T(8,128)(2,1)}, u32[]{:S(2)}) %copy-start.7) | copy-done | bytes 2097176
  9.6 1.0 copy-done.8
  10.6 0.5 shard_map.136
  11.3 1.6 %collective-permute-done.4.refs_3_ = bf16[32,4608]{1,0:T(8,128)(2,1)S(1)} collective-permute-done((bf16[32,4608]{1,0:T(8,128)(2,1)S(1)}, bf16[32,4608]{1,0:T(8,128)(2,1)S(1)}, u32[]{:S(2)}, u32[]{:S(2)}) %collective-permute-start.4) | collective-permute-done | bytes 294944 | tf_op jit(solution)/shard_map/ppermute | solution.py:22
  12.8 1.9 %shard_map.137 = (bf16[64,2048]{1,0:T(8,128)(2,1)S(1)}, bf16[64,2048]{1,0:T(8,128)(2,1)}) custom-call(bf16[32,4608]{1,0:T(8,128)(2,1)S(1)} %get-tuple-element.68.refs_0_, bf16[32,4608]{1,0:T(8,128)(2,1)S(1)} %collective-permute-done.refs_1_, bf16[32,4608]{1,0:T(8,128)(2,1)S(1)} %collective-permute-done.1.refs_2_, ...), custom_call_target="tpu_custom_call" | custom-call | flops 872415232 | bytes 8519680 | tf_op jit(solution)/shard_map/pallas_call | solution.py:68
  15.2 1.3 %collective-permute-done.5.other_ref = bf16[64,2048]{1,0:T(8,128)(2,1)S(1)} collective-permute-done((bf16[64,2048]{1,0:T(8,128)(2,1)}, bf16[64,2048]{1,0:T(8,128)(2,1)S(1)}, u32[]{:S(2)}, u32[]{:S(2)}) %collective-permute-start.5) | collective-permute-done | bytes 262176 | tf_op jit(solution)/shard_map/ppermute | solution.py:22
  16.6 0.9 shard_map.138
  17.5 5.8 %all-to-all-start = ((bf16[8,8,2176]{2,1,0:T(8,128)(2,1)}), bf16[8,8,2176]{2,1,0:T(8,128)(2,1)S(1)}, u32[]{:S(2)}, u32[]{:S(2)}) async-start(bf16[8,8,2176]{2,1,0:T(8,128)(2,1)} %shard_map.138), calls=%async_computation | async-start | bytes 557056 | tf_op jit(solution)/shard_map/all_to_all | solution.py:389
  23.3 0.9 collective-permute-start.6
  24.2 0.5 collective-permute-start.8
  24.7 0.6 collective-permute-done.7
  25.5 6.1 %collective-permute-done.6.refs_3_ = bf16[64,2048]{1,0:T(8,128)(2,1)S(1)} collective-permute-done((bf16[64,2048]{1,0:T(8,128)(2,1)}, bf16[64,2048]{1,0:T(8,128)(2,1)S(1)}, u32[]{:S(2)}, u32[]{:S(2)}) %collective-permute-start.6) | collective-permute-done | bytes 262176 | tf_op jit(solution)/shard_map/ppermute | solution.py:22
  31.6 1.2 all-to-all-done.refs_0_
  32.8 0.9 collective-permute-start.9
  34.1 5.5 %collective-permute-done.9.refs_1_ = bf16[8,8,2176]{2,1,0:T(8,128)(2,1)S(1)} collective-permute-done((bf16[8,8,2176]{2,1,0:T(8,128)(2,1)S(1)}, bf16[8,8,2176]{2,1,0:T(8,128)(2,1)S(1)}, u32[]{:S(2)}, u32[]{:S(2)}) %collective-permute-start.9) | collective-permute-done | bytes 278560 | tf_op jit(solution)/shard_map/ppermute | solution.py:22
  39.7 0.9 copy-done.9
  40.6 0.7 shard_map.139
  41.5 1.8 %collective-permute-done.10.refs_2_.refs_1_ = bf16[128,2048]{1,0:T(8,128)(2,1)S(1)} collective-permute-done((bf16[128,2048]{1,0:T(8,128)(2,1)S(1)}, bf16[128,2048]{1,0:T(8,128)(2,1)S(1)}, u32[]{:S(2)}, u32[]{:S(2)}) %collective-permute-start.10) | collective-permute-done | bytes 524320 | tf_op jit(solution)/shard_map/ppermute | solution.py:22
  43.3 0.5 shard_map.140
  43.8 2.8 %collective-permute-start.12 = (bf16[24,2048]{1,0:T(8,128)(2,1)S(1)}, bf16[24,2048]{1,0:T(8,128)(2,1)S(1)}, u32[]{:S(2)}, u32[]{:S(2)}) collective-permute-start(bf16[24,2048]{1,0:T(8,128)(2,1)S(1)} %get-tuple-element.93), channel_id=1, source_target_pairs={{0,20},{4,16},{8,28},{12,24},{16,4},{20,0},{24,12},{28,8},{1,21},{... | collective-permute-start | bytes 294920 | tf_op jit(solution)/shard_map/ppermute | solution.py:22
  46.6 0.9 collective-permute-start.11
  47.5 0.8 collective-permute-start.16
  48.3 0.9 collective-permute-start.17
  49.2 1.8 %collective-permute-start.18 = (bf16[48,2048]{1,0:T(8,128)(2,1)S(1)}, bf16[48,2048]{1,0:T(8,128)(2,1)S(1)}, u32[]{:S(2)}, u32[]{:S(2)}) collective-permute-start(bf16[48,2048]{1,0:T(8,128)(2,1)S(1)} %get-tuple-element.105), channel_id=1, source_target_pairs={{0,12},{4,8},{8,4},{12,0},{16,28},{20,24},{24,20},{28,16},{1,13},{... | collective-permute-start | bytes 589832 | tf_op jit(solution)/shard_map/ppermute | solution.py:22
  50.9 1.8 %copy-done.5 = bf16[2048,704]{0,1:T(8,128)(2,1)S(1)} copy-done((bf16[2048,704]{0,1:T(8,128)(2,1)S(1)}, bf16[2048,704]{0,1:T(8,128)(2,1)}, u32[]{:S(2)}) %copy-start.5) | copy-done | bytes 2883608
  52.8 1.8 %copy-done.6 = bf16[704,2048]{1,0:T(8,128)(2,1)S(1)} copy-done((bf16[704,2048]{1,0:T(8,128)(2,1)S(1)}, bf16[704,2048]{1,0:T(8,128)(2,1)}, u32[]{:S(2)}) %copy-start.6) | copy-done | bytes 2883608
  54.6 2.6 %shard_map.141 = (f32[128,2048]{1,0:T(8,128)S(1)}, f32[128,2048]{1,0:T(8,128)S(1)}) custom-call(bf16[128,2048]{1,0:T(8,128)(2,1)S(1)} %get-tuple-element.91.refs_1_.refs_0_, bf16[128,2048]{1,0:T(8,128)(2,1)S(1)} %collective-permute-done.10.refs_2_.refs_1_, bf16[704,2048]{1,0:T(8,128)(2,1)S(1)} %bitcast.26, bf16[704,2048]{1,0:T(8,128)(2,1)S(1)} %bitcast.27, ...), custom_call_target="tpu_custom_call" | custom-call | flops 2214592512 | bytes 11796480 | tf_op jit(solution)/shard_map/pallas_call | solution.py:68
  57.3 0.9 collective-permute-start.13
  58.3 3.0 %collective-permute-start.31 = (bf16[24,2048]{1,0:T(8,128)(2,1)S(1)}, bf16[24,2048]{1,0:T(8,128)(2,1)S(1)}, u32[]{:S(2)}, u32[]{:S(2)}) collective-permute-start(bf16[24,2048]{1,0:T(8,128)(2,1)S(1)} %get-tuple-element.116), channel_id=1, source_target_pairs={{0,24},{4,28},{8,16},{12,20},{16,8},{20,12},{24,0},{28,4},{1,25},{... | collective-permute-start | bytes 294920 | tf_op jit(solution)/shard_map/ppermute | solution.py:22
  61.4 1.6 %collective-permute-done.18.refs_3_ = bf16[48,2048]{1,0:T(8,128)(2,1)S(1)} collective-permute-done((bf16[48,2048]{1,0:T(8,128)(2,1)S(1)}, bf16[48,2048]{1,0:T(8,128)(2,1)S(1)}, u32[]{:S(2)}, u32[]{:S(2)}) %collective-permute-start.18) | collective-permute-done | bytes 196640 | tf_op jit(solution)/shard_map/ppermute | solution.py:22
  63.0 0.5 collective-permute-start.21
  63.5 1.2 collective-permute-done.13.refs_1_
  64.7 0.4 collective-permute-done.31
  65.2 3.0 %collective-permute-start.32 = (bf16[24,2048]{1,0:T(8,128)(2,1)S(1)}, bf16[24,2048]{1,0:T(8,128)(2,1)S(1)}, u32[]{:S(2)}, u32[]{:S(2)}) collective-permute-start(bf16[24,2048]{1,0:T(8,128)(2,1)S(1)} %get-tuple-element.117), channel_id=1, source_target_pairs={{0,28},{4,24},{8,20},{12,16},{16,12},{20,8},{24,4},{28,0},{1,29},{... | collective-permute-start | bytes 294920 | tf_op jit(solution)/shard_map/ppermute | solution.py:22
  68.3 3.2 %shard_map.142 = (bf16[192,2048]{1,0:T(8,128)(2,1)S(1)}, bf16[192,2048]{1,0:T(8,128)(2,1)S(1)}) custom-call(bf16[48,2048]{1,0:T(8,128)(2,1)S(1)} %get-tuple-element.98.refs_0_, bf16[48,2048]{1,0:T(8,128)(2,1)S(1)} %collective-permute-done.16.refs_1_, bf16[48,2048]{1,0:T(8,128)(2,1)S(1)} %collective-permute-done.17.refs_2_, ...), custom_call_target="tpu_custom_call" | custom-call | flops 1660944384 | bytes 7471104 | tf_op jit(solution)/shard_map/pallas_call | solution.py:68
  71.5 1.6 %shard_map.143 = (bf16[96,2048]{1,0:T(8,128)(2,1)S(1)}, bf16[96,2048]{1,0:T(8,128)(2,1)S(1)}) custom-call(bf16[48,2048]{1,0:T(8,128)(2,1)S(1)} %pad_maximum_fusion.1.refs_0_, bf16[48,2048]{1,0:T(8,128)(2,1)S(1)} %collective-permute-done.13.refs_1_, bf16[48,2048]{1,0:T(8,128)(2,1)S(1)} %collective-permute-done.14.refs_2_, ...), custom_call_target="tpu_custom_call" | custom-call | flops 830472192 | bytes 5898240 | tf_op jit(solution)/shard_map/pallas_call | solution.py:68
  73.4 1.2 collective-permute-start.33
  74.6 6.0 %collective-permute-done.33.refs_1_ = bf16[48,2048]{1,0:T(8,128)(2,1)S(1)} collective-permute-done((bf16[48,2048]{1,0:T(8,128)(2,1)S(1)}, bf16[48,2048]{1,0:T(8,128)(2,1)S(1)}, u32[]{:S(2)}, u32[]{:S(2)}) %collective-permute-start.33) | collective-permute-done | bytes 196640 | tf_op jit(solution)/shard_map/ppermute | solution.py:22
  80.8 1.1 collective-permute-start.28
  82.1 0.3 collective-permute-start.23
  82.4 1.6 %shard_map.144 = (bf16[96,2048]{1,0:T(8,128)(2,1)S(1)}, bf16[96,2048]{1,0:T(8,128)(2,1)S(1)}) custom-call(bf16[48,2048]{1,0:T(8,128)(2,1)S(1)} %constant_dynamic-update-slice_fusion.refs_0_, bf16[48,2048]{1,0:T(8,128)(2,1)S(1)} %collective-permute-done.33.refs_1_, bf16[48,2048]{1,0:T(8,128)(2,1)S(1)} %collective-permute-done.34.refs_2_, ...), custom_call_target="tpu_custom_call" | custom-call | flops 830472192 | bytes 5898240 | tf_op jit(solution)/shard_map/pallas_call | solution.py:68
  84.0 0.3 collective-permute-start.36
  84.4 3.8 %collective-permute-done.28 = bf16[48,2048]{1,0:T(8,128)(2,1)S(1)} collective-permute-done((bf16[48,2048]{1,0:T(8,128)(2,1)S(1)}, bf16[48,2048]{1,0:T(8,128)(2,1)S(1)}, u32[]{:S(2)}, u32[]{:S(2)}) %collective-permute-start.28) | collective-permute-done | bytes 196640 | tf_op jit(solution)/shard_map/ppermute | solution.py:22
  88.2 1.1 collective-permute-start.29
  89.3 4.2 %collective-permute-start.30 = (bf16[24,2048]{1,0:T(8,128)(2,1)S(1)}, bf16[24,2048]{1,0:T(8,128)(2,1)S(1)}, u32[]{:S(2)}, u32[]{:S(2)}) collective-permute-start(bf16[24,2048]{1,0:T(8,128)(2,1)S(1)} %get-tuple-element.129), channel_id=1, source_target_pairs={{0,20},{4,16},{8,28},{12,24},{16,4},{20,0},{24,12},{28,8},{1,21},{... | collective-permute-start | bytes 294920 | tf_op jit(solution)/shard_map/ppermute | solution.py:22
  93.6 0.4 collective-permute-start.37
  94.0 0.3 add_convert_fusion
  94.4 0.8 collective-permute-start.25
  95.2 4.5 %collective-permute-done.37 = bf16[48,2048]{1,0:T(8,128)(2,1)S(1)} collective-permute-done((bf16[48,2048]{1,0:T(8,128)(2,1)S(1)}, bf16[48,2048]{1,0:T(8,128)(2,1)S(1)}, u32[]{:S(2)}, u32[]{:S(2)}) %collective-permute-start.37) | collective-permute-done | bytes 196640 | tf_op jit(solution)/shard_map/ppermute | solution.py:22
  99.8 1.8 %collective-permute-start.38 = (bf16[24,2048]{1,0:T(8,128)(2,1)S(1)}, bf16[24,2048]{1,0:T(8,128)(2,1)S(1)}, u32[]{:S(2)}, u32[]{:S(2)}) collective-permute-start(bf16[24,2048]{1,0:T(8,128)(2,1)S(1)} %get-tuple-element.128), channel_id=1, source_target_pairs={{0,24},{4,28},{8,16},{12,20},{16,8},{20,12},{24,0},{28,4},{1,25},{... | collective-permute-start | bytes 294920 | tf_op jit(solution)/shard_map/ppermute | solution.py:22
  101.6 1.6 %collective-permute-start.39 = (bf16[24,2048]{1,0:T(8,128)(2,1)S(1)}, bf16[24,2048]{1,0:T(8,128)(2,1)S(1)}, u32[]{:S(2)}, u32[]{:S(2)}) collective-permute-start(bf16[24,2048]{1,0:T(8,128)(2,1)S(1)} %get-tuple-element.127), channel_id=1, source_target_pairs={{0,28},{4,24},{8,20},{12,16},{16,12},{20,8},{24,4},{28,0},{1,29},{... | collective-permute-start | bytes 294920 | tf_op jit(solution)/shard_map/ppermute | solution.py:22
  103.2 5.5 %collective-permute-done.38.refs_8_ = bf16[24,2048]{1,0:T(8,128)(2,1)S(1)} collective-permute-done((bf16[24,2048]{1,0:T(8,128)(2,1)S(1)}, bf16[24,2048]{1,0:T(8,128)(2,1)S(1)}, u32[]{:S(2)}, u32[]{:S(2)}) %collective-permute-start.38) | collective-permute-done | bytes 98336 | tf_op jit(solution)/shard_map/ppermute | solution.py:22
  108.7 1.4 %collective-permute-done.39.refs_9_ = bf16[24,2048]{1,0:T(8,128)(2,1)S(1)} collective-permute-done((bf16[24,2048]{1,0:T(8,128)(2,1)S(1)}, bf16[24,2048]{1,0:T(8,128)(2,1)S(1)}, u32[]{:S(2)}, u32[]{:S(2)}) %collective-permute-start.39) | collective-permute-done | bytes 98336 | tf_op jit(solution)/shard_map/ppermute | solution.py:22
  110.1 2.3 %collective-permute-done.26.refs_5_ = bf16[48,2048]{1,0:T(8,128)(2,1)S(1)} collective-permute-done((bf16[48,2048]{1,0:T(8,128)(2,1)S(1)}, bf16[48,2048]{1,0:T(8,128)(2,1)S(1)}, u32[]{:S(2)}, u32[]{:S(2)}) %collective-permute-start.26) | collective-permute-done | bytes 196640 | tf_op jit(solution)/shard_map/ppermute | solution.py:22
  112.4 0.7 shard_map.146
  113.2 0.7 shard_map.145
  113.9 1.2 collective-permute-done.40
  115.3 1.8 %collective-permute-start.41 = (bf16[64,2048]{1,0:T(8,128)(2,1)S(1)}, bf16[64,2048]{1,0:T(8,128)(2,1)S(1)}, u32[]{:S(2)}, u32[]{:S(2)}) collective-permute-start(bf16[64,2048]{1,0:T(8,128)(2,1)S(1)} %slice.109), channel_id=1, source_target_pairs={{0,2},{1,3},{2,0},{3,1},{4,6},{5,7},{6,4},{7,5},{8,10},{9,11},{10,... | collective-permute-start | bytes 786440 | tf_op jit(solution)/shard_map/ppermute | solution.py:22
  117.0 6.7 %collective-permute-done.41 = bf16[64,2048]{1,0:T(8,128)(2,1)S(1)} collective-permute-done((bf16[64,2048]{1,0:T(8,128)(2,1)S(1)}, bf16[64,2048]{1,0:T(8,128)(2,1)S(1)}, u32[]{:S(2)}, u32[]{:S(2)}) %collective-permute-start.41) | collective-permute-done | bytes 262176 | tf_op jit(solution)/shard_map/ppermute | solution.py:22
  123.7 0.8 add_convert_fusion.4
  (96 shorter events, 2.9 us)
Async XLA Ops:
  0.0 11.2 %collective-permute-start = (bf16[32,4608]{1,0:T(8,128)(2,1)}, bf16[32,4608]{1,0:T(8,128)(2,1)S(1)}, u32[]{:S(2)}, u32[]{:S(2)}) collective-permute-start(bf16[32,4608]{1,0:T(8,128)(2,1)} %refs_2_.1), channel_id=1, source_target_pairs={{0,2},{1,3},{2,0},{3,1},{4,6},{5,7},{6,4},{7,5},{8,10},{9,11},{10,... | collective-permute-start | bytes 884744 | tf_op jit(solution)/shard_map/ppermute | solution.py:22
  3.0 8.2 %collective-permute-start.1 = (bf16[32,4608]{1,0:T(8,128)(2,1)}, bf16[32,4608]{1,0:T(8,128)(2,1)S(1)}, u32[]{:S(2)}, u32[]{:S(2)}) collective-permute-start(bf16[32,4608]{1,0:T(8,128)(2,1)} %refs_2_.1), channel_id=1, source_target_pairs={{0,1},{1,0},{2,3},{3,2},{4,5},{5,4},{6,7},{7,6},{8,9},{9,8},{10,11... | collective-permute-start | bytes 884744 | tf_op jit(solution)/shard_map/ppermute | solution.py:22
  3.7 7.5 %collective-permute-start.3 = (s32[64,4]{0,1:T(4,128)S(1)}, s32[64,4]{0,1:T(4,128)S(1)}, u32[]{:S(2)}, u32[]{:S(2)}) collective-permute-start(s32[64,4]{0,1:T(4,128)S(1)} %pad_add_fusion.1), channel_id=1, source_target_pairs={{0,2},{1,3},{2,0},{3,1},{4,6},{5,7},{6,4},{7,5},{8,10},{9,11},{10,... | collective-permute-start | bytes 3080 | tf_op jit(solution)/shard_map/ppermute | solution.py:22
  3.7 7.5 %collective-permute-start.2 = (s32[32]{0:T(128)}, s32[32]{0:T(128)S(1)}, u32[]{:S(2)}, u32[]{:S(2)}) collective-permute-start(s32[32]{0:T(128)} %param.16), channel_id=1, source_target_pairs={{0,2},{1,3},{2,0},{3,1},{4,6},{5,7},{6,4},{7,5},{8,10},{9,11},{10,... | collective-permute-start | bytes 392 | tf_op jit(solution)/shard_map/ppermute | solution.py:22
  5.7 2.3 %copy-start.3 = (bf16[4608,512]{1,0:T(8,128)(2,1)S(1)}, bf16[4608,512]{1,0:T(8,128)(2,1)}, u32[]{:S(2)}) copy-start(bf16[4608,512]{1,0:T(8,128)(2,1)} %refs_0_.1) | copy-start | bytes 14155780
  8.0 1.6 %copy-start.7 = (bf16[512,2048]{1,0:T(8,128)(2,1)S(1)}, bf16[512,2048]{1,0:T(8,128)(2,1)}, u32[]{:S(2)}) copy-start(bf16[512,2048]{1,0:T(8,128)(2,1)} %refs_1_.1) | copy-start | bytes 6291460
  9.6 1.0 copy-start.8
  11.2 1.6 %collective-permute-start.4 = (bf16[32,4608]{1,0:T(8,128)(2,1)S(1)}, bf16[32,4608]{1,0:T(8,128)(2,1)S(1)}, u32[]{:S(2)}, u32[]{:S(2)}) collective-permute-start(bf16[32,4608]{1,0:T(8,128)(2,1)S(1)} %collective-permute-done.refs_1_), channel_id=1, source_target_pairs={{0,1},{1,0},{2,3},{3,2},{4,5},{5,4},{6,7},{7,6},{8,9},{9,8},{10,11... | collective-permute-start | bytes 884744 | tf_op jit(solution)/shard_map/ppermute | solution.py:22
  12.8 2.1 %copy-start.11 = (s32[32]{0:T(128)S(1)}, s32[32]{0:T(128)}, u32[]{:S(2)}) copy-start(s32[32]{0:T(128)} %param.16) | copy-start | bytes 388
  12.8 26.8 %copy-start.10 = (f32[2048]{0:T(1024)S(1)}, f32[2048]{0:T(1024)}, u32[]{:S(2)}) copy-start(f32[2048]{0:T(1024)} %param.19) | copy-start | bytes 24580
  14.8 36.2 %copy-start.4 = (bf16[2048,704]{0,1:T(8,128)(2,1)S(1)}, bf16[2048,704]{0,1:T(8,128)(2,1)}, u32[]{:S(2)}) copy-start(bf16[2048,704]{0,1:T(8,128)(2,1)} %param.20) | copy-start | bytes 8650756
  14.8 1.7 %collective-permute-start.5 = (bf16[64,2048]{1,0:T(8,128)(2,1)}, bf16[64,2048]{1,0:T(8,128)(2,1)S(1)}, u32[]{:S(2)}, u32[]{:S(2)}) collective-permute-start(bf16[64,2048]{1,0:T(8,128)(2,1)} %get-tuple-element.76), channel_id=1, source_target_pairs={{0,1},{1,0},{2,3},{3,2},{4,5},{5,4},{6,7},{7,6},{8,9},{9,8},{10,11... | collective-permute-start | bytes 786440 | tf_op jit(solution)/shard_map/ppermute | solution.py:22
  17.5 15.3 %all-to-all-start = ((bf16[8,8,2176]{2,1,0:T(8,128)(2,1)}), bf16[8,8,2176]{2,1,0:T(8,128)(2,1)S(1)}, u32[]{:S(2)}, u32[]{:S(2)}) async-start(bf16[8,8,2176]{2,1,0:T(8,128)(2,1)} %shard_map.138), calls=%async_computation | async-start | bytes 557056 | tf_op jit(solution)/shard_map/all_to_all | solution.py:389
  23.3 8.3 %collective-permute-start.6 = (bf16[64,2048]{1,0:T(8,128)(2,1)}, bf16[64,2048]{1,0:T(8,128)(2,1)S(1)}, u32[]{:S(2)}, u32[]{:S(2)}) collective-permute-start(bf16[64,2048]{1,0:T(8,128)(2,1)} %refs_2_.2), channel_id=1, source_target_pairs={{0,2},{1,3},{2,0},{3,1},{4,6},{5,7},{6,4},{7,5},{8,10},{9,11},{10,... | collective-permute-start | bytes 786440 | tf_op jit(solution)/shard_map/ppermute | solution.py:22
  24.2 1.2 collective-permute-start.7
  24.2 1.3 %collective-permute-start.8 = (s32[64,4]{0,1:T(4,128)S(1)}, s32[64,4]{0,1:T(4,128)S(1)}, u32[]{:S(2)}, u32[]{:S(2)}) collective-permute-start(s32[64,4]{0,1:T(4,128)S(1)} %collective-permute-done.3), channel_id=1, source_target_pairs={{0,1},{1,0},{2,3},{3,2},{4,5},{5,4},{6,7},{7,6},{8,9},{9,8},{10,11... | collective-permute-start | bytes 3080 | tf_op jit(solution)/shard_map/ppermute | solution.py:22
  32.8 6.8 %collective-permute-start.9 = (bf16[8,8,2176]{2,1,0:T(8,128)(2,1)S(1)}, bf16[8,8,2176]{2,1,0:T(8,128)(2,1)S(1)}, u32[]{:S(2)}, u32[]{:S(2)}) collective-permute-start(bf16[8,8,2176]{2,1,0:T(8,128)(2,1)S(1)} %all-to-all-done.refs_0_), channel_id=1, source_target_pairs={{0,2},{1,3},{2,0},{3,1},{4,6},{5,7},{6,4},{7,5},{8,10},{9,11},{10,... | collective-permute-start | bytes 835592 | tf_op jit(solution)/shard_map/ppermute | solution.py:22
  39.7 1.0 copy-start.9
  41.3 2.0 %collective-permute-start.10 = (bf16[128,2048]{1,0:T(8,128)(2,1)S(1)}, bf16[128,2048]{1,0:T(8,128)(2,1)S(1)}, u32[]{:S(2)}, u32[]{:S(2)}) collective-permute-start(bf16[128,2048]{1,0:T(8,128)(2,1)S(1)} %get-tuple-element.91.refs_1_.refs_0_), channel_id=1, source_target_pairs={{0,1},{1,0},{2,3},{3,2},{4,5},{5,4},{6,7},{7,6},{8,9},{9,8},{10,11... | collective-permute-start | bytes 1572872 | tf_op jit(solution)/shard_map/ppermute | solution.py:22
  43.8 13.4 %collective-permute-start.12 = (bf16[24,2048]{1,0:T(8,128)(2,1)S(1)}, bf16[24,2048]{1,0:T(8,128)(2,1)S(1)}, u32[]{:S(2)}, u32[]{:S(2)}) collective-permute-start(bf16[24,2048]{1,0:T(8,128)(2,1)S(1)} %get-tuple-element.93), channel_id=1, source_target_pairs={{0,20},{4,16},{8,28},{12,24},{16,4},{20,0},{24,12},{28,8},{1,21},{... | collective-permute-start | bytes 294920 | tf_op jit(solution)/shard_map/ppermute | solution.py:22
  46.6 10.7 %collective-permute-start.11 = (bf16[24,2048]{1,0:T(8,128)(2,1)S(1)}, bf16[24,2048]{1,0:T(8,128)(2,1)S(1)}, u32[]{:S(2)}, u32[]{:S(2)}) collective-permute-start(bf16[24,2048]{1,0:T(8,128)(2,1)S(1)} %get-tuple-element.92), channel_id=1, source_target_pairs={{0,16},{4,20},{8,24},{12,28},{16,0},{20,4},{24,8},{28,12},{1,17},{... | collective-permute-start | bytes 294920 | tf_op jit(solution)/shard_map/ppermute | solution.py:22
  47.5 10.8 %collective-permute-start.16 = (bf16[48,2048]{1,0:T(8,128)(2,1)S(1)}, bf16[48,2048]{1,0:T(8,128)(2,1)S(1)}, u32[]{:S(2)}, u32[]{:S(2)}) collective-permute-start(bf16[48,2048]{1,0:T(8,128)(2,1)S(1)} %get-tuple-element.100), channel_id=1, source_target_pairs={{0,4},{4,0},{8,12},{12,8},{16,20},{20,16},{24,28},{28,24},{1,5},{5... | collective-permute-start | bytes 589832 | tf_op jit(solution)/shard_map/ppermute | solution.py:22
  48.3 13.0 %collective-permute-start.17 = (bf16[48,2048]{1,0:T(8,128)(2,1)S(1)}, bf16[48,2048]{1,0:T(8,128)(2,1)S(1)}, u32[]{:S(2)}, u32[]{:S(2)}) collective-permute-start(bf16[48,2048]{1,0:T(8,128)(2,1)S(1)} %get-tuple-element.103), channel_id=1, source_target_pairs={{0,8},{4,12},{8,0},{12,4},{16,24},{20,28},{24,16},{28,20},{1,9},{5... | collective-permute-start | bytes 589832 | tf_op jit(solution)/shard_map/ppermute | solution.py:22
  49.2 13.8 %collective-permute-start.18 = (bf16[48,2048]{1,0:T(8,128)(2,1)S(1)}, bf16[48,2048]{1,0:T(8,128)(2,1)S(1)}, u32[]{:S(2)}, u32[]{:S(2)}) collective-permute-start(bf16[48,2048]{1,0:T(8,128)(2,1)S(1)} %get-tuple-element.105), channel_id=1, source_target_pairs={{0,12},{4,8},{8,4},{12,0},{16,28},{20,24},{24,20},{28,16},{1,13},{... | collective-permute-start | bytes 589832 | tf_op jit(solution)/shard_map/ppermute | solution.py:22
  50.9 1.8 %copy-start.5 = (bf16[2048,704]{0,1:T(8,128)(2,1)S(1)}, bf16[2048,704]{0,1:T(8,128)(2,1)}, u32[]{:S(2)}) copy-start(bf16[2048,704]{0,1:T(8,128)(2,1)} %param.21) | copy-start | bytes 8650756
  52.8 1.8 %copy-start.6 = (bf16[704,2048]{1,0:T(8,128)(2,1)S(1)}, bf16[704,2048]{1,0:T(8,128)(2,1)}, u32[]{:S(2)}) copy-start(bf16[704,2048]{1,0:T(8,128)(2,1)} %refs_4_.1) | copy-start | bytes 8650756
  54.6 13.7 %copy-start = (bf16[1,2048,352]{1,2,0:T(8,128)(2,1)S(1)}, bf16[1,2048,352]{1,2,0:T(8,128)(2,1)}, u32[]{:S(2)}) copy-start(bf16[1,2048,352]{1,2,0:T(8,128)(2,1)} %param.23) | copy-start | bytes 4325380
  54.6 13.7 %copy-start.1 = (bf16[1,2048,352]{1,2,0:T(8,128)(2,1)S(1)}, bf16[1,2048,352]{1,2,0:T(8,128)(2,1)}, u32[]{:S(2)}) copy-start(bf16[1,2048,352]{1,2,0:T(8,128)(2,1)} %param.24) | copy-start | bytes 4325380
  54.6 13.7 %copy-start.2 = (bf16[1,352,2048]{2,1,0:T(8,128)(2,1)S(1)}, bf16[1,352,2048]{2,1,0:T(8,128)(2,1)}, u32[]{:S(2)}) copy-start(bf16[1,352,2048]{2,1,0:T(8,128)(2,1)} %param.25) | copy-start | bytes 4325380
  57.2 5.8 %collective-permute-start.19 = (bf16[48,2048]{1,0:T(8,128)(2,1)S(1)}, bf16[48,2048]{1,0:T(8,128)(2,1)S(1)}, u32[]{:S(2)}, u32[]{:S(2)}) collective-permute-start(bf16[48,2048]{1,0:T(8,128)(2,1)S(1)} %get-tuple-element.98.refs_0_), channel_id=1, source_target_pairs={{0,1},{1,0},{2,3},{3,2},{4,5},{5,4},{6,7},{7,6},{8,9},{9,8},{10,11... | collective-permute-start | bytes 589832 | tf_op jit(solution)/shard_map/ppermute | solution.py:22
  57.3 7.4 %collective-permute-start.13 = (bf16[48,2048]{1,0:T(8,128)(2,1)S(1)}, bf16[48,2048]{1,0:T(8,128)(2,1)S(1)}, u32[]{:S(2)}, u32[]{:S(2)}) collective-permute-start(bf16[48,2048]{1,0:T(8,128)(2,1)S(1)} %pad_maximum_fusion.1.refs_0_), channel_id=1, source_target_pairs={{0,2},{1,3},{2,0},{3,1},{4,6},{5,7},{6,4},{7,5},{8,10},{9,11},{10,... | collective-permute-start | bytes 589832 | tf_op jit(solution)/shard_map/ppermute | solution.py:22
  58.3 6.8 %collective-permute-start.31 = (bf16[24,2048]{1,0:T(8,128)(2,1)S(1)}, bf16[24,2048]{1,0:T(8,128)(2,1)S(1)}, u32[]{:S(2)}, u32[]{:S(2)}) collective-permute-start(bf16[24,2048]{1,0:T(8,128)(2,1)S(1)} %get-tuple-element.116), channel_id=1, source_target_pairs={{0,24},{4,28},{8,16},{12,20},{16,8},{20,12},{24,0},{28,4},{1,25},{... | collective-permute-start | bytes 294920 | tf_op jit(solution)/shard_map/ppermute | solution.py:22
  61.3 10.2 %collective-permute-start.14 = (bf16[48,2048]{1,0:T(8,128)(2,1)S(1)}, bf16[48,2048]{1,0:T(8,128)(2,1)S(1)}, u32[]{:S(2)}, u32[]{:S(2)}) collective-permute-start(bf16[48,2048]{1,0:T(8,128)(2,1)S(1)} %pad_maximum_fusion.1.refs_0_), channel_id=1, source_target_pairs={{0,1},{1,0},{2,3},{3,2},{4,5},{5,4},{6,7},{7,6},{8,9},{9,8},{10,11... | collective-permute-start | bytes 589832 | tf_op jit(solution)/shard_map/ppermute | solution.py:22
  63.0 2.2 %collective-permute-start.20 = (bf16[48,2048]{1,0:T(8,128)(2,1)S(1)}, bf16[48,2048]{1,0:T(8,128)(2,1)S(1)}, u32[]{:S(2)}, u32[]{:S(2)}) collective-permute-start(bf16[48,2048]{1,0:T(8,128)(2,1)S(1)} %collective-permute-done.16.refs_1_), channel_id=1, source_target_pairs={{0,1},{1,0},{2,3},{3,2},{4,5},{5,4},{6,7},{7,6},{8,9},{9,8},{10,11... | collective-permute-start | bytes 589832 | tf_op jit(solution)/shard_map/ppermute | solution.py:22
  63.0 5.3 %collective-permute-start.21 = (bf16[48,2048]{1,0:T(8,128)(2,1)S(1)}, bf16[48,2048]{1,0:T(8,128)(2,1)S(1)}, u32[]{:S(2)}, u32[]{:S(2)}) collective-permute-start(bf16[48,2048]{1,0:T(8,128)(2,1)S(1)} %collective-permute-done.17.refs_2_), channel_id=1, source_target_pairs={{0,1},{1,0},{2,3},{3,2},{4,5},{5,4},{6,7},{7,6},{8,9},{9,8},{10,11... | collective-permute-start | bytes 589832 | tf_op jit(solution)/shard_map/ppermute | solution.py:22
  64.7 3.6 %collective-permute-start.22 = (bf16[48,2048]{1,0:T(8,128)(2,1)S(1)}, bf16[48,2048]{1,0:T(8,128)(2,1)S(1)}, u32[]{:S(2)}, u32[]{:S(2)}) collective-permute-start(bf16[48,2048]{1,0:T(8,128)(2,1)S(1)} %collective-permute-done.18.refs_3_), channel_id=1, source_target_pairs={{0,1},{1,0},{2,3},{3,2},{4,5},{5,4},{6,7},{7,6},{8,9},{9,8},{10,11... | collective-permute-start | bytes 589832 | tf_op jit(solution)/shard_map/ppermute | solution.py:22
  65.1 6.4 %collective-permute-start.15 = (bf16[48,2048]{1,0:T(8,128)(2,1)S(1)}, bf16[48,2048]{1,0:T(8,128)(2,1)S(1)}, u32[]{:S(2)}, u32[]{:S(2)}) collective-permute-start(bf16[48,2048]{1,0:T(8,128)(2,1)S(1)} %collective-permute-done.13.refs_1_), channel_id=1, source_target_pairs={{0,1},{1,0},{2,3},{3,2},{4,5},{5,4},{6,7},{7,6},{8,9},{9,8},{10,11... | collective-permute-start | bytes 589832 | tf_op jit(solution)/shard_map/ppermute | solution.py:22
  65.2 8.1 %collective-permute-start.32 = (bf16[24,2048]{1,0:T(8,128)(2,1)S(1)}, bf16[24,2048]{1,0:T(8,128)(2,1)S(1)}, u32[]{:S(2)}, u32[]{:S(2)}) collective-permute-start(bf16[24,2048]{1,0:T(8,128)(2,1)S(1)} %get-tuple-element.117), channel_id=1, source_target_pairs={{0,28},{4,24},{8,20},{12,16},{16,12},{20,8},{24,4},{28,0},{1,29},{... | collective-permute-start | bytes 294920 | tf_op jit(solution)/shard_map/ppermute | solution.py:22
  73.2 7.5 %collective-permute-start.27 = (bf16[96,2048]{1,0:T(8,128)(2,1)S(1)}, bf16[96,2048]{1,0:T(8,128)(2,1)S(1)}, u32[]{:S(2)}, u32[]{:S(2)}) collective-permute-start(bf16[96,2048]{1,0:T(8,128)(2,1)S(1)} %get-tuple-element.115), channel_id=1, source_target_pairs={{0,1},{1,0},{2,3},{3,2},{4,5},{5,4},{6,7},{7,6},{8,9},{9,8},{10,11... | collective-permute-start | bytes 1179656 | tf_op jit(solution)/shard_map/ppermute | solution.py:22
  73.4 7.2 %collective-permute-start.33 = (bf16[48,2048]{1,0:T(8,128)(2,1)S(1)}, bf16[48,2048]{1,0:T(8,128)(2,1)S(1)}, u32[]{:S(2)}, u32[]{:S(2)}) collective-permute-start(bf16[48,2048]{1,0:T(8,128)(2,1)S(1)} %constant_dynamic-update-slice_fusion.refs_0_), channel_id=1, source_target_pairs={{0,2},{1,3},{2,0},{3,1},{4,6},{5,7},{6,4},{7,5},{8,10},{9,11},{10,... | collective-permute-start | bytes 589832 | tf_op jit(solution)/shard_map/ppermute | solution.py:22
  74.6 7.8 %collective-permute-start.34 = (bf16[48,2048]{1,0:T(8,128)(2,1)S(1)}, bf16[48,2048]{1,0:T(8,128)(2,1)S(1)}, u32[]{:S(2)}, u32[]{:S(2)}) collective-permute-start(bf16[48,2048]{1,0:T(8,128)(2,1)S(1)} %constant_dynamic-update-slice_fusion.refs_0_), channel_id=1, source_target_pairs={{0,1},{1,0},{2,3},{3,2},{4,5},{5,4},{6,7},{7,6},{8,9},{9,8},{10,11... | collective-permute-start | bytes 589832 | tf_op jit(solution)/shard_map/ppermute | solution.py:22
  80.6 1.8 %collective-permute-start.35 = (bf16[48,2048]{1,0:T(8,128)(2,1)S(1)}, bf16[48,2048]{1,0:T(8,128)(2,1)S(1)}, u32[]{:S(2)}, u32[]{:S(2)}) collective-permute-start(bf16[48,2048]{1,0:T(8,128)(2,1)S(1)} %collective-permute-done.33.refs_1_), channel_id=1, source_target_pairs={{0,1},{1,0},{2,3},{3,2},{4,5},{5,4},{6,7},{7,6},{8,9},{9,8},{10,11... | collective-permute-start | bytes 589832 | tf_op jit(solution)/shard_map/ppermute | solution.py:22
  80.8 7.4 %collective-permute-start.28 = (bf16[48,2048]{1,0:T(8,128)(2,1)S(1)}, bf16[48,2048]{1,0:T(8,128)(2,1)S(1)}, u32[]{:S(2)}, u32[]{:S(2)}) collective-permute-start(bf16[48,2048]{1,0:T(8,128)(2,1)S(1)} %slice.101), channel_id=1, source_target_pairs={{0,2},{1,3},{2,0},{3,1},{4,6},{5,7},{6,4},{7,5},{8,10},{9,11},{10,... | collective-permute-start | bytes 589832 | tf_op jit(solution)/shard_map/ppermute | solution.py:22
  82.1 11.9 %collective-permute-start.23 = (bf16[192,2048]{1,0:T(8,128)(2,1)S(1)}, bf16[192,2048]{1,0:T(8,128)(2,1)S(1)}, u32[]{:S(2)}, u32[]{:S(2)}) collective-permute-start(bf16[192,2048]{1,0:T(8,128)(2,1)S(1)} %get-tuple-element.109), channel_id=1, source_target_pairs={{0,1},{1,0},{2,3},{3,2},{4,5},{5,4},{6,7},{7,6},{8,9},{9,8},{10,11... | collective-permute-start | bytes 2359304 | tf_op jit(solution)/shard_map/ppermute | solution.py:22
  84.0 9.5 %collective-permute-start.36 = (bf16[96,2048]{1,0:T(8,128)(2,1)S(1)}, bf16[96,2048]{1,0:T(8,128)(2,1)S(1)}, u32[]{:S(2)}, u32[]{:S(2)}) collective-permute-start(bf16[96,2048]{1,0:T(8,128)(2,1)S(1)} %get-tuple-element.119), channel_id=1, source_target_pairs={{0,1},{1,0},{2,3},{3,2},{4,5},{5,4},{6,7},{7,6},{8,9},{9,8},{10,11... | collective-permute-start | bytes 1179656 | tf_op jit(solution)/shard_map/ppermute | solution.py:22
  88.2 11.6 %collective-permute-start.29 = (bf16[24,2048]{1,0:T(8,128)(2,1)S(1)}, bf16[24,2048]{1,0:T(8,128)(2,1)S(1)}, u32[]{:S(2)}, u32[]{:S(2)}) collective-permute-start(bf16[24,2048]{1,0:T(8,128)(2,1)S(1)} %get-tuple-element.130), channel_id=1, source_target_pairs={{0,16},{4,20},{8,24},{12,28},{16,0},{20,4},{24,8},{28,12},{1,17},{... | collective-permute-start | bytes 294920 | tf_op jit(solution)/shard_map/ppermute | solution.py:22
  89.3 12.3 %collective-permute-start.30 = (bf16[24,2048]{1,0:T(8,128)(2,1)S(1)}, bf16[24,2048]{1,0:T(8,128)(2,1)S(1)}, u32[]{:S(2)}, u32[]{:S(2)}) collective-permute-start(bf16[24,2048]{1,0:T(8,128)(2,1)S(1)} %get-tuple-element.129), channel_id=1, source_target_pairs={{0,20},{4,16},{8,28},{12,24},{16,4},{20,0},{24,12},{28,8},{1,21},{... | collective-permute-start | bytes 294920 | tf_op jit(solution)/shard_map/ppermute | solution.py:22
  93.6 6.0 %collective-permute-start.37 = (bf16[48,2048]{1,0:T(8,128)(2,1)S(1)}, bf16[48,2048]{1,0:T(8,128)(2,1)S(1)}, u32[]{:S(2)}, u32[]{:S(2)}) collective-permute-start(bf16[48,2048]{1,0:T(8,128)(2,1)S(1)} %slice.105), channel_id=1, source_target_pairs={{0,2},{1,3},{2,0},{3,1},{4,6},{5,7},{6,4},{7,5},{8,10},{9,11},{10,... | collective-permute-start | bytes 589832 | tf_op jit(solution)/shard_map/ppermute | solution.py:22
  94.4 15.8 %collective-permute-start.24 = (bf16[48,2048]{1,0:T(8,128)(2,1)S(1)}, bf16[48,2048]{1,0:T(8,128)(2,1)S(1)}, u32[]{:S(2)}, u32[]{:S(2)}) collective-permute-start(bf16[48,2048]{1,0:T(8,128)(2,1)S(1)} %get-tuple-element.123), channel_id=1, source_target_pairs={{0,4},{4,0},{8,12},{12,8},{16,20},{20,16},{24,28},{28,24},{1,5},{5... | collective-permute-start | bytes 589832 | tf_op jit(solution)/shard_map/ppermute | solution.py:22
  94.4 15.7 %collective-permute-start.25 = (bf16[48,2048]{1,0:T(8,128)(2,1)S(1)}, bf16[48,2048]{1,0:T(8,128)(2,1)S(1)}, u32[]{:S(2)}, u32[]{:S(2)}) collective-permute-start(bf16[48,2048]{1,0:T(8,128)(2,1)S(1)} %get-tuple-element.122), channel_id=1, source_target_pairs={{0,8},{4,12},{8,0},{12,4},{16,24},{20,28},{24,16},{28,20},{1,9},{5... | collective-permute-start | bytes 589832 | tf_op jit(solution)/shard_map/ppermute | solution.py:22
  99.7 12.7 %collective-permute-start.26 = (bf16[48,2048]{1,0:T(8,128)(2,1)S(1)}, bf16[48,2048]{1,0:T(8,128)(2,1)S(1)}, u32[]{:S(2)}, u32[]{:S(2)}) collective-permute-start(bf16[48,2048]{1,0:T(8,128)(2,1)S(1)} %get-tuple-element.121), channel_id=1, source_target_pairs={{0,12},{4,8},{8,4},{12,0},{16,28},{20,24},{24,20},{28,16},{1,13},{... | collective-permute-start | bytes 589832 | tf_op jit(solution)/shard_map/ppermute | solution.py:22
  99.8 8.9 %collective-permute-start.38 = (bf16[24,2048]{1,0:T(8,128)(2,1)S(1)}, bf16[24,2048]{1,0:T(8,128)(2,1)S(1)}, u32[]{:S(2)}, u32[]{:S(2)}) collective-permute-start(bf16[24,2048]{1,0:T(8,128)(2,1)S(1)} %get-tuple-element.128), channel_id=1, source_target_pairs={{0,24},{4,28},{8,16},{12,20},{16,8},{20,12},{24,0},{28,4},{1,25},{... | collective-permute-start | bytes 294920 | tf_op jit(solution)/shard_map/ppermute | solution.py:22
  101.6 8.5 %collective-permute-start.39 = (bf16[24,2048]{1,0:T(8,128)(2,1)S(1)}, bf16[24,2048]{1,0:T(8,128)(2,1)S(1)}, u32[]{:S(2)}, u32[]{:S(2)}) collective-permute-start(bf16[24,2048]{1,0:T(8,128)(2,1)S(1)} %get-tuple-element.127), channel_id=1, source_target_pairs={{0,28},{4,24},{8,20},{12,16},{16,12},{20,8},{24,4},{28,0},{1,29},{... | collective-permute-start | bytes 294920 | tf_op jit(solution)/shard_map/ppermute | solution.py:22
  113.1 2.0 %collective-permute-start.40 = (bf16[128,2048]{1,0:T(8,128)(2,1)S(1)}, bf16[128,2048]{1,0:T(8,128)(2,1)S(1)}, u32[]{:S(2)}, u32[]{:S(2)}) collective-permute-start(bf16[128,2048]{1,0:T(8,128)(2,1)S(1)} %shard_map.146), channel_id=1, source_target_pairs={{0,1},{1,0},{2,3},{3,2},{4,5},{5,4},{6,7},{7,6},{8,9},{9,8},{10,11... | collective-permute-start | bytes 1572872 | tf_op jit(solution)/shard_map/ppermute | solution.py:22
  115.3 8.4 %collective-permute-start.41 = (bf16[64,2048]{1,0:T(8,128)(2,1)S(1)}, bf16[64,2048]{1,0:T(8,128)(2,1)S(1)}, u32[]{:S(2)}, u32[]{:S(2)}) collective-permute-start(bf16[64,2048]{1,0:T(8,128)(2,1)S(1)} %slice.109), channel_id=1, source_target_pairs={{0,2},{1,3},{2,0},{3,1},{4,6},{5,7},{6,4},{7,5},{8,10},{9,11},{10,... | collective-permute-start | bytes 786440 | tf_op jit(solution)/shard_map/ppermute | solution.py:22

commit v4 on v3

--- a/solution.py
+++ b/solution.py
@@ -427,39 +427,41 @@
     got[0] = send[0]
     quarter = n_data // 4
     near, far_one, far_two = range(half), range(half, half + quarter), range(half + quarter, n_data)
+
+    def join(stage):
+        return jnp.concatenate([got[m] for m in stage], axis=0)
+
+    def both(pieces):
+        return pieces + [swap(p, "expert", 1) for p in pieces]
+
+    def send_back(m, rows, i):
+        part = rows[i * sizes[m] : (i + 1) * sizes[m]]
+        return swap(part, "dp", m) if m else part
+
     for m in (*near[1:], *far_one):
         got[m] = swap(send[m], "dp", m)
-    for i, m in enumerate(far_two):
-        late, got[i + 1] = lax.optimization_barrier((send[m], got[i + 1]))
-        got[m] = swap(late, "dp", m)
-
     shared = shared_rows(normed, shared_gate.T, shared_up.T, shared_down)
-    def total_of(keep, give):
-        return sum_rest(add(keep, swap(give, "expert", 1)))
+    one, shared, send = fence(join(far_one), shared, send)
+
+    for m in far_two:
+        got[m] = swap(send[m], "dp", m)
+    one, got = fence(spread(one), got)
 
     experts = (expert_gate[0].T, expert_up[0].T, expert_down[0])
-
-    def join(stage):
-        return jnp.concatenate([got[m] for m in stage], axis=0)
-
-    far = join(far_one)
-    far, shared = lax.optimization_barrier((far, shared))
-    far_pieces = gather(far, "expert")
-    mine = [got[m] for m in near]
-    keep, give = expert_rows(mine + [swap(p, "expert", 1) for p in mine], *experts)
-    far_pieces, keep, give = lax.optimization_barrier((far_pieces, keep, give))
-    back = [None] * n_data
-
-    def send_back(stage, rows):
-        size = sizes[stage[0]]
-        for i, m in enumerate(stage):
-            part = rows[i * size : (i + 1) * size]
-            back[m] = swap(part, "dp", m) if m else part
-
-    send_back(near, add(keep, swap(give, "expert", 1)))
-    send_back(far_one, total_of(*expert_rows(far_pieces, *experts)))
-    pieces = gather(join(far_two), "expert")
-    send_back(far_two, total_of(*expert_rows(pieces, *experts)))
+    one_keep, one_give = expert_rows(both(one), *experts)
+    two, one_keep, one_give = fence(spread(join(far_two)), one_keep, one_give)
+    two_keep, two_give = expert_rows(both(two), *experts)
+    mine = join(near)
+    mine = [mine, swap(mine, "expert", 1)]
+    mine, two_keep = fence(mine, two_keep)
+    keep, give = expert_rows(mine, *experts)
+    one = sum_rest(add(one_keep, swap(one_give, "expert", 1)))
+    one, keep, give = fence(one, keep, give)
+    two = sum_rest(add(two_keep, swap(two_give, "expert", 1)))
+    rows = add(keep, swap(give, "expert", 1))
+    back = [send_back(m, rows, m) for m in near]
+    back += [send_back(m, one, i) for i, m in enumerate(far_one)]
+    back += [send_back(m, two, i) for i, m in enumerate(far_two)]
 
     middle = group_rows // 2
     keep, give = [

time: 125 us -> 122 us (0.976)
  waiting for transfers between devices: 52.9 us -> 50.2 us
    ppermute x42 -> x39, waiting for transfers between devices: 51.7 us -> 49 us  [swap(): return lax.ppermute(rows, axis, [(i, i ^ mask) for i in range(count)])]
    ppermute x42 -> x39, starting transfers between devices: 37.2 us -> 37 us  [swap(): return lax.ppermute(rows, axis, [(i, i ^ mask) for i in range(count)])]
    unnamed x25 -> x28, local copies, waits for them, and re-layouts: 9.5 us -> 9.54 us
  transfers between devices with their start and end apart: 43 -> 40, of which waited for: 19 -> 24; matrix products, arithmetic and copies ran while one was open for 2% -> 2% of each run, Pallas kernels for 8% -> 9%
where the time goes in v4:
time: 122 us
  waiting for transfers between devices  50.2 us (41%)
  starting transfers between devices  42.8 us (35%)
  Pallas kernels  15.2 us (12%)
  local copies, waits for them, and re-layouts  9.87 us (8%)
  other arithmetic  2.95 us (2%)
    ppermute x39, waiting for transfers between devices, swap(): return lax.ppermute(rows, axis, [(i, i ^ mask) for i in range(count)])  49 us
    ppermute x39, starting transfers between devices, swap(): return lax.ppermute(rows, axis, [(i, i ^ mask) for i in range(count)])  37 us
    pallas_call x10, Pallas kernels, local_kernel(): pl.pallas_call(body, out_shape=list(outs), in_specs=[pl.BlockSpec(memory_...  14.6 us
    unnamed x28, local copies, waits for them, and re-layouts  9.54 us
    all_to_all x1, starting transfers between devices, shards(): lax.all_to_all(leaving, 'dp', split_axis=0, concat_axis=0, tiled=True)  5.81 us
  transfers between devices with their start and end apart: 40, of which 24 were waited for; matrix products, arithmetic and copies ran while one was open for 2% of the time, Pallas kernels for 9%

profile of v4, /device:TPU:0, one launch (start us, length us, event | category | flops | bytes accessed | tf_op | source)
XLA Modules:
  0.0 121.6 jit_solution(17280332577443837125)
XLA Ops:
  0.0 3.0 %collective-permute-start = (bf16[32,4608]{1,0:T(8,128)(2,1)}, bf16[32,4608]{1,0:T(8,128)(2,1)S(1)}, u32[]{:S(2)}, u32[]{:S(2)}) collective-permute-start(bf16[32,4608]{1,0:T(8,128)(2,1)} %refs_2_.1), channel_id=1, source_target_pairs={{0,2},{1,3},{2,0},{3,1},{4,6},{5,7},{6,4},{7,5},{8,10},{9,11},{10,... | collective-permute-start | bytes 884744 | tf_op jit(solution)/shard_map/ppermute | solution.py:22
  3.0 0.7 pad_add_fusion.1
  3.7 2.0 %collective-permute-start.2 = (s32[32]{0:T(128)}, s32[32]{0:T(128)S(1)}, u32[]{:S(2)}, u32[]{:S(2)}) collective-permute-start(s32[32]{0:T(128)} %param.16), channel_id=1, source_target_pairs={{0,2},{1,3},{2,0},{3,1},{4,6},{5,7},{6,4},{7,5},{8,10},{9,11},{10,... | collective-permute-start | bytes 392 | tf_op jit(solution)/shard_map/ppermute | solution.py:22
  5.7 2.3 %copy-done.3 = bf16[4608,512]{1,0:T(8,128)(2,1)S(1)} copy-done((bf16[4608,512]{1,0:T(8,128)(2,1)S(1)}, bf16[4608,512]{1,0:T(8,128)(2,1)}, u32[]{:S(2)}) %copy-start.3) | copy-done | bytes 4718616
  8.0 1.6 %copy-done.7 = bf16[512,2048]{1,0:T(8,128)(2,1)S(1)} copy-done((bf16[512,2048]{1,0:T(8,128)(2,1)S(1)}, bf16[512,2048]{1,0:T(8,128)(2,1)}, u32[]{:S(2)}) %copy-start.7) | copy-done | bytes 2097176
  9.6 1.0 copy-done.8
  10.6 0.5 shard_map.136
  11.3 1.6 %collective-permute-done.4.refs_3_ = bf16[32,4608]{1,0:T(8,128)(2,1)S(1)} collective-permute-done((bf16[32,4608]{1,0:T(8,128)(2,1)S(1)}, bf16[32,4608]{1,0:T(8,128)(2,1)S(1)}, u32[]{:S(2)}, u32[]{:S(2)}) %collective-permute-start.4) | collective-permute-done | bytes 294944 | tf_op jit(solution)/shard_map/ppermute | solution.py:22
  12.8 1.9 %shard_map.137 = (bf16[64,2048]{1,0:T(8,128)(2,1)S(1)}, bf16[64,2048]{1,0:T(8,128)(2,1)}) custom-call(bf16[32,4608]{1,0:T(8,128)(2,1)S(1)} %get-tuple-element.78.refs_0_, bf16[32,4608]{1,0:T(8,128)(2,1)S(1)} %collective-permute-done.refs_1_, bf16[32,4608]{1,0:T(8,128)(2,1)S(1)} %collective-permute-done.1.refs_2_, ...), custom_call_target="tpu_custom_call" | custom-call | flops 872415232 | bytes 8519680 | tf_op jit(solution)/shard_map/pallas_call | solution.py:68
  15.2 1.3 %collective-permute-done.5.other_ref = bf16[64,2048]{1,0:T(8,128)(2,1)S(1)} collective-permute-done((bf16[64,2048]{1,0:T(8,128)(2,1)}, bf16[64,2048]{1,0:T(8,128)(2,1)S(1)}, u32[]{:S(2)}, u32[]{:S(2)}) %collective-permute-start.5) | collective-permute-done | bytes 262176 | tf_op jit(solution)/shard_map/ppermute | solution.py:22
  16.6 0.9 shard_map.138
  17.5 5.8 %all-to-all-start = ((bf16[8,8,2176]{2,1,0:T(8,128)(2,1)}), bf16[8,8,2176]{2,1,0:T(8,128)(2,1)S(1)}, u32[]{:S(2)}, u32[]{:S(2)}) async-start(bf16[8,8,2176]{2,1,0:T(8,128)(2,1)} %shard_map.138), calls=%async_computation | async-start | bytes 557056 | tf_op jit(solution)/shard_map/all_to_all | solution.py:389
  23.3 0.9 collective-permute-start.6
  24.2 0.5 collective-permute-start.8
  24.7 0.6 collective-permute-done.7
  25.5 6.1 %collective-permute-done.6.refs_3_ = bf16[64,2048]{1,0:T(8,128)(2,1)S(1)} collective-permute-done((bf16[64,2048]{1,0:T(8,128)(2,1)}, bf16[64,2048]{1,0:T(8,128)(2,1)S(1)}, u32[]{:S(2)}, u32[]{:S(2)}) %collective-permute-start.6) | collective-permute-done | bytes 262176 | tf_op jit(solution)/shard_map/ppermute | solution.py:22
  31.6 1.2 %all-to-all-done.refs_0_ = bf16[8,8,2176]{2,1,0:T(8,128)(2,1)S(1)} async-done(((bf16[8,8,2176]{2,1,0:T(8,128)(2,1)}), bf16[8,8,2176]{2,1,0:T(8,128)(2,1)S(1)}, u32[]{:S(2)}, u32[]{:S(2)}) %all-to-all-start) | async-done | bytes 278560 | tf_op jit(solution)/shard_map/all_to_all | solution.py:389
  32.8 0.9 collective-permute-start.9
  34.1 5.5 %collective-permute-done.9.refs_1_ = bf16[8,8,2176]{2,1,0:T(8,128)(2,1)S(1)} collective-permute-done((bf16[8,8,2176]{2,1,0:T(8,128)(2,1)S(1)}, bf16[8,8,2176]{2,1,0:T(8,128)(2,1)S(1)}, u32[]{:S(2)}, u32[]{:S(2)}) %collective-permute-start.9) | collective-permute-done | bytes 278560 | tf_op jit(solution)/shard_map/ppermute | solution.py:22
  39.6 0.9 copy-done.9
  40.6 0.7 shard_map.139
  41.5 1.8 %collective-permute-done.10.refs_2_.refs_1_ = bf16[128,2048]{1,0:T(8,128)(2,1)S(1)} collective-permute-done((bf16[128,2048]{1,0:T(8,128)(2,1)S(1)}, bf16[128,2048]{1,0:T(8,128)(2,1)S(1)}, u32[]{:S(2)}, u32[]{:S(2)}) %collective-permute-start.10) | collective-permute-done | bytes 524320 | tf_op jit(solution)/shard_map/ppermute | solution.py:22
  43.3 0.5 shard_map.140
  43.8 2.8 %collective-permute-start.12 = (bf16[24,2048]{1,0:T(8,128)(2,1)S(1)}, bf16[24,2048]{1,0:T(8,128)(2,1)S(1)}, u32[]{:S(2)}, u32[]{:S(2)}) collective-permute-start(bf16[24,2048]{1,0:T(8,128)(2,1)S(1)} %get-tuple-element.103), channel_id=1, source_target_pairs={{0,20},{4,16},{8,28},{12,24},{16,4},{20,0},{24,12},{28,8},{1,21},{... | collective-permute-start | bytes 294920 | tf_op jit(solution)/shard_map/ppermute | solution.py:22
  46.6 0.8 collective-permute-start.11
  47.4 0.8 collective-permute-start.14
  48.3 0.9 collective-permute-start.15
  49.2 1.8 %collective-permute-start.16 = (bf16[48,2048]{1,0:T(8,128)(2,1)S(1)}, bf16[48,2048]{1,0:T(8,128)(2,1)S(1)}, u32[]{:S(2)}, u32[]{:S(2)}) collective-permute-start(bf16[48,2048]{1,0:T(8,128)(2,1)S(1)} %get-tuple-element.109), channel_id=1, source_target_pairs={{0,12},{4,8},{8,4},{12,0},{16,28},{20,24},{24,20},{28,16},{1,13},{... | collective-permute-start | bytes 589832 | tf_op jit(solution)/shard_map/ppermute | solution.py:22
  50.9 1.8 %copy-done.5 = bf16[2048,704]{0,1:T(8,128)(2,1)S(1)} copy-done((bf16[2048,704]{0,1:T(8,128)(2,1)S(1)}, bf16[2048,704]{0,1:T(8,128)(2,1)}, u32[]{:S(2)}) %copy-start.5) | copy-done | bytes 2883608
  52.7 1.8 %copy-done.6 = bf16[704,2048]{1,0:T(8,128)(2,1)S(1)} copy-done((bf16[704,2048]{1,0:T(8,128)(2,1)S(1)}, bf16[704,2048]{1,0:T(8,128)(2,1)}, u32[]{:S(2)}) %copy-start.6) | copy-done | bytes 2883608
  54.6 2.6 %shard_map.141 = (f32[128,2048]{1,0:T(8,128)S(1)}, f32[128,2048]{1,0:T(8,128)S(1)}) custom-call(bf16[128,2048]{1,0:T(8,128)(2,1)S(1)} %get-tuple-element.101.refs_1_.refs_0_, bf16[128,2048]{1,0:T(8,128)(2,1)S(1)} %collective-permute-done.10.refs_2_.refs_1_, bf16[704,2048]{1,0:T(8,128)(2,1)S(1)} %bitcast.26, bf16[704,2048]{1,0:T(8,128)(2,1)S(1)} %bitcast.27, ...), custom_call_target="tpu_custom_call" | custom-call | flops 2214592512 | bytes 11796480 | tf_op jit(solution)/shard_map/pallas_call | solution.py:68
  57.3 0.9 collective-permute-start.13
  58.2 3.0 %collective-permute-start.17 = (bf16[24,2048]{1,0:T(8,128)(2,1)S(1)}, bf16[24,2048]{1,0:T(8,128)(2,1)S(1)}, u32[]{:S(2)}, u32[]{:S(2)}) collective-permute-start(bf16[24,2048]{1,0:T(8,128)(2,1)S(1)} %get-tuple-element.114), channel_id=1, source_target_pairs={{0,24},{4,28},{8,16},{12,20},{16,8},{20,12},{24,0},{28,4},{1,25},{... | collective-permute-start | bytes 294920 | tf_op jit(solution)/shard_map/ppermute | solution.py:22
  61.2 1.1 collective-permute-start.18
  62.3 2.8 %collective-permute-done.16 = bf16[48,2048]{1,0:T(8,128)(2,1)S(1)} collective-permute-done((bf16[48,2048]{1,0:T(8,128)(2,1)S(1)}, bf16[48,2048]{1,0:T(8,128)(2,1)S(1)}, u32[]{:S(2)}, u32[]{:S(2)}) %collective-permute-start.16) | collective-permute-done | bytes 196640 | tf_op jit(solution)/shard_map/ppermute | solution.py:22
  65.1 3.5 %collective-permute-done.18 = bf16[24,2048]{1,0:T(8,128)(2,1)S(1)} collective-permute-done((bf16[24,2048]{1,0:T(8,128)(2,1)S(1)}, bf16[24,2048]{1,0:T(8,128)(2,1)S(1)}, u32[]{:S(2)}, u32[]{:S(2)}) %collective-permute-start.18) | collective-permute-done | bytes 98336 | tf_op jit(solution)/shard_map/ppermute | solution.py:22
  68.6 1.2 collective-permute-start.19
  69.8 0.5 collective-permute-start.21
  70.4 0.9 collective-permute-done.20.refs_2_
  71.6 1.7 %shard_map.142 = (bf16[96,2048]{1,0:T(8,128)(2,1)S(1)}, bf16[96,2048]{1,0:T(8,128)(2,1)S(1)}) custom-call(bf16[48,2048]{1,0:T(8,128)(2,1)S(1)} %pad_maximum_fusion.1.refs_0_, bf16[48,2048]{1,0:T(8,128)(2,1)S(1)} %collective-permute-done.13.refs_1_, bf16[48,2048]{1,0:T(8,128)(2,1)S(1)} %collective-permute-done.20.refs_2_, ...), custom_call_target="tpu_custom_call" | custom-call | flops 830472192 | bytes 5898240 | tf_op jit(solution)/shard_map/pallas_call | solution.py:68
  73.2 1.1 collective-permute-done.19.refs_1_
  74.4 0.6 collective-permute-start.24
  76.2 1.2 collective-permute-start.23
  77.8 1.7 %shard_map.143 = (bf16[96,2048]{1,0:T(8,128)(2,1)S(1)}, bf16[96,2048]{1,0:T(8,128)(2,1)S(1)}) custom-call(bf16[48,2048]{1,0:T(8,128)(2,1)S(1)} %constant_dynamic-update-slice_fusion.refs_0_, bf16[48,2048]{1,0:T(8,128)(2,1)S(1)} %collective-permute-done.19.refs_1_, bf16[48,2048]{1,0:T(8,128)(2,1)S(1)} %collective-permute-done.25.refs_2_, ...), custom_call_target="tpu_custom_call" | custom-call | flops 830472192 | bytes 5898240 | tf_op jit(solution)/shard_map/pallas_call | solution.py:68
  79.6 3.2 %shard_map.144 = (bf16[192,2048]{1,0:T(8,128)(2,1)S(1)}, bf16[192,2048]{1,0:T(8,128)(2,1)S(1)}) custom-call(bf16[192,2048]{1,0:T(8,128)(2,1)S(1)} %constant_dynamic-update-slice_fusion.2.refs_0_, bf16[192,2048]{1,0:T(8,128)(2,1)S(1)} %collective-permute-done.24.refs_1_, bf16[352,2048]{1,0:T(8,128)(2,1)S(1)} %bitcast.19, bf16[352,2048]{1,0:T(8,128)(2,1)S(1)} %bitcast.22, ...), custom_call_target="tpu_custom_call" | custom-call | flops 1660944384 | bytes 7471104 | tf_op jit(solution)/shard_map/pallas_call | solution.py:68
  83.5 1.2 collective-permute-start.34
  84.7 1.4 %collective-permute-start.31 = (bf16[24,2048]{1,0:T(8,128)(2,1)S(1)}, bf16[24,2048]{1,0:T(8,128)(2,1)S(1)}, u32[]{:S(2)}, u32[]{:S(2)}) collective-permute-start(bf16[24,2048]{1,0:T(8,128)(2,1)S(1)} %get-tuple-element.150), channel_id=1, source_target_pairs={{0,16},{4,20},{8,24},{12,28},{16,0},{20,4},{24,8},{28,12},{1,17},{... | collective-permute-start | bytes 294920 | tf_op jit(solution)/shard_map/ppermute | solution.py:22
  86.1 1.6 %collective-permute-start.32 = (bf16[24,2048]{1,0:T(8,128)(2,1)S(1)}, bf16[24,2048]{1,0:T(8,128)(2,1)S(1)}, u32[]{:S(2)}, u32[]{:S(2)}) collective-permute-start(bf16[24,2048]{1,0:T(8,128)(2,1)S(1)} %get-tuple-element.149), channel_id=1, source_target_pairs={{0,20},{4,16},{8,28},{12,24},{16,4},{20,0},{24,12},{28,8},{1,21},{... | collective-permute-start | bytes 294920 | tf_op jit(solution)/shard_map/ppermute | solution.py:22
  87.7 3.1 %collective-permute-done.34 = bf16[48,2048]{1,0:T(8,128)(2,1)S(1)} collective-permute-done((bf16[48,2048]{1,0:T(8,128)(2,1)S(1)}, bf16[48,2048]{1,0:T(8,128)(2,1)S(1)}, u32[]{:S(2)}, u32[]{:S(2)}) %collective-permute-start.34) | collective-permute-done | bytes 196640 | tf_op jit(solution)/shard_map/ppermute | solution.py:22
  91.3 0.6 collective-permute-start.28
  91.9 1.4 %collective-permute-start.29 = (bf16[48,2048]{1,0:T(8,128)(2,1)S(1)}, bf16[48,2048]{1,0:T(8,128)(2,1)S(1)}, u32[]{:S(2)}, u32[]{:S(2)}) collective-permute-start(bf16[48,2048]{1,0:T(8,128)(2,1)S(1)} %get-tuple-element.142), channel_id=1, source_target_pairs={{0,8},{4,12},{8,0},{12,4},{16,24},{20,28},{24,16},{28,20},{1,9},{5... | collective-permute-start | bytes 589832 | tf_op jit(solution)/shard_map/ppermute | solution.py:22
  93.3 1.5 %collective-permute-start.30 = (bf16[48,2048]{1,0:T(8,128)(2,1)S(1)}, bf16[48,2048]{1,0:T(8,128)(2,1)S(1)}, u32[]{:S(2)}, u32[]{:S(2)}) collective-permute-start(bf16[48,2048]{1,0:T(8,128)(2,1)S(1)} %get-tuple-element.141), channel_id=1, source_target_pairs={{0,12},{4,8},{8,4},{12,0},{16,28},{20,24},{24,20},{28,16},{1,13},{... | collective-permute-start | bytes 589832 | tf_op jit(solution)/shard_map/ppermute | solution.py:22
  94.8 0.5 collective-permute-done.31.refs_6_
  95.3 1.8 %collective-permute-start.35 = (bf16[24,2048]{1,0:T(8,128)(2,1)S(1)}, bf16[24,2048]{1,0:T(8,128)(2,1)S(1)}, u32[]{:S(2)}, u32[]{:S(2)}) collective-permute-start(bf16[24,2048]{1,0:T(8,128)(2,1)S(1)} %get-tuple-element.148), channel_id=1, source_target_pairs={{0,24},{4,28},{8,16},{12,20},{16,8},{20,12},{24,0},{28,4},{1,25},{... | collective-permute-start | bytes 294920 | tf_op jit(solution)/shard_map/ppermute | solution.py:22
  97.1 2.4 %collective-permute-start.36 = (bf16[24,2048]{1,0:T(8,128)(2,1)S(1)}, bf16[24,2048]{1,0:T(8,128)(2,1)S(1)}, u32[]{:S(2)}, u32[]{:S(2)}) collective-permute-start(bf16[24,2048]{1,0:T(8,128)(2,1)S(1)} %get-tuple-element.147), channel_id=1, source_target_pairs={{0,28},{4,24},{8,20},{12,16},{16,12},{20,8},{24,4},{28,0},{1,29},{... | collective-permute-start | bytes 294920 | tf_op jit(solution)/shard_map/ppermute | solution.py:22
  99.6 8.2 %collective-permute-done.35.refs_8_ = bf16[24,2048]{1,0:T(8,128)(2,1)S(1)} collective-permute-done((bf16[24,2048]{1,0:T(8,128)(2,1)S(1)}, bf16[24,2048]{1,0:T(8,128)(2,1)S(1)}, u32[]{:S(2)}, u32[]{:S(2)}) %collective-permute-start.35) | collective-permute-done | bytes 98336 | tf_op jit(solution)/shard_map/ppermute | solution.py:22
  107.8 0.6 collective-permute-done.36.refs_9_
  108.4 1.2 collective-permute-done.30.refs_5_
  109.5 0.7 shard_map.146
  110.4 0.7 shard_map.145
  111.1 1.2 collective-permute-done.37
  112.4 1.0 collective-permute-start.38
  113.4 7.5 %collective-permute-done.38 = bf16[64,2048]{1,0:T(8,128)(2,1)S(1)} collective-permute-done((bf16[64,2048]{1,0:T(8,128)(2,1)S(1)}, bf16[64,2048]{1,0:T(8,128)(2,1)S(1)}, u32[]{:S(2)}, u32[]{:S(2)}) %collective-permute-start.38) | collective-permute-done | bytes 262176 | tf_op jit(solution)/shard_map/ppermute | solution.py:22
  120.8 0.8 add_convert_fusion.4
  (94 shorter events, 4.9 us)
Async XLA Ops:
  0.0 11.2 %collective-permute-start = (bf16[32,4608]{1,0:T(8,128)(2,1)}, bf16[32,4608]{1,0:T(8,128)(2,1)S(1)}, u32[]{:S(2)}, u32[]{:S(2)}) collective-permute-start(bf16[32,4608]{1,0:T(8,128)(2,1)} %refs_2_.1), channel_id=1, source_target_pairs={{0,2},{1,3},{2,0},{3,1},{4,6},{5,7},{6,4},{7,5},{8,10},{9,11},{10,... | collective-permute-start | bytes 884744 | tf_op jit(solution)/shard_map/ppermute | solution.py:22
  3.0 8.2 %collective-permute-start.1 = (bf16[32,4608]{1,0:T(8,128)(2,1)}, bf16[32,4608]{1,0:T(8,128)(2,1)S(1)}, u32[]{:S(2)}, u32[]{:S(2)}) collective-permute-start(bf16[32,4608]{1,0:T(8,128)(2,1)} %refs_2_.1), channel_id=1, source_target_pairs={{0,1},{1,0},{2,3},{3,2},{4,5},{5,4},{6,7},{7,6},{8,9},{9,8},{10,11... | collective-permute-start | bytes 884744 | tf_op jit(solution)/shard_map/ppermute | solution.py:22
  3.7 7.5 %collective-permute-start.3 = (s32[64,4]{0,1:T(4,128)S(1)}, s32[64,4]{0,1:T(4,128)S(1)}, u32[]{:S(2)}, u32[]{:S(2)}) collective-permute-start(s32[64,4]{0,1:T(4,128)S(1)} %pad_add_fusion.1), channel_id=1, source_target_pairs={{0,2},{1,3},{2,0},{3,1},{4,6},{5,7},{6,4},{7,5},{8,10},{9,11},{10,... | collective-permute-start | bytes 3080 | tf_op jit(solution)/shard_map/ppermute | solution.py:22
  3.7 7.5 %collective-permute-start.2 = (s32[32]{0:T(128)}, s32[32]{0:T(128)S(1)}, u32[]{:S(2)}, u32[]{:S(2)}) collective-permute-start(s32[32]{0:T(128)} %param.16), channel_id=1, source_target_pairs={{0,2},{1,3},{2,0},{3,1},{4,6},{5,7},{6,4},{7,5},{8,10},{9,11},{10,... | collective-permute-start | bytes 392 | tf_op jit(solution)/shard_map/ppermute | solution.py:22
  5.7 2.3 %copy-start.3 = (bf16[4608,512]{1,0:T(8,128)(2,1)S(1)}, bf16[4608,512]{1,0:T(8,128)(2,1)}, u32[]{:S(2)}) copy-start(bf16[4608,512]{1,0:T(8,128)(2,1)} %refs_0_.1) | copy-start | bytes 14155780
  8.0 1.6 %copy-start.7 = (bf16[512,2048]{1,0:T(8,128)(2,1)S(1)}, bf16[512,2048]{1,0:T(8,128)(2,1)}, u32[]{:S(2)}) copy-start(bf16[512,2048]{1,0:T(8,128)(2,1)} %refs_1_.1) | copy-start | bytes 6291460
  9.6 1.0 copy-start.8
  11.2 1.6 %collective-permute-start.4 = (bf16[32,4608]{1,0:T(8,128)(2,1)S(1)}, bf16[32,4608]{1,0:T(8,128)(2,1)S(1)}, u32[]{:S(2)}, u32[]{:S(2)}) collective-permute-start(bf16[32,4608]{1,0:T(8,128)(2,1)S(1)} %collective-permute-done.refs_1_), channel_id=1, source_target_pairs={{0,1},{1,0},{2,3},{3,2},{4,5},{5,4},{6,7},{7,6},{8,9},{9,8},{10,11... | collective-permute-start | bytes 884744 | tf_op jit(solution)/shard_map/ppermute | solution.py:22
  12.8 2.1 %copy-start.11 = (s32[32]{0:T(128)S(1)}, s32[32]{0:T(128)}, u32[]{:S(2)}) copy-start(s32[32]{0:T(128)} %param.16) | copy-start | bytes 388
  12.8 26.8 %copy-start.10 = (f32[2048]{0:T(1024)S(1)}, f32[2048]{0:T(1024)}, u32[]{:S(2)}) copy-start(f32[2048]{0:T(1024)} %param.19) | copy-start | bytes 24580
  14.8 36.2 %copy-start.4 = (bf16[2048,704]{0,1:T(8,128)(2,1)S(1)}, bf16[2048,704]{0,1:T(8,128)(2,1)}, u32[]{:S(2)}) copy-start(bf16[2048,704]{0,1:T(8,128)(2,1)} %param.20) | copy-start | bytes 8650756
  14.8 1.7 %collective-permute-start.5 = (bf16[64,2048]{1,0:T(8,128)(2,1)}, bf16[64,2048]{1,0:T(8,128)(2,1)S(1)}, u32[]{:S(2)}, u32[]{:S(2)}) collective-permute-start(bf16[64,2048]{1,0:T(8,128)(2,1)} %get-tuple-element.86), channel_id=1, source_target_pairs={{0,1},{1,0},{2,3},{3,2},{4,5},{5,4},{6,7},{7,6},{8,9},{9,8},{10,11... | collective-permute-start | bytes 786440 | tf_op jit(solution)/shard_map/ppermute | solution.py:22
  17.5 15.3 %all-to-all-start = ((bf16[8,8,2176]{2,1,0:T(8,128)(2,1)}), bf16[8,8,2176]{2,1,0:T(8,128)(2,1)S(1)}, u32[]{:S(2)}, u32[]{:S(2)}) async-start(bf16[8,8,2176]{2,1,0:T(8,128)(2,1)} %shard_map.138), calls=%async_computation | async-start | bytes 557056 | tf_op jit(solution)/shard_map/all_to_all | solution.py:389
  23.3 8.3 %collective-permute-start.6 = (bf16[64,2048]{1,0:T(8,128)(2,1)}, bf16[64,2048]{1,0:T(8,128)(2,1)S(1)}, u32[]{:S(2)}, u32[]{:S(2)}) collective-permute-start(bf16[64,2048]{1,0:T(8,128)(2,1)} %refs_2_.2), channel_id=1, source_target_pairs={{0,2},{1,3},{2,0},{3,1},{4,6},{5,7},{6,4},{7,5},{8,10},{9,11},{10,... | collective-permute-start | bytes 786440 | tf_op jit(solution)/shard_map/ppermute | solution.py:22
  24.2 1.2 collective-permute-start.7
  24.2 1.3 %collective-permute-start.8 = (s32[64,4]{0,1:T(4,128)S(1)}, s32[64,4]{0,1:T(4,128)S(1)}, u32[]{:S(2)}, u32[]{:S(2)}) collective-permute-start(s32[64,4]{0,1:T(4,128)S(1)} %collective-permute-done.3), channel_id=1, source_target_pairs={{0,1},{1,0},{2,3},{3,2},{4,5},{5,4},{6,7},{7,6},{8,9},{9,8},{10,11... | collective-permute-start | bytes 3080 | tf_op jit(solution)/shard_map/ppermute | solution.py:22
  32.8 6.8 %collective-permute-start.9 = (bf16[8,8,2176]{2,1,0:T(8,128)(2,1)S(1)}, bf16[8,8,2176]{2,1,0:T(8,128)(2,1)S(1)}, u32[]{:S(2)}, u32[]{:S(2)}) collective-permute-start(bf16[8,8,2176]{2,1,0:T(8,128)(2,1)S(1)} %all-to-all-done.refs_0_), channel_id=1, source_target_pairs={{0,2},{1,3},{2,0},{3,1},{4,6},{5,7},{6,4},{7,5},{8,10},{9,11},{10,... | collective-permute-start | bytes 835592 | tf_op jit(solution)/shard_map/ppermute | solution.py:22
  39.6 1.0 copy-start.9
  41.3 2.0 %collective-permute-start.10 = (bf16[128,2048]{1,0:T(8,128)(2,1)S(1)}, bf16[128,2048]{1,0:T(8,128)(2,1)S(1)}, u32[]{:S(2)}, u32[]{:S(2)}) collective-permute-start(bf16[128,2048]{1,0:T(8,128)(2,1)S(1)} %get-tuple-element.101.refs_1_.refs_0_), channel_id=1, source_target_pairs={{0,1},{1,0},{2,3},{3,2},{4,5},{5,4},{6,7},{7,6},{8,9},{9,8},{10,11... | collective-permute-start | bytes 1572872 | tf_op jit(solution)/shard_map/ppermute | solution.py:22
  43.8 13.4 %collective-permute-start.12 = (bf16[24,2048]{1,0:T(8,128)(2,1)S(1)}, bf16[24,2048]{1,0:T(8,128)(2,1)S(1)}, u32[]{:S(2)}, u32[]{:S(2)}) collective-permute-start(bf16[24,2048]{1,0:T(8,128)(2,1)S(1)} %get-tuple-element.103), channel_id=1, source_target_pairs={{0,20},{4,16},{8,28},{12,24},{16,4},{20,0},{24,12},{28,8},{1,21},{... | collective-permute-start | bytes 294920 | tf_op jit(solution)/shard_map/ppermute | solution.py:22
  46.6 10.6 %collective-permute-start.11 = (bf16[24,2048]{1,0:T(8,128)(2,1)S(1)}, bf16[24,2048]{1,0:T(8,128)(2,1)S(1)}, u32[]{:S(2)}, u32[]{:S(2)}) collective-permute-start(bf16[24,2048]{1,0:T(8,128)(2,1)S(1)} %get-tuple-element.102), channel_id=1, source_target_pairs={{0,16},{4,20},{8,24},{12,28},{16,0},{20,4},{24,8},{28,12},{1,17},{... | collective-permute-start | bytes 294920 | tf_op jit(solution)/shard_map/ppermute | solution.py:22
  47.4 13.8 %collective-permute-start.14 = (bf16[48,2048]{1,0:T(8,128)(2,1)S(1)}, bf16[48,2048]{1,0:T(8,128)(2,1)S(1)}, u32[]{:S(2)}, u32[]{:S(2)}) collective-permute-start(bf16[48,2048]{1,0:T(8,128)(2,1)S(1)} %get-tuple-element.107), channel_id=1, source_target_pairs={{0,4},{4,0},{8,12},{12,8},{16,20},{20,16},{24,28},{28,24},{1,5},{5... | collective-permute-start | bytes 589832 | tf_op jit(solution)/shard_map/ppermute | solution.py:22
  48.3 14.0 %collective-permute-start.15 = (bf16[48,2048]{1,0:T(8,128)(2,1)S(1)}, bf16[48,2048]{1,0:T(8,128)(2,1)S(1)}, u32[]{:S(2)}, u32[]{:S(2)}) collective-permute-start(bf16[48,2048]{1,0:T(8,128)(2,1)S(1)} %get-tuple-element.108), channel_id=1, source_target_pairs={{0,8},{4,12},{8,0},{12,4},{16,24},{20,28},{24,16},{28,20},{1,9},{5... | collective-permute-start | bytes 589832 | tf_op jit(solution)/shard_map/ppermute | solution.py:22
  49.2 15.9 %collective-permute-start.16 = (bf16[48,2048]{1,0:T(8,128)(2,1)S(1)}, bf16[48,2048]{1,0:T(8,128)(2,1)S(1)}, u32[]{:S(2)}, u32[]{:S(2)}) collective-permute-start(bf16[48,2048]{1,0:T(8,128)(2,1)S(1)} %get-tuple-element.109), channel_id=1, source_target_pairs={{0,12},{4,8},{8,4},{12,0},{16,28},{20,24},{24,20},{28,16},{1,13},{... | collective-permute-start | bytes 589832 | tf_op jit(solution)/shard_map/ppermute | solution.py:22
  50.9 1.8 %copy-start.5 = (bf16[2048,704]{0,1:T(8,128)(2,1)S(1)}, bf16[2048,704]{0,1:T(8,128)(2,1)}, u32[]{:S(2)}) copy-start(bf16[2048,704]{0,1:T(8,128)(2,1)} %param.21) | copy-start | bytes 8650756
  52.7 1.8 %copy-start.6 = (bf16[704,2048]{1,0:T(8,128)(2,1)S(1)}, bf16[704,2048]{1,0:T(8,128)(2,1)}, u32[]{:S(2)}) copy-start(bf16[704,2048]{1,0:T(8,128)(2,1)} %refs_4_.1) | copy-start | bytes 8650756
  54.6 17.0 %copy-start.1 = (bf16[1,2048,352]{1,2,0:T(8,128)(2,1)S(1)}, bf16[1,2048,352]{1,2,0:T(8,128)(2,1)}, u32[]{:S(2)}) copy-start(bf16[1,2048,352]{1,2,0:T(8,128)(2,1)} %param.24) | copy-start | bytes 4325380
  54.6 17.0 %copy-start.2 = (bf16[1,352,2048]{2,1,0:T(8,128)(2,1)S(1)}, bf16[1,352,2048]{2,1,0:T(8,128)(2,1)}, u32[]{:S(2)}) copy-start(bf16[1,352,2048]{2,1,0:T(8,128)(2,1)} %param.25) | copy-start | bytes 4325380
  57.2 14.4 %copy-start = (bf16[1,2048,352]{1,2,0:T(8,128)(2,1)S(1)}, bf16[1,2048,352]{1,2,0:T(8,128)(2,1)}, u32[]{:S(2)}) copy-start(bf16[1,2048,352]{1,2,0:T(8,128)(2,1)} %param.23) | copy-start | bytes 4325380
  57.3 11.3 %collective-permute-start.13 = (bf16[48,2048]{1,0:T(8,128)(2,1)S(1)}, bf16[48,2048]{1,0:T(8,128)(2,1)S(1)}, u32[]{:S(2)}, u32[]{:S(2)}) collective-permute-start(bf16[48,2048]{1,0:T(8,128)(2,1)S(1)} %pad_maximum_fusion.1.refs_0_), channel_id=1, source_target_pairs={{0,2},{1,3},{2,0},{3,1},{4,6},{5,7},{6,4},{7,5},{8,10},{9,11},{10,... | collective-permute-start | bytes 589832 | tf_op jit(solution)/shard_map/ppermute | solution.py:22
  58.2 6.9 %collective-permute-start.17 = (bf16[24,2048]{1,0:T(8,128)(2,1)S(1)}, bf16[24,2048]{1,0:T(8,128)(2,1)S(1)}, u32[]{:S(2)}, u32[]{:S(2)}) collective-permute-start(bf16[24,2048]{1,0:T(8,128)(2,1)S(1)} %get-tuple-element.114), channel_id=1, source_target_pairs={{0,24},{4,28},{8,16},{12,20},{16,8},{20,12},{24,0},{28,4},{1,25},{... | collective-permute-start | bytes 294920 | tf_op jit(solution)/shard_map/ppermute | solution.py:22
  61.2 7.4 %collective-permute-start.18 = (bf16[24,2048]{1,0:T(8,128)(2,1)S(1)}, bf16[24,2048]{1,0:T(8,128)(2,1)S(1)}, u32[]{:S(2)}, u32[]{:S(2)}) collective-permute-start(bf16[24,2048]{1,0:T(8,128)(2,1)S(1)} %get-tuple-element.115), channel_id=1, source_target_pairs={{0,28},{4,24},{8,20},{12,16},{16,12},{20,8},{24,4},{28,0},{1,29},{... | collective-permute-start | bytes 294920 | tf_op jit(solution)/shard_map/ppermute | solution.py:22
  68.6 5.7 %collective-permute-start.19 = (bf16[48,2048]{1,0:T(8,128)(2,1)S(1)}, bf16[48,2048]{1,0:T(8,128)(2,1)S(1)}, u32[]{:S(2)}, u32[]{:S(2)}) collective-permute-start(bf16[48,2048]{1,0:T(8,128)(2,1)S(1)} %constant_dynamic-update-slice_fusion.refs_0_), channel_id=1, source_target_pairs={{0,2},{1,3},{2,0},{3,1},{4,6},{5,7},{6,4},{7,5},{8,10},{9,11},{10,... | collective-permute-start | bytes 589832 | tf_op jit(solution)/shard_map/ppermute | solution.py:22
  69.8 1.4 %collective-permute-start.20 = (bf16[48,2048]{1,0:T(8,128)(2,1)S(1)}, bf16[48,2048]{1,0:T(8,128)(2,1)S(1)}, u32[]{:S(2)}, u32[]{:S(2)}) collective-permute-start(bf16[48,2048]{1,0:T(8,128)(2,1)S(1)} %pad_maximum_fusion.1.refs_0_), channel_id=1, source_target_pairs={{0,1},{1,0},{2,3},{3,2},{4,5},{5,4},{6,7},{7,6},{8,9},{9,8},{10,11... | collective-permute-start | bytes 589832 | tf_op jit(solution)/shard_map/ppermute | solution.py:22
  69.8 1.7 %collective-permute-start.21 = (bf16[48,2048]{1,0:T(8,128)(2,1)S(1)}, bf16[48,2048]{1,0:T(8,128)(2,1)S(1)}, u32[]{:S(2)}, u32[]{:S(2)}) collective-permute-start(bf16[48,2048]{1,0:T(8,128)(2,1)S(1)} %collective-permute-done.13.refs_1_), channel_id=1, source_target_pairs={{0,1},{1,0},{2,3},{3,2},{4,5},{5,4},{6,7},{7,6},{8,9},{9,8},{10,11... | collective-permute-start | bytes 589832 | tf_op jit(solution)/shard_map/ppermute | solution.py:22
  74.4 1.7 %collective-permute-start.22 = (bf16[96,2048]{1,0:T(8,128)(2,1)S(1)}, bf16[96,2048]{1,0:T(8,128)(2,1)S(1)}, u32[]{:S(2)}, u32[]{:S(2)}) collective-permute-start(bf16[96,2048]{1,0:T(8,128)(2,1)S(1)} %get-tuple-element.123), channel_id=1, source_target_pairs={{0,1},{1,0},{2,3},{3,2},{4,5},{5,4},{6,7},{7,6},{8,9},{9,8},{10,11... | collective-permute-start | bytes 1179656 | tf_op jit(solution)/shard_map/ppermute | solution.py:22
  74.4 5.3 %collective-permute-start.24 = (bf16[192,2048]{1,0:T(8,128)(2,1)S(1)}, bf16[192,2048]{1,0:T(8,128)(2,1)S(1)}, u32[]{:S(2)}, u32[]{:S(2)}) collective-permute-start(bf16[192,2048]{1,0:T(8,128)(2,1)S(1)} %constant_dynamic-update-slice_fusion.2.refs_0_), channel_id=1, source_target_pairs={{0,1},{1,0},{2,3},{3,2},{4,5},{5,4},{6,7},{7,6},{8,9},{9,8},{10,11... | collective-permute-start | bytes 2359304 | tf_op jit(solution)/shard_map/ppermute | solution.py:22
  75.2 2.3 %collective-permute-start.25 = (bf16[48,2048]{1,0:T(8,128)(2,1)S(1)}, bf16[48,2048]{1,0:T(8,128)(2,1)S(1)}, u32[]{:S(2)}, u32[]{:S(2)}) collective-permute-start(bf16[48,2048]{1,0:T(8,128)(2,1)S(1)} %constant_dynamic-update-slice_fusion.refs_0_), channel_id=1, source_target_pairs={{0,1},{1,0},{2,3},{3,2},{4,5},{5,4},{6,7},{7,6},{8,9},{9,8},{10,11... | collective-permute-start | bytes 589832 | tf_op jit(solution)/shard_map/ppermute | solution.py:22
  75.3 2.5 %collective-permute-start.26 = (bf16[48,2048]{1,0:T(8,128)(2,1)S(1)}, bf16[48,2048]{1,0:T(8,128)(2,1)S(1)}, u32[]{:S(2)}, u32[]{:S(2)}) collective-permute-start(bf16[48,2048]{1,0:T(8,128)(2,1)S(1)} %collective-permute-done.19.refs_1_), channel_id=1, source_target_pairs={{0,1},{1,0},{2,3},{3,2},{4,5},{5,4},{6,7},{7,6},{8,9},{9,8},{10,11... | collective-permute-start | bytes 589832 | tf_op jit(solution)/shard_map/ppermute | solution.py:22
  76.2 7.0 %collective-permute-start.23 = (bf16[48,2048]{1,0:T(8,128)(2,1)S(1)}, bf16[48,2048]{1,0:T(8,128)(2,1)S(1)}, u32[]{:S(2)}, u32[]{:S(2)}) collective-permute-start(bf16[48,2048]{1,0:T(8,128)(2,1)S(1)} %slice.97), channel_id=1, source_target_pairs={{0,2},{1,3},{2,0},{3,1},{4,6},{5,7},{6,4},{7,5},{8,10},{9,11},{10,... | collective-permute-start | bytes 589832 | tf_op jit(solution)/shard_map/ppermute | solution.py:22
  79.4 3.9 %collective-permute-start.33 = (bf16[96,2048]{1,0:T(8,128)(2,1)S(1)}, bf16[96,2048]{1,0:T(8,128)(2,1)S(1)}, u32[]{:S(2)}, u32[]{:S(2)}) collective-permute-start(bf16[96,2048]{1,0:T(8,128)(2,1)S(1)} %get-tuple-element.139), channel_id=1, source_target_pairs={{0,1},{1,0},{2,3},{3,2},{4,5},{5,4},{6,7},{7,6},{8,9},{9,8},{10,11... | collective-permute-start | bytes 1179656 | tf_op jit(solution)/shard_map/ppermute | solution.py:22
  83.3 7.6 %collective-permute-start.27 = (bf16[192,2048]{1,0:T(8,128)(2,1)S(1)}, bf16[192,2048]{1,0:T(8,128)(2,1)S(1)}, u32[]{:S(2)}, u32[]{:S(2)}) collective-permute-start(bf16[192,2048]{1,0:T(8,128)(2,1)S(1)} %get-tuple-element.136), channel_id=1, source_target_pairs={{0,1},{1,0},{2,3},{3,2},{4,5},{5,4},{6,7},{7,6},{8,9},{9,8},{10,11... | collective-permute-start | bytes 2359304 | tf_op jit(solution)/shard_map/ppermute | solution.py:22
  83.5 7.4 %collective-permute-start.34 = (bf16[48,2048]{1,0:T(8,128)(2,1)S(1)}, bf16[48,2048]{1,0:T(8,128)(2,1)S(1)}, u32[]{:S(2)}, u32[]{:S(2)}) collective-permute-start(bf16[48,2048]{1,0:T(8,128)(2,1)S(1)} %slice.103), channel_id=1, source_target_pairs={{0,2},{1,3},{2,0},{3,1},{4,6},{5,7},{6,4},{7,5},{8,10},{9,11},{10,... | collective-permute-start | bytes 589832 | tf_op jit(solution)/shard_map/ppermute | solution.py:22
  84.7 10.6 %collective-permute-start.31 = (bf16[24,2048]{1,0:T(8,128)(2,1)S(1)}, bf16[24,2048]{1,0:T(8,128)(2,1)S(1)}, u32[]{:S(2)}, u32[]{:S(2)}) collective-permute-start(bf16[24,2048]{1,0:T(8,128)(2,1)S(1)} %get-tuple-element.150), channel_id=1, source_target_pairs={{0,16},{4,20},{8,24},{12,28},{16,0},{20,4},{24,8},{28,12},{1,17},{... | collective-permute-start | bytes 294920 | tf_op jit(solution)/shard_map/ppermute | solution.py:22
  86.1 11.0 %collective-permute-start.32 = (bf16[24,2048]{1,0:T(8,128)(2,1)S(1)}, bf16[24,2048]{1,0:T(8,128)(2,1)S(1)}, u32[]{:S(2)}, u32[]{:S(2)}) collective-permute-start(bf16[24,2048]{1,0:T(8,128)(2,1)S(1)} %get-tuple-element.149), channel_id=1, source_target_pairs={{0,20},{4,16},{8,28},{12,24},{16,4},{20,0},{24,12},{28,8},{1,21},{... | collective-permute-start | bytes 294920 | tf_op jit(solution)/shard_map/ppermute | solution.py:22
  91.3 17.1 %collective-permute-start.28 = (bf16[48,2048]{1,0:T(8,128)(2,1)S(1)}, bf16[48,2048]{1,0:T(8,128)(2,1)S(1)}, u32[]{:S(2)}, u32[]{:S(2)}) collective-permute-start(bf16[48,2048]{1,0:T(8,128)(2,1)S(1)} %get-tuple-element.143), channel_id=1, source_target_pairs={{0,4},{4,0},{8,12},{12,8},{16,20},{20,16},{24,28},{28,24},{1,5},{5... | collective-permute-start | bytes 589832 | tf_op jit(solution)/shard_map/ppermute | solution.py:22
  91.9 16.5 %collective-permute-start.29 = (bf16[48,2048]{1,0:T(8,128)(2,1)S(1)}, bf16[48,2048]{1,0:T(8,128)(2,1)S(1)}, u32[]{:S(2)}, u32[]{:S(2)}) collective-permute-start(bf16[48,2048]{1,0:T(8,128)(2,1)S(1)} %get-tuple-element.142), channel_id=1, source_target_pairs={{0,8},{4,12},{8,0},{12,4},{16,24},{20,28},{24,16},{28,20},{1,9},{5... | collective-permute-start | bytes 589832 | tf_op jit(solution)/shard_map/ppermute | solution.py:22
  93.3 16.2 %collective-permute-start.30 = (bf16[48,2048]{1,0:T(8,128)(2,1)S(1)}, bf16[48,2048]{1,0:T(8,128)(2,1)S(1)}, u32[]{:S(2)}, u32[]{:S(2)}) collective-permute-start(bf16[48,2048]{1,0:T(8,128)(2,1)S(1)} %get-tuple-element.141), channel_id=1, source_target_pairs={{0,12},{4,8},{8,4},{12,0},{16,28},{20,24},{24,20},{28,16},{1,13},{... | collective-permute-start | bytes 589832 | tf_op jit(solution)/shard_map/ppermute | solution.py:22
  95.3 12.5 %collective-permute-start.35 = (bf16[24,2048]{1,0:T(8,128)(2,1)S(1)}, bf16[24,2048]{1,0:T(8,128)(2,1)S(1)}, u32[]{:S(2)}, u32[]{:S(2)}) collective-permute-start(bf16[24,2048]{1,0:T(8,128)(2,1)S(1)} %get-tuple-element.148), channel_id=1, source_target_pairs={{0,24},{4,28},{8,16},{12,20},{16,8},{20,12},{24,0},{28,4},{1,25},{... | collective-permute-start | bytes 294920 | tf_op jit(solution)/shard_map/ppermute | solution.py:22
  97.1 11.2 %collective-permute-start.36 = (bf16[24,2048]{1,0:T(8,128)(2,1)S(1)}, bf16[24,2048]{1,0:T(8,128)(2,1)S(1)}, u32[]{:S(2)}, u32[]{:S(2)}) collective-permute-start(bf16[24,2048]{1,0:T(8,128)(2,1)S(1)} %get-tuple-element.147), channel_id=1, source_target_pairs={{0,28},{4,24},{8,20},{12,16},{16,12},{20,8},{24,4},{28,0},{1,29},{... | collective-permute-start | bytes 294920 | tf_op jit(solution)/shard_map/ppermute | solution.py:22
  110.3 2.0 %collective-permute-start.37 = (bf16[128,2048]{1,0:T(8,128)(2,1)S(1)}, bf16[128,2048]{1,0:T(8,128)(2,1)S(1)}, u32[]{:S(2)}, u32[]{:S(2)}) collective-permute-start(bf16[128,2048]{1,0:T(8,128)(2,1)S(1)} %shard_map.146), channel_id=1, source_target_pairs={{0,1},{1,0},{2,3},{3,2},{4,5},{5,4},{6,7},{7,6},{8,9},{9,8},{10,11... | collective-permute-start | bytes 1572872 | tf_op jit(solution)/shard_map/ppermute | solution.py:22
  112.4 8.4 %collective-permute-start.38 = (bf16[64,2048]{1,0:T(8,128)(2,1)S(1)}, bf16[64,2048]{1,0:T(8,128)(2,1)S(1)}, u32[]{:S(2)}, u32[]{:S(2)}) collective-permute-start(bf16[64,2048]{1,0:T(8,128)(2,1)S(1)} %slice.107), channel_id=1, source_target_pairs={{0,2},{1,3},{2,0},{3,1},{4,6},{5,7},{6,4},{7,5},{8,10},{9,11},{10,... | collective-permute-start | bytes 786440 | tf_op jit(solution)/shard_map/ppermute | solution.py:22

commit v5 on v4

--- a/solution.py
+++ b/solution.py
@@ -440,8 +440,7 @@
 
     for m in (*near[1:], *far_one):
         got[m] = swap(send[m], "dp", m)
-    shared = shared_rows(normed, shared_gate.T, shared_up.T, shared_down)
-    one, shared, send = fence(join(far_one), shared, send)
+    one, send = fence(join(far_one), send)
 
     for m in far_two:
         got[m] = swap(send[m], "dp", m)
@@ -456,12 +455,13 @@
     mine, two_keep = fence(mine, two_keep)
     keep, give = expert_rows(mine, *experts)
     one = sum_rest(add(one_keep, swap(one_give, "expert", 1)))
-    one, keep, give = fence(one, keep, give)
+    one, keep, give, normed = fence(one, keep, give, normed)
     two = sum_rest(add(two_keep, swap(two_give, "expert", 1)))
     rows = add(keep, swap(give, "expert", 1))
     back = [send_back(m, rows, m) for m in near]
     back += [send_back(m, one, i) for i, m in enumerate(far_one)]
     back += [send_back(m, two, i) for i, m in enumerate(far_two)]
+    shared = shared_rows(normed, shared_gate.T, shared_up.T, shared_down)
 
     middle = group_rows // 2
     keep, give = [

time: 122 us -> 119 us (0.975)
  waiting for transfers between devices: 50.2 us -> 54.9 us
  local copies, waits for them, and re-layouts: 9.87 us -> 5.3 us
  starting transfers between devices: 42.8 us -> 40.8 us
    unnamed x28, local copies, waits for them, and re-layouts: 9.54 us -> 4.98 us
    ppermute x39, waiting for transfers between devices: 49 us -> 53.5 us  [swap(): return lax.ppermute(rows, axis, [(i, i ^ mask) for i in range(count)])]
    ppermute x39, starting transfers between devices: 37 us -> 35 us  [swap(): return lax.ppermute(rows, axis, [(i, i ^ mask) for i in range(count)])]
  transfers between devices with their start and end apart: 40 -> 40, of which waited for: 24 -> 26; matrix products, arithmetic and copies ran while one was open for 2% -> 2% of each run, Pallas kernels for 9% -> 9%
where the time goes in v5:
time: 119 us
  waiting for transfers between devices  54.9 us (46%)
  starting transfers between devices  40.8 us (34%)
  Pallas kernels  14.4 us (12%)
  local copies, waits for them, and re-layouts  5.3 us (4%)
  other arithmetic  2.95 us (2%)
    ppermute x39, waiting for transfers between devices, swap(): return lax.ppermute(rows, axis, [(i, i ^ mask) for i in range(count)])  53.5 us
    ppermute x39, starting transfers between devices, swap(): return lax.ppermute(rows, axis, [(i, i ^ mask) for i in range(count)])  35 us
    pallas_call x10, Pallas kernels, local_kernel(): pl.pallas_call(body, out_shape=list(outs), in_specs=[pl.BlockSpec(memory_...  13.9 us
    all_to_all x1, starting transfers between devices, shards(): lax.all_to_all(leaving, 'dp', split_axis=0, concat_axis=0, tiled=True)  5.82 us
    unnamed x28, local copies, waits for them, and re-layouts  4.98 us
  transfers between devices with their start and end apart: 40, of which 26 were waited for; matrix products, arithmetic and copies ran while one was open for 2% of the time, Pallas kernels for 9%

profile of v5, /device:TPU:0, one launch (start us, length us, event | category | flops | bytes accessed | tf_op | source)
XLA Modules:
  0.0 119.1 jit_solution(13840452477379152534)
XLA Ops:
  0.0 3.0 %collective-permute-start = (bf16[32,4608]{1,0:T(8,128)(2,1)}, bf16[32,4608]{1,0:T(8,128)(2,1)S(1)}, u32[]{:S(2)}, u32[]{:S(2)}) collective-permute-start(bf16[32,4608]{1,0:T(8,128)(2,1)} %refs_2_.1), channel_id=1, source_target_pairs={{0,2},{1,3},{2,0},{3,1},{4,6},{5,7},{6,4},{7,5},{8,10},{9,11},{10,... | collective-permute-start | bytes 884744 | tf_op jit(solution)/shard_map/ppermute | solution.py:22
  3.0 0.7 pad_add_fusion.1
  3.7 2.0 %collective-permute-start.2 = (s32[32]{0:T(128)}, s32[32]{0:T(128)S(1)}, u32[]{:S(2)}, u32[]{:S(2)}) collective-permute-start(s32[32]{0:T(128)} %param.16), channel_id=1, source_target_pairs={{0,2},{1,3},{2,0},{3,1},{4,6},{5,7},{6,4},{7,5},{8,10},{9,11},{10,... | collective-permute-start | bytes 392 | tf_op jit(solution)/shard_map/ppermute | solution.py:22
  5.7 2.3 %copy-done.3 = bf16[4608,512]{1,0:T(8,128)(2,1)S(1)} copy-done((bf16[4608,512]{1,0:T(8,128)(2,1)S(1)}, bf16[4608,512]{1,0:T(8,128)(2,1)}, u32[]{:S(2)}) %copy-start.3) | copy-done | bytes 4718616
  8.0 1.6 %copy-done.7 = bf16[512,2048]{1,0:T(8,128)(2,1)S(1)} copy-done((bf16[512,2048]{1,0:T(8,128)(2,1)S(1)}, bf16[512,2048]{1,0:T(8,128)(2,1)}, u32[]{:S(2)}) %copy-start.7) | copy-done | bytes 2097176
  9.6 1.0 copy-done.8
  10.6 0.5 shard_map.136
  11.3 1.6 %collective-permute-done.4.refs_3_ = bf16[32,4608]{1,0:T(8,128)(2,1)S(1)} collective-permute-done((bf16[32,4608]{1,0:T(8,128)(2,1)S(1)}, bf16[32,4608]{1,0:T(8,128)(2,1)S(1)}, u32[]{:S(2)}, u32[]{:S(2)}) %collective-permute-start.4) | collective-permute-done | bytes 294944 | tf_op jit(solution)/shard_map/ppermute | solution.py:22
  12.8 1.2 %shard_map.137 = (bf16[64,2048]{1,0:T(8,128)(2,1)S(1)}, bf16[64,2048]{1,0:T(8,128)(2,1)S(1)}) custom-call(bf16[32,4608]{1,0:T(8,128)(2,1)S(1)} %get-tuple-element.78.refs_0_, bf16[32,4608]{1,0:T(8,128)(2,1)S(1)} %collective-permute-done.refs_1_, bf16[32,4608]{1,0:T(8,128)(2,1)S(1)} %collective-permute-done.1.refs_2_, ...), custom_call_target="tpu_custom_call" | custom-call | flops 872415232 | bytes 8519680 | tf_op jit(solution)/shard_map/pallas_call | solution.py:68
  14.6 1.1 collective-permute-done.5.other_ref
  15.7 0.9 shard_map.138
  16.7 5.8 %all-to-all-start = ((bf16[8,8,2176]{2,1,0:T(8,128)(2,1)}), bf16[8,8,2176]{2,1,0:T(8,128)(2,1)S(1)}, u32[]{:S(2)}, u32[]{:S(2)}) async-start(bf16[8,8,2176]{2,1,0:T(8,128)(2,1)} %shard_map.138), calls=%async_computation | async-start | bytes 557056 | tf_op jit(solution)/shard_map/all_to_all | solution.py:389
  22.5 0.9 collective-permute-start.6
  23.4 0.5 collective-permute-start.8
  23.9 0.6 collective-permute-done.7
  24.8 5.8 %collective-permute-done.6.refs_3_ = bf16[64,2048]{1,0:T(8,128)(2,1)S(1)} collective-permute-done((bf16[64,2048]{1,0:T(8,128)(2,1)S(1)}, bf16[64,2048]{1,0:T(8,128)(2,1)S(1)}, u32[]{:S(2)}, u32[]{:S(2)}) %collective-permute-start.6) | collective-permute-done | bytes 262176 | tf_op jit(solution)/shard_map/ppermute | solution.py:22
  30.6 1.4 %all-to-all-done.refs_0_ = bf16[8,8,2176]{2,1,0:T(8,128)(2,1)S(1)} async-done(((bf16[8,8,2176]{2,1,0:T(8,128)(2,1)}), bf16[8,8,2176]{2,1,0:T(8,128)(2,1)S(1)}, u32[]{:S(2)}, u32[]{:S(2)}) %all-to-all-start) | async-done | bytes 278560 | tf_op jit(solution)/shard_map/all_to_all | solution.py:389
  32.0 0.9 collective-permute-start.9
  33.3 5.5 %collective-permute-done.9.refs_1_ = bf16[8,8,2176]{2,1,0:T(8,128)(2,1)S(1)} collective-permute-done((bf16[8,8,2176]{2,1,0:T(8,128)(2,1)S(1)}, bf16[8,8,2176]{2,1,0:T(8,128)(2,1)S(1)}, u32[]{:S(2)}, u32[]{:S(2)}) %collective-permute-start.9) | collective-permute-done | bytes 278560 | tf_op jit(solution)/shard_map/ppermute | solution.py:22
  38.8 0.7 shard_map.139
  39.7 1.8 %collective-permute-done.10.refs_2_.refs_1_ = bf16[128,2048]{1,0:T(8,128)(2,1)S(1)} collective-permute-done((bf16[128,2048]{1,0:T(8,128)(2,1)S(1)}, bf16[128,2048]{1,0:T(8,128)(2,1)S(1)}, u32[]{:S(2)}, u32[]{:S(2)}) %collective-permute-start.10) | collective-permute-done | bytes 524320 | tf_op jit(solution)/shard_map/ppermute | solution.py:22
  41.5 0.5 shard_map.140
  42.0 2.6 %collective-permute-start.12 = (bf16[24,2048]{1,0:T(8,128)(2,1)S(1)}, bf16[24,2048]{1,0:T(8,128)(2,1)S(1)}, u32[]{:S(2)}, u32[]{:S(2)}) collective-permute-start(bf16[24,2048]{1,0:T(8,128)(2,1)S(1)} %get-tuple-element.103), channel_id=1, source_target_pairs={{0,20},{4,16},{8,28},{12,24},{16,4},{20,0},{24,12},{28,8},{1,21},{... | collective-permute-start | bytes 294920 | tf_op jit(solution)/shard_map/ppermute | solution.py:22
  44.6 1.1 collective-permute-start.11
  45.7 0.8 collective-permute-start.14
  46.5 0.8 collective-permute-start.15
  47.3 1.8 %collective-permute-start.16 = (bf16[48,2048]{1,0:T(8,128)(2,1)S(1)}, bf16[48,2048]{1,0:T(8,128)(2,1)S(1)}, u32[]{:S(2)}, u32[]{:S(2)}) collective-permute-start(bf16[48,2048]{1,0:T(8,128)(2,1)S(1)} %get-tuple-element.107), channel_id=1, source_target_pairs={{0,12},{4,8},{8,4},{12,0},{16,28},{20,24},{24,20},{28,16},{1,13},{... | collective-permute-start | bytes 589832 | tf_op jit(solution)/shard_map/ppermute | solution.py:22
  49.2 4.2 %collective-permute-done.12 = bf16[24,2048]{1,0:T(8,128)(2,1)S(1)} collective-permute-done((bf16[24,2048]{1,0:T(8,128)(2,1)S(1)}, bf16[24,2048]{1,0:T(8,128)(2,1)S(1)}, u32[]{:S(2)}, u32[]{:S(2)}) %collective-permute-start.12) | collective-permute-done | bytes 98336 | tf_op jit(solution)/shard_map/ppermute | solution.py:22
  53.4 1.4 %collective-permute-done.11 = bf16[24,2048]{1,0:T(8,128)(2,1)S(1)} collective-permute-done((bf16[24,2048]{1,0:T(8,128)(2,1)S(1)}, bf16[24,2048]{1,0:T(8,128)(2,1)S(1)}, u32[]{:S(2)}, u32[]{:S(2)}) %collective-permute-start.11) | collective-permute-done | bytes 98336 | tf_op jit(solution)/shard_map/ppermute | solution.py:22
  54.8 0.9 collective-permute-start.13
  55.8 2.9 %collective-permute-start.17 = (bf16[24,2048]{1,0:T(8,128)(2,1)S(1)}, bf16[24,2048]{1,0:T(8,128)(2,1)S(1)}, u32[]{:S(2)}, u32[]{:S(2)}) collective-permute-start(bf16[24,2048]{1,0:T(8,128)(2,1)S(1)} %get-tuple-element.111), channel_id=1, source_target_pairs={{0,24},{4,28},{8,16},{12,20},{16,8},{20,12},{24,0},{28,4},{1,25},{... | collective-permute-start | bytes 294920 | tf_op jit(solution)/shard_map/ppermute | solution.py:22
  58.6 1.3 %collective-permute-start.18 = (bf16[24,2048]{1,0:T(8,128)(2,1)S(1)}, bf16[24,2048]{1,0:T(8,128)(2,1)S(1)}, u32[]{:S(2)}, u32[]{:S(2)}) collective-permute-start(bf16[24,2048]{1,0:T(8,128)(2,1)S(1)} %get-tuple-element.112), channel_id=1, source_target_pairs={{0,28},{4,24},{8,20},{12,16},{16,12},{20,8},{24,4},{28,0},{1,29},{... | collective-permute-start | bytes 294920 | tf_op jit(solution)/shard_map/ppermute | solution.py:22
  60.0 3.5 %collective-permute-done.16 = bf16[48,2048]{1,0:T(8,128)(2,1)S(1)} collective-permute-done((bf16[48,2048]{1,0:T(8,128)(2,1)S(1)}, bf16[48,2048]{1,0:T(8,128)(2,1)S(1)}, u32[]{:S(2)}, u32[]{:S(2)}) %collective-permute-start.16) | collective-permute-done | bytes 196640 | tf_op jit(solution)/shard_map/ppermute | solution.py:22
  63.4 2.5 %collective-permute-done.18 = bf16[24,2048]{1,0:T(8,128)(2,1)S(1)} collective-permute-done((bf16[24,2048]{1,0:T(8,128)(2,1)S(1)}, bf16[24,2048]{1,0:T(8,128)(2,1)S(1)}, u32[]{:S(2)}, u32[]{:S(2)}) %collective-permute-start.18) | collective-permute-done | bytes 98336 | tf_op jit(solution)/shard_map/ppermute | solution.py:22
  66.0 1.2 %collective-permute-start.19 = (bf16[48,2048]{1,0:T(8,128)(2,1)S(1)}, bf16[48,2048]{1,0:T(8,128)(2,1)S(1)}, u32[]{:S(2)}, u32[]{:S(2)}) collective-permute-start(bf16[48,2048]{1,0:T(8,128)(2,1)S(1)} %constant_dynamic-update-slice_fusion.refs_0_), channel_id=1, source_target_pairs={{0,2},{1,3},{2,0},{3,1},{4,6},{5,7},{6,4},{7,5},{8,10},{9,11},{10,... | collective-permute-start | bytes 589832 | tf_op jit(solution)/shard_map/ppermute | solution.py:22
  67.2 0.5 collective-permute-start.21
  67.7 0.9 collective-permute-done.20.refs_2_
  68.6 0.3 collective-permute-done.21.refs_3_
  68.9 1.6 %shard_map.141 = (bf16[96,2048]{1,0:T(8,128)(2,1)S(1)}, bf16[96,2048]{1,0:T(8,128)(2,1)S(1)}) custom-call(bf16[48,2048]{1,0:T(8,128)(2,1)S(1)} %pad_maximum_fusion.1.refs_0_, bf16[48,2048]{1,0:T(8,128)(2,1)S(1)} %collective-permute-done.13.refs_1_, bf16[48,2048]{1,0:T(8,128)(2,1)S(1)} %collective-permute-done.20.refs_2_, ...), custom_call_target="tpu_custom_call" | custom-call | flops 830472192 | bytes 5898240 | tf_op jit(solution)/shard_map/pallas_call | solution.py:68
  70.6 1.1 collective-permute-done.19.refs_1_
  71.7 0.6 collective-permute-start.24
  72.6 0.5 collective-permute-start.26
  73.1 0.3 collective-permute-done.22
  73.5 1.2 %collective-permute-start.23 = (bf16[48,2048]{1,0:T(8,128)(2,1)S(1)}, bf16[48,2048]{1,0:T(8,128)(2,1)S(1)}, u32[]{:S(2)}, u32[]{:S(2)}) collective-permute-start(bf16[48,2048]{1,0:T(8,128)(2,1)S(1)} %slice.92), channel_id=1, source_target_pairs={{0,2},{1,3},{2,0},{3,1},{4,6},{5,7},{6,4},{7,5},{8,10},{9,11},{10,... | collective-permute-start | bytes 589832 | tf_op jit(solution)/shard_map/ppermute | solution.py:22
  74.8 0.3 collective-permute-done.26.refs_3_
  75.1 1.6 %shard_map.142 = (bf16[96,2048]{1,0:T(8,128)(2,1)S(1)}, bf16[96,2048]{1,0:T(8,128)(2,1)S(1)}) custom-call(bf16[48,2048]{1,0:T(8,128)(2,1)S(1)} %constant_dynamic-update-slice_fusion.refs_0_, bf16[48,2048]{1,0:T(8,128)(2,1)S(1)} %collective-permute-done.19.refs_1_, bf16[48,2048]{1,0:T(8,128)(2,1)S(1)} %collective-permute-done.25.refs_2_, ...), custom_call_target="tpu_custom_call" | custom-call | flops 830472192 | bytes 5898240 | tf_op jit(solution)/shard_map/pallas_call | solution.py:68
  77.0 3.2 %shard_map.143 = (bf16[192,2048]{1,0:T(8,128)(2,1)S(1)}, bf16[192,2048]{1,0:T(8,128)(2,1)S(1)}) custom-call(bf16[192,2048]{1,0:T(8,128)(2,1)S(1)} %constant_dynamic-update-slice_fusion.2.refs_0_, bf16[192,2048]{1,0:T(8,128)(2,1)S(1)} %collective-permute-done.24.refs_1_, bf16[352,2048]{1,0:T(8,128)(2,1)S(1)} %bitcast.19, bf16[352,2048]{1,0:T(8,128)(2,1)S(1)} %bitcast.22, ...), custom_call_target="tpu_custom_call" | custom-call | flops 1660944384 | bytes 7471104 | tf_op jit(solution)/shard_map/pallas_call | solution.py:68
  80.1 0.4 collective-permute-done.23
  80.8 1.2 %collective-permute-start.34 = (bf16[48,2048]{1,0:T(8,128)(2,1)S(1)}, bf16[48,2048]{1,0:T(8,128)(2,1)S(1)}, u32[]{:S(2)}, u32[]{:S(2)}) collective-permute-start(bf16[48,2048]{1,0:T(8,128)(2,1)S(1)} %slice.103), channel_id=1, source_target_pairs={{0,2},{1,3},{2,0},{3,1},{4,6},{5,7},{6,4},{7,5},{8,10},{9,11},{10,... | collective-permute-start | bytes 589832 | tf_op jit(solution)/shard_map/ppermute | solution.py:22
  82.1 0.8 collective-permute-start.31
  82.9 2.3 %collective-permute-start.32 = (bf16[24,2048]{1,0:T(8,128)(2,1)S(1)}, bf16[24,2048]{1,0:T(8,128)(2,1)S(1)}, u32[]{:S(2)}, u32[]{:S(2)}) collective-permute-start(bf16[24,2048]{1,0:T(8,128)(2,1)S(1)} %get-tuple-element.149), channel_id=1, source_target_pairs={{0,20},{4,16},{8,28},{12,24},{16,4},{20,0},{24,12},{28,8},{1,21},{... | collective-permute-start | bytes 294920 | tf_op jit(solution)/shard_map/ppermute | solution.py:22
  85.2 3.0 %collective-permute-done.34 = bf16[48,2048]{1,0:T(8,128)(2,1)S(1)} collective-permute-done((bf16[48,2048]{1,0:T(8,128)(2,1)S(1)}, bf16[48,2048]{1,0:T(8,128)(2,1)S(1)}, u32[]{:S(2)}, u32[]{:S(2)}) %collective-permute-start.34) | collective-permute-done | bytes 196640 | tf_op jit(solution)/shard_map/ppermute | solution.py:22
  88.3 2.5 %collective-permute-start.35 = (bf16[24,2048]{1,0:T(8,128)(2,1)S(1)}, bf16[24,2048]{1,0:T(8,128)(2,1)S(1)}, u32[]{:S(2)}, u32[]{:S(2)}) collective-permute-start(bf16[24,2048]{1,0:T(8,128)(2,1)S(1)} %get-tuple-element.148), channel_id=1, source_target_pairs={{0,24},{4,28},{8,16},{12,20},{16,8},{20,12},{24,0},{28,4},{1,25},{... | collective-permute-start | bytes 294920 | tf_op jit(solution)/shard_map/ppermute | solution.py:22
  90.7 1.5 %collective-permute-start.36 = (bf16[24,2048]{1,0:T(8,128)(2,1)S(1)}, bf16[24,2048]{1,0:T(8,128)(2,1)S(1)}, u32[]{:S(2)}, u32[]{:S(2)}) collective-permute-start(bf16[24,2048]{1,0:T(8,128)(2,1)S(1)} %get-tuple-element.147), channel_id=1, source_target_pairs={{0,28},{4,24},{8,20},{12,16},{16,12},{20,8},{24,4},{28,0},{1,29},{... | collective-permute-start | bytes 294920 | tf_op jit(solution)/shard_map/ppermute | solution.py:22
  92.6 1.4 %collective-permute-start.28 = (bf16[48,2048]{1,0:T(8,128)(2,1)S(1)}, bf16[48,2048]{1,0:T(8,128)(2,1)S(1)}, u32[]{:S(2)}, u32[]{:S(2)}) collective-permute-start(bf16[48,2048]{1,0:T(8,128)(2,1)S(1)} %get-tuple-element.143), channel_id=1, source_target_pairs={{0,4},{4,0},{8,12},{12,8},{16,20},{20,16},{24,28},{28,24},{1,5},{5... | collective-permute-start | bytes 589832 | tf_op jit(solution)/shard_map/ppermute | solution.py:22
  94.0 5.3 %collective-permute-done.32.refs_7_ = bf16[24,2048]{1,0:T(8,128)(2,1)S(1)} collective-permute-done((bf16[24,2048]{1,0:T(8,128)(2,1)S(1)}, bf16[24,2048]{1,0:T(8,128)(2,1)S(1)}, u32[]{:S(2)}, u32[]{:S(2)}) %collective-permute-start.32) | collective-permute-done | bytes 98336 | tf_op jit(solution)/shard_map/ppermute | solution.py:22
  99.3 2.6 %shard_map.144 = (f32[128,2048]{1,0:T(8,128)S(1)}, f32[128,2048]{1,0:T(8,128)S(1)}) custom-call(bf16[128,2048]{1,0:T(8,128)(2,1)S(1)} %get-tuple-element.132.refs_1_.refs_0_, bf16[128,2048]{1,0:T(8,128)(2,1)S(1)} %collective-permute-done.10.refs_2_.refs_1_, bf16[704,2048]{1,0:T(8,128)(2,1)S(1)} %bitcast.26, bf16[704,2048]{1,0:T(8,128)(2,1)S(1)} %bitcast.27, ...), custom_call_target="tpu_custom_call" | custom-call | flops 2214592512 | bytes 11796480 | tf_op jit(solution)/shard_map/pallas_call | solution.py:68
  102.3 4.7 %collective-permute-done.30.refs_5_ = bf16[48,2048]{1,0:T(8,128)(2,1)S(1)} collective-permute-done((bf16[48,2048]{1,0:T(8,128)(2,1)S(1)}, bf16[48,2048]{1,0:T(8,128)(2,1)S(1)}, u32[]{:S(2)}, u32[]{:S(2)}) %collective-permute-start.30) | collective-permute-done | bytes 196640 | tf_op jit(solution)/shard_map/ppermute | solution.py:22
  107.0 0.7 shard_map.146
  107.8 0.7 shard_map.145
  108.5 1.2 collective-permute-done.37
  109.8 1.0 collective-permute-start.38
  110.8 7.5 %collective-permute-done.38 = bf16[64,2048]{1,0:T(8,128)(2,1)S(1)} collective-permute-done((bf16[64,2048]{1,0:T(8,128)(2,1)S(1)}, bf16[64,2048]{1,0:T(8,128)(2,1)S(1)}, u32[]{:S(2)}, u32[]{:S(2)}) %collective-permute-start.38) | collective-permute-done | bytes 262176 | tf_op jit(solution)/shard_map/ppermute | solution.py:22
  118.3 0.8 add_convert_fusion.4
  (94 shorter events, 3.5 us)
Async XLA Ops:
  0.0 11.2 %collective-permute-start = (bf16[32,4608]{1,0:T(8,128)(2,1)}, bf16[32,4608]{1,0:T(8,128)(2,1)S(1)}, u32[]{:S(2)}, u32[]{:S(2)}) collective-permute-start(bf16[32,4608]{1,0:T(8,128)(2,1)} %refs_2_.1), channel_id=1, source_target_pairs={{0,2},{1,3},{2,0},{3,1},{4,6},{5,7},{6,4},{7,5},{8,10},{9,11},{10,... | collective-permute-start | bytes 884744 | tf_op jit(solution)/shard_map/ppermute | solution.py:22
  3.0 8.2 %collective-permute-start.1 = (bf16[32,4608]{1,0:T(8,128)(2,1)}, bf16[32,4608]{1,0:T(8,128)(2,1)S(1)}, u32[]{:S(2)}, u32[]{:S(2)}) collective-permute-start(bf16[32,4608]{1,0:T(8,128)(2,1)} %refs_2_.1), channel_id=1, source_target_pairs={{0,1},{1,0},{2,3},{3,2},{4,5},{5,4},{6,7},{7,6},{8,9},{9,8},{10,11... | collective-permute-start | bytes 884744 | tf_op jit(solution)/shard_map/ppermute | solution.py:22
  3.7 7.5 %collective-permute-start.3 = (s32[64,4]{0,1:T(4,128)S(1)}, s32[64,4]{0,1:T(4,128)S(1)}, u32[]{:S(2)}, u32[]{:S(2)}) collective-permute-start(s32[64,4]{0,1:T(4,128)S(1)} %pad_add_fusion.1), channel_id=1, source_target_pairs={{0,2},{1,3},{2,0},{3,1},{4,6},{5,7},{6,4},{7,5},{8,10},{9,11},{10,... | collective-permute-start | bytes 3080 | tf_op jit(solution)/shard_map/ppermute | solution.py:22
  3.7 7.5 %collective-permute-start.2 = (s32[32]{0:T(128)}, s32[32]{0:T(128)S(1)}, u32[]{:S(2)}, u32[]{:S(2)}) collective-permute-start(s32[32]{0:T(128)} %param.16), channel_id=1, source_target_pairs={{0,2},{1,3},{2,0},{3,1},{4,6},{5,7},{6,4},{7,5},{8,10},{9,11},{10,... | collective-permute-start | bytes 392 | tf_op jit(solution)/shard_map/ppermute | solution.py:22
  5.7 2.3 %copy-start.3 = (bf16[4608,512]{1,0:T(8,128)(2,1)S(1)}, bf16[4608,512]{1,0:T(8,128)(2,1)}, u32[]{:S(2)}) copy-start(bf16[4608,512]{1,0:T(8,128)(2,1)} %refs_0_.1) | copy-start | bytes 14155780
  8.0 1.6 %copy-start.7 = (bf16[512,2048]{1,0:T(8,128)(2,1)S(1)}, bf16[512,2048]{1,0:T(8,128)(2,1)}, u32[]{:S(2)}) copy-start(bf16[512,2048]{1,0:T(8,128)(2,1)} %refs_1_.1) | copy-start | bytes 6291460
  9.6 1.0 copy-start.8
  11.2 1.6 %collective-permute-start.4 = (bf16[32,4608]{1,0:T(8,128)(2,1)S(1)}, bf16[32,4608]{1,0:T(8,128)(2,1)S(1)}, u32[]{:S(2)}, u32[]{:S(2)}) collective-permute-start(bf16[32,4608]{1,0:T(8,128)(2,1)S(1)} %collective-permute-done.refs_1_), channel_id=1, source_target_pairs={{0,1},{1,0},{2,3},{3,2},{4,5},{5,4},{6,7},{7,6},{8,9},{9,8},{10,11... | collective-permute-start | bytes 884744 | tf_op jit(solution)/shard_map/ppermute | solution.py:22
  12.8 1.4 %copy-start.11 = (s32[32]{0:T(128)S(1)}, s32[32]{0:T(128)}, u32[]{:S(2)}) copy-start(s32[32]{0:T(128)} %param.16) | copy-start | bytes 388
  12.8 9.6 %copy-start.9 = (bf16[64,2048]{1,0:T(8,128)(2,1)S(1)}, bf16[64,2048]{1,0:T(8,128)(2,1)}, u32[]{:S(2)}) copy-start(bf16[64,2048]{1,0:T(8,128)(2,1)} %refs_2_.2) | copy-start | bytes 786436
  12.8 26.0 %copy-start.10 = (f32[2048]{0:T(1024)S(1)}, f32[2048]{0:T(1024)}, u32[]{:S(2)}) copy-start(f32[2048]{0:T(1024)} %param.19) | copy-start | bytes 24580
  14.1 1.6 %collective-permute-start.5 = (bf16[64,2048]{1,0:T(8,128)(2,1)S(1)}, bf16[64,2048]{1,0:T(8,128)(2,1)S(1)}, u32[]{:S(2)}, u32[]{:S(2)}) collective-permute-start(bf16[64,2048]{1,0:T(8,128)(2,1)S(1)} %get-tuple-element.86), channel_id=1, source_target_pairs={{0,1},{1,0},{2,3},{3,2},{4,5},{5,4},{6,7},{7,6},{8,9},{9,8},{10,11... | collective-permute-start | bytes 786440 | tf_op jit(solution)/shard_map/ppermute | solution.py:22
  16.7 15.3 %all-to-all-start = ((bf16[8,8,2176]{2,1,0:T(8,128)(2,1)}), bf16[8,8,2176]{2,1,0:T(8,128)(2,1)S(1)}, u32[]{:S(2)}, u32[]{:S(2)}) async-start(bf16[8,8,2176]{2,1,0:T(8,128)(2,1)} %shard_map.138), calls=%async_computation | async-start | bytes 557056 | tf_op jit(solution)/shard_map/all_to_all | solution.py:389
  22.5 8.1 %collective-permute-start.6 = (bf16[64,2048]{1,0:T(8,128)(2,1)S(1)}, bf16[64,2048]{1,0:T(8,128)(2,1)S(1)}, u32[]{:S(2)}, u32[]{:S(2)}) collective-permute-start(bf16[64,2048]{1,0:T(8,128)(2,1)S(1)} %copy-done.9), channel_id=1, source_target_pairs={{0,2},{1,3},{2,0},{3,1},{4,6},{5,7},{6,4},{7,5},{8,10},{9,11},{10,... | collective-permute-start | bytes 786440 | tf_op jit(solution)/shard_map/ppermute | solution.py:22
  23.4 1.2 collective-permute-start.7
  23.4 1.3 %collective-permute-start.8 = (s32[64,4]{0,1:T(4,128)S(1)}, s32[64,4]{0,1:T(4,128)S(1)}, u32[]{:S(2)}, u32[]{:S(2)}) collective-permute-start(s32[64,4]{0,1:T(4,128)S(1)} %collective-permute-done.3), channel_id=1, source_target_pairs={{0,1},{1,0},{2,3},{3,2},{4,5},{5,4},{6,7},{7,6},{8,9},{9,8},{10,11... | collective-permute-start | bytes 3080 | tf_op jit(solution)/shard_map/ppermute | solution.py:22
  32.0 6.8 %collective-permute-start.9 = (bf16[8,8,2176]{2,1,0:T(8,128)(2,1)S(1)}, bf16[8,8,2176]{2,1,0:T(8,128)(2,1)S(1)}, u32[]{:S(2)}, u32[]{:S(2)}) collective-permute-start(bf16[8,8,2176]{2,1,0:T(8,128)(2,1)S(1)} %all-to-all-done.refs_0_), channel_id=1, source_target_pairs={{0,2},{1,3},{2,0},{3,1},{4,6},{5,7},{6,4},{7,5},{8,10},{9,11},{10,... | collective-permute-start | bytes 835592 | tf_op jit(solution)/shard_map/ppermute | solution.py:22
  38.8 30.1 %copy-start = (bf16[1,2048,352]{1,2,0:T(8,128)(2,1)S(1)}, bf16[1,2048,352]{1,2,0:T(8,128)(2,1)}, u32[]{:S(2)}) copy-start(bf16[1,2048,352]{1,2,0:T(8,128)(2,1)} %param.23) | copy-start | bytes 4325380
  38.8 30.1 %copy-start.1 = (bf16[1,2048,352]{1,2,0:T(8,128)(2,1)S(1)}, bf16[1,2048,352]{1,2,0:T(8,128)(2,1)}, u32[]{:S(2)}) copy-start(bf16[1,2048,352]{1,2,0:T(8,128)(2,1)} %param.24) | copy-start | bytes 4325380
  38.8 30.1 %copy-start.2 = (bf16[1,352,2048]{2,1,0:T(8,128)(2,1)S(1)}, bf16[1,352,2048]{2,1,0:T(8,128)(2,1)}, u32[]{:S(2)}) copy-start(bf16[1,352,2048]{2,1,0:T(8,128)(2,1)} %param.25) | copy-start | bytes 4325380
  39.5 2.0 %collective-permute-start.10 = (bf16[128,2048]{1,0:T(8,128)(2,1)S(1)}, bf16[128,2048]{1,0:T(8,128)(2,1)S(1)}, u32[]{:S(2)}, u32[]{:S(2)}) collective-permute-start(bf16[128,2048]{1,0:T(8,128)(2,1)S(1)} %get-tuple-element.132.refs_1_.refs_0_), channel_id=1, source_target_pairs={{0,1},{1,0},{2,3},{3,2},{4,5},{5,4},{6,7},{7,6},{8,9},{9,8},{10,11... | collective-permute-start | bytes 1572872 | tf_op jit(solution)/shard_map/ppermute | solution.py:22
  42.0 11.4 %collective-permute-start.12 = (bf16[24,2048]{1,0:T(8,128)(2,1)S(1)}, bf16[24,2048]{1,0:T(8,128)(2,1)S(1)}, u32[]{:S(2)}, u32[]{:S(2)}) collective-permute-start(bf16[24,2048]{1,0:T(8,128)(2,1)S(1)} %get-tuple-element.103), channel_id=1, source_target_pairs={{0,20},{4,16},{8,28},{12,24},{16,4},{20,0},{24,12},{28,8},{1,21},{... | collective-permute-start | bytes 294920 | tf_op jit(solution)/shard_map/ppermute | solution.py:22
  44.6 10.2 %collective-permute-start.11 = (bf16[24,2048]{1,0:T(8,128)(2,1)S(1)}, bf16[24,2048]{1,0:T(8,128)(2,1)S(1)}, u32[]{:S(2)}, u32[]{:S(2)}) collective-permute-start(bf16[24,2048]{1,0:T(8,128)(2,1)S(1)} %get-tuple-element.102), channel_id=1, source_target_pairs={{0,16},{4,20},{8,24},{12,28},{16,0},{20,4},{24,8},{28,12},{1,17},{... | collective-permute-start | bytes 294920 | tf_op jit(solution)/shard_map/ppermute | solution.py:22
  45.7 13.0 %collective-permute-start.14 = (bf16[48,2048]{1,0:T(8,128)(2,1)S(1)}, bf16[48,2048]{1,0:T(8,128)(2,1)S(1)}, u32[]{:S(2)}, u32[]{:S(2)}) collective-permute-start(bf16[48,2048]{1,0:T(8,128)(2,1)S(1)} %get-tuple-element.105), channel_id=1, source_target_pairs={{0,4},{4,0},{8,12},{12,8},{16,20},{20,16},{24,28},{28,24},{1,5},{5... | collective-permute-start | bytes 589832 | tf_op jit(solution)/shard_map/ppermute | solution.py:22
  46.5 13.5 %collective-permute-start.15 = (bf16[48,2048]{1,0:T(8,128)(2,1)S(1)}, bf16[48,2048]{1,0:T(8,128)(2,1)S(1)}, u32[]{:S(2)}, u32[]{:S(2)}) collective-permute-start(bf16[48,2048]{1,0:T(8,128)(2,1)S(1)} %get-tuple-element.106), channel_id=1, source_target_pairs={{0,8},{4,12},{8,0},{12,4},{16,24},{20,28},{24,16},{28,20},{1,9},{5... | collective-permute-start | bytes 589832 | tf_op jit(solution)/shard_map/ppermute | solution.py:22
  47.3 16.1 %collective-permute-start.16 = (bf16[48,2048]{1,0:T(8,128)(2,1)S(1)}, bf16[48,2048]{1,0:T(8,128)(2,1)S(1)}, u32[]{:S(2)}, u32[]{:S(2)}) collective-permute-start(bf16[48,2048]{1,0:T(8,128)(2,1)S(1)} %get-tuple-element.107), channel_id=1, source_target_pairs={{0,12},{4,8},{8,4},{12,0},{16,28},{20,24},{24,20},{28,16},{1,13},{... | collective-permute-start | bytes 589832 | tf_op jit(solution)/shard_map/ppermute | solution.py:22
  54.8 11.1 %collective-permute-start.13 = (bf16[48,2048]{1,0:T(8,128)(2,1)S(1)}, bf16[48,2048]{1,0:T(8,128)(2,1)S(1)}, u32[]{:S(2)}, u32[]{:S(2)}) collective-permute-start(bf16[48,2048]{1,0:T(8,128)(2,1)S(1)} %pad_maximum_fusion.1.refs_0_), channel_id=1, source_target_pairs={{0,2},{1,3},{2,0},{3,1},{4,6},{5,7},{6,4},{7,5},{8,10},{9,11},{10,... | collective-permute-start | bytes 589832 | tf_op jit(solution)/shard_map/ppermute | solution.py:22
  55.8 7.7 %collective-permute-start.17 = (bf16[24,2048]{1,0:T(8,128)(2,1)S(1)}, bf16[24,2048]{1,0:T(8,128)(2,1)S(1)}, u32[]{:S(2)}, u32[]{:S(2)}) collective-permute-start(bf16[24,2048]{1,0:T(8,128)(2,1)S(1)} %get-tuple-element.111), channel_id=1, source_target_pairs={{0,24},{4,28},{8,16},{12,20},{16,8},{20,12},{24,0},{28,4},{1,25},{... | collective-permute-start | bytes 294920 | tf_op jit(solution)/shard_map/ppermute | solution.py:22
  58.6 7.3 %collective-permute-start.18 = (bf16[24,2048]{1,0:T(8,128)(2,1)S(1)}, bf16[24,2048]{1,0:T(8,128)(2,1)S(1)}, u32[]{:S(2)}, u32[]{:S(2)}) collective-permute-start(bf16[24,2048]{1,0:T(8,128)(2,1)S(1)} %get-tuple-element.112), channel_id=1, source_target_pairs={{0,28},{4,24},{8,20},{12,16},{16,12},{20,8},{24,4},{28,0},{1,29},{... | collective-permute-start | bytes 294920 | tf_op jit(solution)/shard_map/ppermute | solution.py:22
  66.0 5.7 %collective-permute-start.19 = (bf16[48,2048]{1,0:T(8,128)(2,1)S(1)}, bf16[48,2048]{1,0:T(8,128)(2,1)S(1)}, u32[]{:S(2)}, u32[]{:S(2)}) collective-permute-start(bf16[48,2048]{1,0:T(8,128)(2,1)S(1)} %constant_dynamic-update-slice_fusion.refs_0_), channel_id=1, source_target_pairs={{0,2},{1,3},{2,0},{3,1},{4,6},{5,7},{6,4},{7,5},{8,10},{9,11},{10,... | collective-permute-start | bytes 589832 | tf_op jit(solution)/shard_map/ppermute | solution.py:22
  67.2 1.4 %collective-permute-start.20 = (bf16[48,2048]{1,0:T(8,128)(2,1)S(1)}, bf16[48,2048]{1,0:T(8,128)(2,1)S(1)}, u32[]{:S(2)}, u32[]{:S(2)}) collective-permute-start(bf16[48,2048]{1,0:T(8,128)(2,1)S(1)} %pad_maximum_fusion.1.refs_0_), channel_id=1, source_target_pairs={{0,1},{1,0},{2,3},{3,2},{4,5},{5,4},{6,7},{7,6},{8,9},{9,8},{10,11... | collective-permute-start | bytes 589832 | tf_op jit(solution)/shard_map/ppermute | solution.py:22
  67.2 1.7 %collective-permute-start.21 = (bf16[48,2048]{1,0:T(8,128)(2,1)S(1)}, bf16[48,2048]{1,0:T(8,128)(2,1)S(1)}, u32[]{:S(2)}, u32[]{:S(2)}) collective-permute-start(bf16[48,2048]{1,0:T(8,128)(2,1)S(1)} %collective-permute-done.13.refs_1_), channel_id=1, source_target_pairs={{0,1},{1,0},{2,3},{3,2},{4,5},{5,4},{6,7},{7,6},{8,9},{9,8},{10,11... | collective-permute-start | bytes 589832 | tf_op jit(solution)/shard_map/ppermute | solution.py:22
  71.7 1.7 %collective-permute-start.22 = (bf16[96,2048]{1,0:T(8,128)(2,1)S(1)}, bf16[96,2048]{1,0:T(8,128)(2,1)S(1)}, u32[]{:S(2)}, u32[]{:S(2)}) collective-permute-start(bf16[96,2048]{1,0:T(8,128)(2,1)S(1)} %get-tuple-element.120), channel_id=1, source_target_pairs={{0,1},{1,0},{2,3},{3,2},{4,5},{5,4},{6,7},{7,6},{8,9},{9,8},{10,11... | collective-permute-start | bytes 1179656 | tf_op jit(solution)/shard_map/ppermute | solution.py:22
  71.7 5.2 %collective-permute-start.24 = (bf16[192,2048]{1,0:T(8,128)(2,1)S(1)}, bf16[192,2048]{1,0:T(8,128)(2,1)S(1)}, u32[]{:S(2)}, u32[]{:S(2)}) collective-permute-start(bf16[192,2048]{1,0:T(8,128)(2,1)S(1)} %constant_dynamic-update-slice_fusion.2.refs_0_), channel_id=1, source_target_pairs={{0,1},{1,0},{2,3},{3,2},{4,5},{5,4},{6,7},{7,6},{8,9},{9,8},{10,11... | collective-permute-start | bytes 2359304 | tf_op jit(solution)/shard_map/ppermute | solution.py:22
  72.6 2.3 %collective-permute-start.25 = (bf16[48,2048]{1,0:T(8,128)(2,1)S(1)}, bf16[48,2048]{1,0:T(8,128)(2,1)S(1)}, u32[]{:S(2)}, u32[]{:S(2)}) collective-permute-start(bf16[48,2048]{1,0:T(8,128)(2,1)S(1)} %constant_dynamic-update-slice_fusion.refs_0_), channel_id=1, source_target_pairs={{0,1},{1,0},{2,3},{3,2},{4,5},{5,4},{6,7},{7,6},{8,9},{9,8},{10,11... | collective-permute-start | bytes 589832 | tf_op jit(solution)/shard_map/ppermute | solution.py:22
  72.6 2.5 %collective-permute-start.26 = (bf16[48,2048]{1,0:T(8,128)(2,1)S(1)}, bf16[48,2048]{1,0:T(8,128)(2,1)S(1)}, u32[]{:S(2)}, u32[]{:S(2)}) collective-permute-start(bf16[48,2048]{1,0:T(8,128)(2,1)S(1)} %collective-permute-done.19.refs_1_), channel_id=1, source_target_pairs={{0,1},{1,0},{2,3},{3,2},{4,5},{5,4},{6,7},{7,6},{8,9},{9,8},{10,11... | collective-permute-start | bytes 589832 | tf_op jit(solution)/shard_map/ppermute | solution.py:22
  73.5 7.0 %collective-permute-start.23 = (bf16[48,2048]{1,0:T(8,128)(2,1)S(1)}, bf16[48,2048]{1,0:T(8,128)(2,1)S(1)}, u32[]{:S(2)}, u32[]{:S(2)}) collective-permute-start(bf16[48,2048]{1,0:T(8,128)(2,1)S(1)} %slice.92), channel_id=1, source_target_pairs={{0,2},{1,3},{2,0},{3,1},{4,6},{5,7},{6,4},{7,5},{8,10},{9,11},{10,... | collective-permute-start | bytes 589832 | tf_op jit(solution)/shard_map/ppermute | solution.py:22
  76.8 3.9 %collective-permute-start.33 = (bf16[96,2048]{1,0:T(8,128)(2,1)S(1)}, bf16[96,2048]{1,0:T(8,128)(2,1)S(1)}, u32[]{:S(2)}, u32[]{:S(2)}) collective-permute-start(bf16[96,2048]{1,0:T(8,128)(2,1)S(1)} %get-tuple-element.139), channel_id=1, source_target_pairs={{0,1},{1,0},{2,3},{3,2},{4,5},{5,4},{6,7},{7,6},{8,9},{9,8},{10,11... | collective-permute-start | bytes 1179656 | tf_op jit(solution)/shard_map/ppermute | solution.py:22
  77.0 22.3 %copy-start.6 = (bf16[704,2048]{1,0:T(8,128)(2,1)S(1)}, bf16[704,2048]{1,0:T(8,128)(2,1)}, u32[]{:S(2)}) copy-start(bf16[704,2048]{1,0:T(8,128)(2,1)} %refs_4_.1) | copy-start | bytes 8650756
  80.6 11.7 %collective-permute-start.27 = (bf16[192,2048]{1,0:T(8,128)(2,1)S(1)}, bf16[192,2048]{1,0:T(8,128)(2,1)S(1)}, u32[]{:S(2)}, u32[]{:S(2)}) collective-permute-start(bf16[192,2048]{1,0:T(8,128)(2,1)S(1)} %get-tuple-element.136), channel_id=1, source_target_pairs={{0,1},{1,0},{2,3},{3,2},{4,5},{5,4},{6,7},{7,6},{8,9},{9,8},{10,11... | collective-permute-start | bytes 2359304 | tf_op jit(solution)/shard_map/ppermute | solution.py:22
  80.7 18.6 %copy-start.5 = (bf16[2048,704]{0,1:T(8,128)(2,1)S(1)}, bf16[2048,704]{0,1:T(8,128)(2,1)}, u32[]{:S(2)}) copy-start(bf16[2048,704]{0,1:T(8,128)(2,1)} %param.21) | copy-start | bytes 8650756
  80.8 7.4 %collective-permute-start.34 = (bf16[48,2048]{1,0:T(8,128)(2,1)S(1)}, bf16[48,2048]{1,0:T(8,128)(2,1)S(1)}, u32[]{:S(2)}, u32[]{:S(2)}) collective-permute-start(bf16[48,2048]{1,0:T(8,128)(2,1)S(1)} %slice.103), channel_id=1, source_target_pairs={{0,2},{1,3},{2,0},{3,1},{4,6},{5,7},{6,4},{7,5},{8,10},{9,11},{10,... | collective-permute-start | bytes 589832 | tf_op jit(solution)/shard_map/ppermute | solution.py:22
  82.1 12.0 %collective-permute-start.31 = (bf16[24,2048]{1,0:T(8,128)(2,1)S(1)}, bf16[24,2048]{1,0:T(8,128)(2,1)S(1)}, u32[]{:S(2)}, u32[]{:S(2)}) collective-permute-start(bf16[24,2048]{1,0:T(8,128)(2,1)S(1)} %get-tuple-element.150), channel_id=1, source_target_pairs={{0,16},{4,20},{8,24},{12,28},{16,0},{20,4},{24,8},{28,12},{1,17},{... | collective-permute-start | bytes 294920 | tf_op jit(solution)/shard_map/ppermute | solution.py:22
  82.9 16.4 %collective-permute-start.32 = (bf16[24,2048]{1,0:T(8,128)(2,1)S(1)}, bf16[24,2048]{1,0:T(8,128)(2,1)S(1)}, u32[]{:S(2)}, u32[]{:S(2)}) collective-permute-start(bf16[24,2048]{1,0:T(8,128)(2,1)S(1)} %get-tuple-element.149), channel_id=1, source_target_pairs={{0,20},{4,16},{8,28},{12,24},{16,4},{20,0},{24,12},{28,8},{1,21},{... | collective-permute-start | bytes 294920 | tf_op jit(solution)/shard_map/ppermute | solution.py:22
  88.2 11.1 %copy-start.4 = (bf16[2048,704]{0,1:T(8,128)(2,1)S(1)}, bf16[2048,704]{0,1:T(8,128)(2,1)}, u32[]{:S(2)}) copy-start(bf16[2048,704]{0,1:T(8,128)(2,1)} %param.20) | copy-start | bytes 8650756
  88.3 13.7 %collective-permute-start.35 = (bf16[24,2048]{1,0:T(8,128)(2,1)S(1)}, bf16[24,2048]{1,0:T(8,128)(2,1)S(1)}, u32[]{:S(2)}, u32[]{:S(2)}) collective-permute-start(bf16[24,2048]{1,0:T(8,128)(2,1)S(1)} %get-tuple-element.148), channel_id=1, source_target_pairs={{0,24},{4,28},{8,16},{12,20},{16,8},{20,12},{24,0},{28,4},{1,25},{... | collective-permute-start | bytes 294920 | tf_op jit(solution)/shard_map/ppermute | solution.py:22
  90.7 11.2 %collective-permute-start.36 = (bf16[24,2048]{1,0:T(8,128)(2,1)S(1)}, bf16[24,2048]{1,0:T(8,128)(2,1)S(1)}, u32[]{:S(2)}, u32[]{:S(2)}) collective-permute-start(bf16[24,2048]{1,0:T(8,128)(2,1)S(1)} %get-tuple-element.147), channel_id=1, source_target_pairs={{0,28},{4,24},{8,20},{12,16},{16,12},{20,8},{24,4},{28,0},{1,29},{... | collective-permute-start | bytes 294920 | tf_op jit(solution)/shard_map/ppermute | solution.py:22
  92.6 9.6 %collective-permute-start.28 = (bf16[48,2048]{1,0:T(8,128)(2,1)S(1)}, bf16[48,2048]{1,0:T(8,128)(2,1)S(1)}, u32[]{:S(2)}, u32[]{:S(2)}) collective-permute-start(bf16[48,2048]{1,0:T(8,128)(2,1)S(1)} %get-tuple-element.143), channel_id=1, source_target_pairs={{0,4},{4,0},{8,12},{12,8},{16,20},{20,16},{24,28},{28,24},{1,5},{5... | collective-permute-start | bytes 589832 | tf_op jit(solution)/shard_map/ppermute | solution.py:22
  94.0 8.3 %collective-permute-start.29 = (bf16[48,2048]{1,0:T(8,128)(2,1)S(1)}, bf16[48,2048]{1,0:T(8,128)(2,1)S(1)}, u32[]{:S(2)}, u32[]{:S(2)}) collective-permute-start(bf16[48,2048]{1,0:T(8,128)(2,1)S(1)} %get-tuple-element.142), channel_id=1, source_target_pairs={{0,8},{4,12},{8,0},{12,4},{16,24},{20,28},{24,16},{28,20},{1,9},{5... | collective-permute-start | bytes 589832 | tf_op jit(solution)/shard_map/ppermute | solution.py:22
  99.3 7.7 %collective-permute-start.30 = (bf16[48,2048]{1,0:T(8,128)(2,1)S(1)}, bf16[48,2048]{1,0:T(8,128)(2,1)S(1)}, u32[]{:S(2)}, u32[]{:S(2)}) collective-permute-start(bf16[48,2048]{1,0:T(8,128)(2,1)S(1)} %get-tuple-element.141), channel_id=1, source_target_pairs={{0,12},{4,8},{8,4},{12,0},{16,28},{20,24},{24,20},{28,16},{1,13},{... | collective-permute-start | bytes 589832 | tf_op jit(solution)/shard_map/ppermute | solution.py:22
  107.7 2.0 %collective-permute-start.37 = (bf16[128,2048]{1,0:T(8,128)(2,1)S(1)}, bf16[128,2048]{1,0:T(8,128)(2,1)S(1)}, u32[]{:S(2)}, u32[]{:S(2)}) collective-permute-start(bf16[128,2048]{1,0:T(8,128)(2,1)S(1)} %shard_map.146), channel_id=1, source_target_pairs={{0,1},{1,0},{2,3},{3,2},{4,5},{5,4},{6,7},{7,6},{8,9},{9,8},{10,11... | collective-permute-start | bytes 1572872 | tf_op jit(solution)/shard_map/ppermute | solution.py:22
  109.8 8.4 %collective-permute-start.38 = (bf16[64,2048]{1,0:T(8,128)(2,1)S(1)}, bf16[64,2048]{1,0:T(8,128)(2,1)S(1)}, u32[]{:S(2)}, u32[]{:S(2)}) collective-permute-start(bf16[64,2048]{1,0:T(8,128)(2,1)S(1)} %slice.107), channel_id=1, source_target_pairs={{0,2},{1,3},{2,0},{3,1},{4,6},{5,7},{6,4},{7,5},{8,10},{9,11},{10,... | collective-permute-start | bytes 786440 | tf_op jit(solution)/shard_map/ppermute | solution.py:22

commit v6 on v5

--- a/solution.py
+++ b/solution.py
@@ -124,12 +124,18 @@
     return all(p.shape[0] % 16 == 0 for p in pieces)
 
 
-def expert_rows(pieces, gate, up, down):
+def expert_rows(pieces, gate, up, down, order=None):
     count = sum(p.shape[0] for p in pieces)
     units, width = gate.shape
+
+    def in_order(rows):
+        if order is None:
+            return rows
+        return jnp.concatenate([rows[at : at + size] for at, size in order], axis=0)
+
     if not fits(pieces) or count % 32:
         part = dot(gated(jnp.concatenate(pieces, axis=0), gate, up), down).astype(BF)
-        return part[: count // 2], part[count // 2 :]
+        return in_order(part[: count // 2]), in_order(part[count // 2 :])
 
     def body(*refs):
         n = len(pieces)
@@ -137,12 +143,12 @@
         put_together(refs[:n], whole)
         if count <= 256:
             part = dot(gated(whole[...], gate_ref[...], up_ref[...]), down_ref[...])
-            keep[...] = part[: count // 2].astype(BF)
-            give[...] = part[count // 2 :].astype(BF)
+            keep[...] = in_order(part[: count // 2]).astype(BF)
+            give[...] = in_order(part[count // 2 :]).astype(BF)
             return
         for rows, result in ((slice(count // 2, count), give), (slice(0, count // 2), keep)):
             hidden = gated(whole[rows], gate_ref[...], up_ref[...])
-            result[...] = dot(hidden, down_ref[...]).astype(BF)
+            result[...] = in_order(dot(hidden, down_ref[...])).astype(BF)
 
     return local_kernel(
         body,
@@ -304,7 +310,7 @@
     )
 
 
-def combine_rows(total, coef, backs, starts, dtype):
+def combine_rows(total, coef, backs, starts, dtype, cuts):
     count, width = total.shape
     slots = coef.shape[2]
     ends = list(starts[1:]) + [slots]
@@ -313,26 +319,30 @@
             [jnp.pad(b, ((0, e - s - b.shape[0]), (0, 0))) for b, s, e in zip(backs, starts, ends)],
             axis=0,
         )
-        return (total + dot(coef[0], whole) + dot(coef[1], whole)).astype(dtype)
-
-    def body(*refs):
-        total_ref, coef_ref, result, whole = refs[0], refs[1], refs[-2], refs[-1]
-        for ref, at, end in zip(refs[2:-2], starts, ends):
+        value = (total + dot(coef[0], whole) + dot(coef[1], whole)).astype(dtype)
+        return jnp.split(value, cuts, axis=1)
+
+    def body(*refs):
+        total_ref, coef_ref, whole = refs[0], refs[1], refs[-1]
+        for ref, at, end in zip(refs[2 : 2 + len(backs)], starts, ends):
             size = ref.shape[0]
             if size != end - at:
                 whole[end - 16 : end] = jnp.zeros((16, width), BF)
             whole[at : at + size] = ref[...]
         rows = whole[...]
         value = total_ref[...] + dot(coef_ref[0], rows)
-        result[...] = (value + dot(coef_ref[1], rows)).astype(dtype)
-
-    return local_kernel(
-        body,
-        [out(count, width, dtype)],
+        value = (value + dot(coef_ref[1], rows)).astype(dtype)
+        step = width // cuts
+        for i, result in enumerate(refs[2 + len(backs) : -1]):
+            result[...] = value[:, i * step : (i + 1) * step]
+
+    return local_kernel(
+        body,
+        [out(count, width // cuts, dtype)] * cuts,
         [total, coef, *backs],
         [pltpu.VMEM((slots, width), BF)],
         2 * count * width * slots,
-    )[0]
+    )
 
 
 def one_hot(places, count):
@@ -402,22 +412,33 @@
     rank = jnp.sum(jnp.where(named, counts[:, None, :], 0.0), axis=2).astype(jnp.int32)
     distance = ids ^ lax.axis_index("dp")
 
-    half = n_data // 2
-    wide = 2 * capacity // 4
-    core = my_place % 2
-    near_slot = jnp.where((distance < half) & (rank // wide == core), distance * wide + rank % wide, -1)
+    half, wide = n_data // 2, capacity // 2
+    core, chip, chips = my_place % 2, my_place // 2, n_group // 2
     apart = -(-share // 16) * 16
-    far_slot = jnp.where(
-        (distance >= half) & (rank // share == my_place),
-        (distance - half) * apart + rank % share + half * wide,
-        -1,
-    )
-    slot = jnp.maximum(near_slot, far_slot)
+    mine = rank // wide == core
+    block = rank % wide // share
+    turned = reversed_bits(block ^ chip, chips) * share + rank % share
+    near_slot = distance * wide + jnp.where(distance < 2, rank % wide, turned)
+    far_slot = half * wide + (distance - half) * apart + rank % share
+    slot = jnp.where(
+        distance < half,
+        jnp.where(mine, near_slot, -1),
+        jnp.where(rank // share == my_place, far_slot, -1),
+    )
     sizes = [wide] * half + [share] * (n_data - half)
     starts = [m * wide if m < half else half * wide + (m - half) * apart for m in range(n_data)]
-    slots = half * wide + (n_data - half) * apart
-    hits = [one_hot(slot[:, k], slots) for k in range(top)]
-    picks = sum(hit.astype(BF) for hit in hits)
+    picks = sum(
+        one_hot(slot[:, k], half * wide + (n_data - half) * apart).astype(BF) for k in range(top)
+    )
+
+    owned = jnp.where(distance < half, mine & (block == chip), rank // share == my_place)
+    back_slot = jnp.where(
+        distance < 2,
+        jnp.where(mine, distance * wide + rank % wide, -1),
+        jnp.where(owned, 2 * wide + (distance - 2) * apart + rank % share, -1),
+    )
+    back_starts = [m * wide if m < 2 else 2 * wide + (m - 2) * apart for m in range(n_data)]
+    hits = [one_hot(back_slot[:, k], 2 * wide + (n_data - 2) * apart) for k in range(top)]
     coef = sum(jnp.where(hit, weights[:, k][None, :], 0.0) for k, hit in enumerate(hits)).T
     coef_hi = coef.astype(BF)
     coef = jnp.stack([coef_hi, (coef - coef_hi.astype(F32)).astype(BF)])
@@ -433,10 +454,6 @@
 
     def both(pieces):
         return pieces + [swap(p, "expert", 1) for p in pieces]
-
-    def send_back(m, rows, i):
-        part = rows[i * sizes[m] : (i + 1) * sizes[m]]
-        return swap(part, "dp", m) if m else part
 
     for m in (*near[1:], *far_one):
         got[m] = swap(send[m], "dp", m)
@@ -453,23 +470,33 @@
     mine = join(near)
     mine = [mine, swap(mine, "expert", 1)]
     mine, two_keep = fence(mine, two_keep)
-    keep, give = expert_rows(mine, *experts)
+    order = [(0, 2 * wide)]
+    order += [(m * wide + p * share, share) for p in range(chips) for m in near[2:]]
+    keep, give = expert_rows(mine, *experts, order)
     one = sum_rest(add(one_keep, swap(one_give, "expert", 1)))
     one, keep, give, normed = fence(one, keep, give, normed)
     two = sum_rest(add(two_keep, swap(two_give, "expert", 1)))
     rows = add(keep, swap(give, "expert", 1))
-    back = [send_back(m, rows, m) for m in near]
-    back += [send_back(m, one, i) for i, m in enumerate(far_one)]
-    back += [send_back(m, two, i) for i, m in enumerate(far_two)]
+    rest = sum_rest(rows[2 * wide :])
+
+    def send_back(m, rows, at, size):
+        part = rows[at : at + size]
+        return swap(part, "dp", m) if m else part
+
+    back = [send_back(m, rows, m * wide, wide) for m in near[:2]]
+    rest, two = fence(rest, two)
+    back += [send_back(m, rest, i * share, share) for i, m in enumerate(near[2:])]
+    back += [send_back(m, one, i * share, share) for i, m in enumerate(far_one)]
+    back += [send_back(m, two, i * share, share) for i, m in enumerate(far_two)]
     shared = shared_rows(normed, shared_gate.T, shared_up.T, shared_down)
 
     middle = group_rows // 2
     keep, give = [
-        combine_rows(part, coef[:, rows], back, starts, BF)
+        combine_rows(part, coef[:, rows], back, back_starts, BF, 2)
         for part, rows in zip(shared, (slice(0, middle), slice(middle, None)))
     ]
-    total = sum_rest(add(keep, swap(give, "expert", 1)))
-    return (embed_f + total.astype(F32)).astype(BF)
+    total = [sum_rest(add(k, swap(g, "expert", 1))) for k, g in zip(keep, give)]
+    return (embed_f + jnp.concatenate(total, axis=1).astype(F32)).astype(BF)
 
 
 def solution(mesh):

time: 119 us -> 117 us (0.983)
  waiting for transfers between devices: 54.9 us -> 47.5 us
  starting transfers between devices: 40.8 us -> 45.3 us
    ppermute x39 -> x42, waiting for transfers between devices: 53.5 us -> 46.1 us  [swap(): return lax.ppermute(rows, axis, [(i, i ^ mask) for i in range(count)])]
    ppermute x39 -> x42, starting transfers between devices: 35 us -> 39.5 us  [swap(): return lax.ppermute(rows, axis, [(i, i ^ mask) for i in range(count)])]
  transfers between devices with their start and end apart: 40 -> 43, of which waited for: 26 -> 26; matrix products, arithmetic and copies ran while one was open for 2% -> 2% of each run, Pallas kernels for 9% -> 9%
where the time goes in v6:
time: 117 us; the launch traced here: 116 us
  waiting for transfers between devices  47.5 us (41%)
  starting transfers between devices  45.3 us (39%)
  Pallas kernels  14.5 us (12%)
  local copies, waits for them, and re-layouts  5.31 us (5%)
  other arithmetic  3.05 us (3%)
    ppermute x42, waiting for transfers between devices, swap(): return lax.ppermute(rows, axis, [(i, i ^ mask) for i in range(count)])  46.1 us
    ppermute x42, starting transfers between devices, swap(): return lax.ppermute(rows, axis, [(i, i ^ mask) for i in range(count)])  39.5 us
    pallas_call x10, Pallas kernels, local_kernel(): pl.pallas_call(body, out_shape=list(outs), in_specs=[pl.BlockSpec(memory_...  13.9 us
    all_to_all x1, starting transfers between devices, shards(): lax.all_to_all(leaving, 'dp', split_axis=0, concat_axis=0, tiled=True)  5.82 us
    unnamed x28, local copies, waits for them, and re-layouts  4.98 us
  transfers between devices with their start and end apart: 43, of which 26 were waited for; matrix products, arithmetic and copies ran while one was open for 2% of the time, Pallas kernels for 9%

profile of v6, /device:TPU:0, one launch (start us, length us, event | category | flops | bytes accessed | tf_op | source)
XLA Modules:
  0.0 116.3 jit_solution(16572932445414959493)
XLA Ops:
  0.0 3.0 %collective-permute-start = (bf16[32,4608]{1,0:T(8,128)(2,1)}, bf16[32,4608]{1,0:T(8,128)(2,1)S(1)}, u32[]{:S(2)}, u32[]{:S(2)}) collective-permute-start(bf16[32,4608]{1,0:T(8,128)(2,1)} %refs_2_.1), channel_id=1, source_target_pairs={{0,2},{1,3},{2,0},{3,1},{4,6},{5,7},{6,4},{7,5},{8,10},{9,11},{10,... | collective-permute-start | bytes 884744 | tf_op jit(solution)/shard_map/ppermute | solution.py:22
  3.0 0.7 pad_add_fusion.1
  3.7 2.0 %collective-permute-start.2 = (s32[32]{0:T(128)}, s32[32]{0:T(128)S(1)}, u32[]{:S(2)}, u32[]{:S(2)}) collective-permute-start(s32[32]{0:T(128)} %param.16), channel_id=1, source_target_pairs={{0,2},{1,3},{2,0},{3,1},{4,6},{5,7},{6,4},{7,5},{8,10},{9,11},{10,... | collective-permute-start | bytes 392 | tf_op jit(solution)/shard_map/ppermute | solution.py:22
  5.7 2.3 %copy-done.3 = bf16[4608,512]{1,0:T(8,128)(2,1)S(1)} copy-done((bf16[4608,512]{1,0:T(8,128)(2,1)S(1)}, bf16[4608,512]{1,0:T(8,128)(2,1)}, u32[]{:S(2)}) %copy-start.3) | copy-done | bytes 4718616
  8.0 1.6 %copy-done.7 = bf16[512,2048]{1,0:T(8,128)(2,1)S(1)} copy-done((bf16[512,2048]{1,0:T(8,128)(2,1)S(1)}, bf16[512,2048]{1,0:T(8,128)(2,1)}, u32[]{:S(2)}) %copy-start.7) | copy-done | bytes 2097176
  9.6 1.0 copy-done.8
  10.6 0.5 shard_map.136
  11.3 1.6 %collective-permute-done.4.refs_3_ = bf16[32,4608]{1,0:T(8,128)(2,1)S(1)} collective-permute-done((bf16[32,4608]{1,0:T(8,128)(2,1)S(1)}, bf16[32,4608]{1,0:T(8,128)(2,1)S(1)}, u32[]{:S(2)}, u32[]{:S(2)}) %collective-permute-start.4) | collective-permute-done | bytes 294944 | tf_op jit(solution)/shard_map/ppermute | solution.py:22
  12.8 1.2 %shard_map.137 = (bf16[64,2048]{1,0:T(8,128)(2,1)S(1)}, bf16[64,2048]{1,0:T(8,128)(2,1)S(1)}) custom-call(bf16[32,4608]{1,0:T(8,128)(2,1)S(1)} %get-tuple-element.84.refs_0_, bf16[32,4608]{1,0:T(8,128)(2,1)S(1)} %collective-permute-done.refs_1_, bf16[32,4608]{1,0:T(8,128)(2,1)S(1)} %collective-permute-done.1.refs_2_, ...), custom_call_target="tpu_custom_call" | custom-call | flops 872415232 | bytes 8519680 | tf_op jit(solution)/shard_map/pallas_call | solution.py:68
  14.6 1.1 collective-permute-done.5.other_ref
  15.7 1.0 shard_map.138
  16.7 5.8 %all-to-all-start = ((bf16[8,8,2176]{2,1,0:T(8,128)(2,1)}), bf16[8,8,2176]{2,1,0:T(8,128)(2,1)S(1)}, u32[]{:S(2)}, u32[]{:S(2)}) async-start(bf16[8,8,2176]{2,1,0:T(8,128)(2,1)} %shard_map.138), calls=%async_computation | async-start | bytes 557056 | tf_op jit(solution)/shard_map/all_to_all | solution.py:399
  22.5 0.9 collective-permute-start.6
  23.5 0.5 collective-permute-start.8
  24.0 0.6 collective-permute-done.7
  24.8 5.8 %collective-permute-done.6.refs_3_ = bf16[64,2048]{1,0:T(8,128)(2,1)S(1)} collective-permute-done((bf16[64,2048]{1,0:T(8,128)(2,1)S(1)}, bf16[64,2048]{1,0:T(8,128)(2,1)S(1)}, u32[]{:S(2)}, u32[]{:S(2)}) %collective-permute-start.6) | collective-permute-done | bytes 262176 | tf_op jit(solution)/shard_map/ppermute | solution.py:22
  30.6 1.4 %all-to-all-done.refs_0_ = bf16[8,8,2176]{2,1,0:T(8,128)(2,1)S(1)} async-done(((bf16[8,8,2176]{2,1,0:T(8,128)(2,1)}), bf16[8,8,2176]{2,1,0:T(8,128)(2,1)S(1)}, u32[]{:S(2)}, u32[]{:S(2)}) %all-to-all-start) | async-done | bytes 278560 | tf_op jit(solution)/shard_map/all_to_all | solution.py:399
  32.0 0.9 collective-permute-start.9
  33.3 5.5 %collective-permute-done.9.refs_1_ = bf16[8,8,2176]{2,1,0:T(8,128)(2,1)S(1)} collective-permute-done((bf16[8,8,2176]{2,1,0:T(8,128)(2,1)S(1)}, bf16[8,8,2176]{2,1,0:T(8,128)(2,1)S(1)}, u32[]{:S(2)}, u32[]{:S(2)}) %collective-permute-start.9) | collective-permute-done | bytes 278560 | tf_op jit(solution)/shard_map/ppermute | solution.py:22
  38.8 0.7 shard_map.139
  39.8 1.8 %collective-permute-done.10.refs_2_.refs_1_ = bf16[128,2048]{1,0:T(8,128)(2,1)S(1)} collective-permute-done((bf16[128,2048]{1,0:T(8,128)(2,1)S(1)}, bf16[128,2048]{1,0:T(8,128)(2,1)S(1)}, u32[]{:S(2)}, u32[]{:S(2)}) %collective-permute-start.10) | collective-permute-done | bytes 524320 | tf_op jit(solution)/shard_map/ppermute | solution.py:22
  41.5 0.5 shard_map.140
  42.0 2.6 %collective-permute-start.12 = (bf16[24,2048]{1,0:T(8,128)(2,1)S(1)}, bf16[24,2048]{1,0:T(8,128)(2,1)S(1)}, u32[]{:S(2)}, u32[]{:S(2)}) collective-permute-start(bf16[24,2048]{1,0:T(8,128)(2,1)S(1)} %get-tuple-element.109), channel_id=1, source_target_pairs={{0,20},{4,16},{8,28},{12,24},{16,4},{20,0},{24,12},{28,8},{1,21},{... | collective-permute-start | bytes 294920 | tf_op jit(solution)/shard_map/ppermute | solution.py:22
  44.6 1.1 collective-permute-start.11
  45.7 0.8 collective-permute-start.14
  46.5 0.8 collective-permute-start.15
  47.3 1.8 %collective-permute-start.16 = (bf16[48,2048]{1,0:T(8,128)(2,1)S(1)}, bf16[48,2048]{1,0:T(8,128)(2,1)S(1)}, u32[]{:S(2)}, u32[]{:S(2)}) collective-permute-start(bf16[48,2048]{1,0:T(8,128)(2,1)S(1)} %get-tuple-element.113), channel_id=1, source_target_pairs={{0,12},{4,8},{8,4},{12,0},{16,28},{20,24},{24,20},{28,16},{1,13},{... | collective-permute-start | bytes 589832 | tf_op jit(solution)/shard_map/ppermute | solution.py:22
  49.2 4.2 %collective-permute-done.12 = bf16[24,2048]{1,0:T(8,128)(2,1)S(1)} collective-permute-done((bf16[24,2048]{1,0:T(8,128)(2,1)S(1)}, bf16[24,2048]{1,0:T(8,128)(2,1)S(1)}, u32[]{:S(2)}, u32[]{:S(2)}) %collective-permute-start.12) | collective-permute-done | bytes 98336 | tf_op jit(solution)/shard_map/ppermute | solution.py:22
  53.4 1.4 %collective-permute-done.11 = bf16[24,2048]{1,0:T(8,128)(2,1)S(1)} collective-permute-done((bf16[24,2048]{1,0:T(8,128)(2,1)S(1)}, bf16[24,2048]{1,0:T(8,128)(2,1)S(1)}, u32[]{:S(2)}, u32[]{:S(2)}) %collective-permute-start.11) | collective-permute-done | bytes 98336 | tf_op jit(solution)/shard_map/ppermute | solution.py:22
  54.8 0.9 collective-permute-start.13
  55.8 2.9 %collective-permute-start.17 = (bf16[24,2048]{1,0:T(8,128)(2,1)S(1)}, bf16[24,2048]{1,0:T(8,128)(2,1)S(1)}, u32[]{:S(2)}, u32[]{:S(2)}) collective-permute-start(bf16[24,2048]{1,0:T(8,128)(2,1)S(1)} %get-tuple-element.117), channel_id=1, source_target_pairs={{0,24},{4,28},{8,16},{12,20},{16,8},{20,12},{24,0},{28,4},{1,25},{... | collective-permute-start | bytes 294920 | tf_op jit(solution)/shard_map/ppermute | solution.py:22
  58.6 1.3 %collective-permute-start.18 = (bf16[24,2048]{1,0:T(8,128)(2,1)S(1)}, bf16[24,2048]{1,0:T(8,128)(2,1)S(1)}, u32[]{:S(2)}, u32[]{:S(2)}) collective-permute-start(bf16[24,2048]{1,0:T(8,128)(2,1)S(1)} %get-tuple-element.118), channel_id=1, source_target_pairs={{0,28},{4,24},{8,20},{12,16},{16,12},{20,8},{24,4},{28,0},{1,29},{... | collective-permute-start | bytes 294920 | tf_op jit(solution)/shard_map/ppermute | solution.py:22
  60.0 3.4 %collective-permute-done.16 = bf16[48,2048]{1,0:T(8,128)(2,1)S(1)} collective-permute-done((bf16[48,2048]{1,0:T(8,128)(2,1)S(1)}, bf16[48,2048]{1,0:T(8,128)(2,1)S(1)}, u32[]{:S(2)}, u32[]{:S(2)}) %collective-permute-start.16) | collective-permute-done | bytes 196640 | tf_op jit(solution)/shard_map/ppermute | solution.py:22
  63.4 2.5 %collective-permute-done.18 = bf16[24,2048]{1,0:T(8,128)(2,1)S(1)} collective-permute-done((bf16[24,2048]{1,0:T(8,128)(2,1)S(1)}, bf16[24,2048]{1,0:T(8,128)(2,1)S(1)}, u32[]{:S(2)}, u32[]{:S(2)}) %collective-permute-start.18) | collective-permute-done | bytes 98336 | tf_op jit(solution)/shard_map/ppermute | solution.py:22
  66.0 1.2 %collective-permute-start.19 = (bf16[48,2048]{1,0:T(8,128)(2,1)S(1)}, bf16[48,2048]{1,0:T(8,128)(2,1)S(1)}, u32[]{:S(2)}, u32[]{:S(2)}) collective-permute-start(bf16[48,2048]{1,0:T(8,128)(2,1)S(1)} %constant_dynamic-update-slice_fusion.refs_0_), channel_id=1, source_target_pairs={{0,2},{1,3},{2,0},{3,1},{4,6},{5,7},{6,4},{7,5},{8,10},{9,11},{10,... | collective-permute-start | bytes 589832 | tf_op jit(solution)/shard_map/ppermute | solution.py:22
  67.2 0.5 collective-permute-start.21
  67.8 0.9 collective-permute-done.20.refs_2_
  68.9 1.6 %shard_map.141 = (bf16[96,2048]{1,0:T(8,128)(2,1)S(1)}, bf16[96,2048]{1,0:T(8,128)(2,1)S(1)}) custom-call(bf16[48,2048]{1,0:T(8,128)(2,1)S(1)} %pad_maximum_fusion.1.refs_0_, bf16[48,2048]{1,0:T(8,128)(2,1)S(1)} %collective-permute-done.13.refs_1_, bf16[48,2048]{1,0:T(8,128)(2,1)S(1)} %collective-permute-done.20.refs_2_, ...), custom_call_target="tpu_custom_call" | custom-call | flops 830472192 | bytes 5898240 | tf_op jit(solution)/shard_map/pallas_call | solution.py:68
  70.6 1.1 collective-permute-done.19.refs_1_
  71.8 0.6 collective-permute-start.24
  72.7 0.5 collective-permute-start.26
  73.6 1.2 %collective-permute-start.23 = (bf16[48,2048]{1,0:T(8,128)(2,1)S(1)}, bf16[48,2048]{1,0:T(8,128)(2,1)S(1)}, u32[]{:S(2)}, u32[]{:S(2)}) collective-permute-start(bf16[48,2048]{1,0:T(8,128)(2,1)S(1)} %slice.119), channel_id=1, source_target_pairs={{0,2},{1,3},{2,0},{3,1},{4,6},{5,7},{6,4},{7,5},{8,10},{9,11},{10,... | collective-permute-start | bytes 589832 | tf_op jit(solution)/shard_map/ppermute | solution.py:22
  75.1 1.6 %shard_map.142 = (bf16[96,2048]{1,0:T(8,128)(2,1)S(1)}, bf16[96,2048]{1,0:T(8,128)(2,1)S(1)}) custom-call(bf16[48,2048]{1,0:T(8,128)(2,1)S(1)} %constant_dynamic-update-slice_fusion.refs_0_, bf16[48,2048]{1,0:T(8,128)(2,1)S(1)} %collective-permute-done.19.refs_1_, bf16[48,2048]{1,0:T(8,128)(2,1)S(1)} %collective-permute-done.25.refs_2_, ...), custom_call_target="tpu_custom_call" | custom-call | flops 830472192 | bytes 5898240 | tf_op jit(solution)/shard_map/pallas_call | solution.py:68
  77.0 3.2 %shard_map.143 = (bf16[192,2048]{1,0:T(8,128)(2,1)S(1)}, bf16[192,2048]{1,0:T(8,128)(2,1)S(1)}) custom-call(bf16[192,2048]{1,0:T(8,128)(2,1)S(1)} %constant_dynamic-update-slice_fusion.2.refs_0_, bf16[192,2048]{1,0:T(8,128)(2,1)S(1)} %collective-permute-done.24.refs_1_, bf16[352,2048]{1,0:T(8,128)(2,1)S(1)} %bitcast.21, bf16[352,2048]{1,0:T(8,128)(2,1)S(1)} %bitcast.24, ...), custom_call_target="tpu_custom_call" | custom-call | flops 1660944384 | bytes 7471104 | tf_op jit(solution)/shard_map/pallas_call | solution.py:68
  80.9 1.2 %collective-permute-start.31 = (bf16[48,2048]{1,0:T(8,128)(2,1)S(1)}, bf16[48,2048]{1,0:T(8,128)(2,1)S(1)}, u32[]{:S(2)}, u32[]{:S(2)}) collective-permute-start(bf16[48,2048]{1,0:T(8,128)(2,1)S(1)} %slice.132), channel_id=1, source_target_pairs={{0,2},{1,3},{2,0},{3,1},{4,6},{5,7},{6,4},{7,5},{8,10},{9,11},{10,... | collective-permute-start | bytes 589832 | tf_op jit(solution)/shard_map/ppermute | solution.py:22
  82.1 0.8 collective-permute-start.34
  82.9 2.3 %collective-permute-start.35 = (bf16[24,2048]{1,0:T(8,128)(2,1)S(1)}, bf16[24,2048]{1,0:T(8,128)(2,1)S(1)}, u32[]{:S(2)}, u32[]{:S(2)}) collective-permute-start(bf16[24,2048]{1,0:T(8,128)(2,1)S(1)} %get-tuple-element.160), channel_id=1, source_target_pairs={{0,20},{4,16},{8,28},{12,24},{16,4},{20,0},{24,12},{28,8},{1,21},{... | collective-permute-start | bytes 294920 | tf_op jit(solution)/shard_map/ppermute | solution.py:22
  85.5 0.9 collective-permute-start.29
  86.5 2.1 %collective-permute-done.31 = bf16[48,2048]{1,0:T(8,128)(2,1)S(1)} collective-permute-done((bf16[48,2048]{1,0:T(8,128)(2,1)S(1)}, bf16[48,2048]{1,0:T(8,128)(2,1)S(1)}, u32[]{:S(2)}, u32[]{:S(2)}) %collective-permute-start.31) | collective-permute-done | bytes 196640 | tf_op jit(solution)/shard_map/ppermute | solution.py:22
  89.0 3.4 %collective-permute-done.29 = bf16[48,2048]{1,0:T(8,128)(2,1)S(1)} collective-permute-done((bf16[48,2048]{1,0:T(8,128)(2,1)S(1)}, bf16[48,2048]{1,0:T(8,128)(2,1)S(1)}, u32[]{:S(2)}, u32[]{:S(2)}) %collective-permute-start.29) | collective-permute-done | bytes 196640 | tf_op jit(solution)/shard_map/ppermute | solution.py:22
  92.5 1.0 collective-permute-start.32
  93.6 1.4 %collective-permute-start.33 = (bf16[24,2048]{1,0:T(8,128)(2,1)S(1)}, bf16[24,2048]{1,0:T(8,128)(2,1)S(1)}, u32[]{:S(2)}, u32[]{:S(2)}) collective-permute-start(bf16[24,2048]{1,0:T(8,128)(2,1)S(1)} %get-tuple-element.162), channel_id=1, source_target_pairs={{0,12},{4,8},{8,4},{12,0},{16,28},{20,24},{24,20},{28,16},{1,13},{... | collective-permute-start | bytes 294920 | tf_op jit(solution)/shard_map/ppermute | solution.py:22
  95.0 2.3 %collective-permute-start.36 = (bf16[24,2048]{1,0:T(8,128)(2,1)S(1)}, bf16[24,2048]{1,0:T(8,128)(2,1)S(1)}, u32[]{:S(2)}, u32[]{:S(2)}) collective-permute-start(bf16[24,2048]{1,0:T(8,128)(2,1)S(1)} %get-tuple-element.159), channel_id=1, source_target_pairs={{0,24},{4,28},{8,16},{12,20},{16,8},{20,12},{24,0},{28,4},{1,25},{... | collective-permute-start | bytes 294920 | tf_op jit(solution)/shard_map/ppermute | solution.py:22
  97.3 2.1 %collective-permute-start.37 = (bf16[24,2048]{1,0:T(8,128)(2,1)S(1)}, bf16[24,2048]{1,0:T(8,128)(2,1)S(1)}, u32[]{:S(2)}, u32[]{:S(2)}) collective-permute-start(bf16[24,2048]{1,0:T(8,128)(2,1)S(1)} %get-tuple-element.158), channel_id=1, source_target_pairs={{0,28},{4,24},{8,20},{12,16},{16,12},{20,8},{24,4},{28,0},{1,29},{... | collective-permute-start | bytes 294920 | tf_op jit(solution)/shard_map/ppermute | solution.py:22
  99.4 2.6 %shard_map.144 = (f32[128,2048]{1,0:T(8,128)S(1)}, f32[128,2048]{1,0:T(8,128)S(1)}) custom-call(bf16[128,2048]{1,0:T(8,128)(2,1)S(1)} %get-tuple-element.138.refs_1_.refs_0_, bf16[128,2048]{1,0:T(8,128)(2,1)S(1)} %collective-permute-done.10.refs_2_.refs_1_, bf16[704,2048]{1,0:T(8,128)(2,1)S(1)} %bitcast.28, bf16[704,2048]{1,0:T(8,128)(2,1)S(1)} %bitcast.29, ...), custom_call_target="tpu_custom_call" | custom-call | flops 2214592512 | bytes 11796480 | tf_op jit(solution)/shard_map/pallas_call | solution.py:68
  102.3 2.3 %collective-permute-done.37.refs_9_ = bf16[24,2048]{1,0:T(8,128)(2,1)S(1)} collective-permute-done((bf16[24,2048]{1,0:T(8,128)(2,1)S(1)}, bf16[24,2048]{1,0:T(8,128)(2,1)S(1)}, u32[]{:S(2)}, u32[]{:S(2)}) %collective-permute-start.37) | collective-permute-done | bytes 98336 | tf_op jit(solution)/shard_map/ppermute | solution.py:22
  104.7 0.7 shard_map.146
  105.5 0.5 collective-permute-start.38
  106.0 0.7 shard_map.145
  107.1 1.1 collective-permute-start.41
  108.3 1.0 collective-permute-start.39
  109.3 4.2 %collective-permute-done.41 = bf16[64,1024]{1,0:T(8,128)(2,1)S(1)} collective-permute-done((bf16[64,1024]{1,0:T(8,128)(2,1)S(1)}, bf16[64,1024]{1,0:T(8,128)(2,1)S(1)}, u32[]{:S(2)}, u32[]{:S(2)}) %collective-permute-start.41) | collective-permute-done | bytes 131104 | tf_op jit(solution)/shard_map/ppermute | solution.py:22
  113.5 2.0 %collective-permute-done.39 = bf16[64,1024]{1,0:T(8,128)(2,1)S(1)} collective-permute-done((bf16[64,1024]{1,0:T(8,128)(2,1)S(1)}, bf16[64,1024]{1,0:T(8,128)(2,1)S(1)}, u32[]{:S(2)}, u32[]{:S(2)}) %collective-permute-start.39) | collective-permute-done | bytes 131104 | tf_op jit(solution)/shard_map/ppermute | solution.py:22
  115.5 0.8 add_convert_fusion.3
  (106 shorter events, 5.5 us)
Async XLA Ops:
  0.0 11.2 %collective-permute-start = (bf16[32,4608]{1,0:T(8,128)(2,1)}, bf16[32,4608]{1,0:T(8,128)(2,1)S(1)}, u32[]{:S(2)}, u32[]{:S(2)}) collective-permute-start(bf16[32,4608]{1,0:T(8,128)(2,1)} %refs_2_.1), channel_id=1, source_target_pairs={{0,2},{1,3},{2,0},{3,1},{4,6},{5,7},{6,4},{7,5},{8,10},{9,11},{10,... | collective-permute-start | bytes 884744 | tf_op jit(solution)/shard_map/ppermute | solution.py:22
  3.0 8.2 %collective-permute-start.1 = (bf16[32,4608]{1,0:T(8,128)(2,1)}, bf16[32,4608]{1,0:T(8,128)(2,1)S(1)}, u32[]{:S(2)}, u32[]{:S(2)}) collective-permute-start(bf16[32,4608]{1,0:T(8,128)(2,1)} %refs_2_.1), channel_id=1, source_target_pairs={{0,1},{1,0},{2,3},{3,2},{4,5},{5,4},{6,7},{7,6},{8,9},{9,8},{10,11... | collective-permute-start | bytes 884744 | tf_op jit(solution)/shard_map/ppermute | solution.py:22
  3.7 7.5 %collective-permute-start.3 = (s32[64,4]{0,1:T(4,128)S(1)}, s32[64,4]{0,1:T(4,128)S(1)}, u32[]{:S(2)}, u32[]{:S(2)}) collective-permute-start(s32[64,4]{0,1:T(4,128)S(1)} %pad_add_fusion.1), channel_id=1, source_target_pairs={{0,2},{1,3},{2,0},{3,1},{4,6},{5,7},{6,4},{7,5},{8,10},{9,11},{10,... | collective-permute-start | bytes 3080 | tf_op jit(solution)/shard_map/ppermute | solution.py:22
  3.7 7.5 %collective-permute-start.2 = (s32[32]{0:T(128)}, s32[32]{0:T(128)S(1)}, u32[]{:S(2)}, u32[]{:S(2)}) collective-permute-start(s32[32]{0:T(128)} %param.16), channel_id=1, source_target_pairs={{0,2},{1,3},{2,0},{3,1},{4,6},{5,7},{6,4},{7,5},{8,10},{9,11},{10,... | collective-permute-start | bytes 392 | tf_op jit(solution)/shard_map/ppermute | solution.py:22
  5.7 2.3 %copy-start.3 = (bf16[4608,512]{1,0:T(8,128)(2,1)S(1)}, bf16[4608,512]{1,0:T(8,128)(2,1)}, u32[]{:S(2)}) copy-start(bf16[4608,512]{1,0:T(8,128)(2,1)} %refs_0_.1) | copy-start | bytes 14155780
  8.0 1.6 %copy-start.7 = (bf16[512,2048]{1,0:T(8,128)(2,1)S(1)}, bf16[512,2048]{1,0:T(8,128)(2,1)}, u32[]{:S(2)}) copy-start(bf16[512,2048]{1,0:T(8,128)(2,1)} %refs_1_.1) | copy-start | bytes 6291460
  9.6 1.0 copy-start.8
  11.2 1.6 %collective-permute-start.4 = (bf16[32,4608]{1,0:T(8,128)(2,1)S(1)}, bf16[32,4608]{1,0:T(8,128)(2,1)S(1)}, u32[]{:S(2)}, u32[]{:S(2)}) collective-permute-start(bf16[32,4608]{1,0:T(8,128)(2,1)S(1)} %collective-permute-done.refs_1_), channel_id=1, source_target_pairs={{0,1},{1,0},{2,3},{3,2},{4,5},{5,4},{6,7},{7,6},{8,9},{9,8},{10,11... | collective-permute-start | bytes 884744 | tf_op jit(solution)/shard_map/ppermute | solution.py:22
  12.8 1.4 %copy-start.11 = (s32[32]{0:T(128)S(1)}, s32[32]{0:T(128)}, u32[]{:S(2)}) copy-start(s32[32]{0:T(128)} %param.16) | copy-start | bytes 388
  12.8 9.7 %copy-start.9 = (bf16[64,2048]{1,0:T(8,128)(2,1)S(1)}, bf16[64,2048]{1,0:T(8,128)(2,1)}, u32[]{:S(2)}) copy-start(bf16[64,2048]{1,0:T(8,128)(2,1)} %refs_2_.2) | copy-start | bytes 786436
  12.8 26.0 %copy-start.10 = (f32[2048]{0:T(1024)S(1)}, f32[2048]{0:T(1024)}, u32[]{:S(2)}) copy-start(f32[2048]{0:T(1024)} %param.19) | copy-start | bytes 24580
  14.1 1.6 %collective-permute-start.5 = (bf16[64,2048]{1,0:T(8,128)(2,1)S(1)}, bf16[64,2048]{1,0:T(8,128)(2,1)S(1)}, u32[]{:S(2)}, u32[]{:S(2)}) collective-permute-start(bf16[64,2048]{1,0:T(8,128)(2,1)S(1)} %get-tuple-element.92), channel_id=1, source_target_pairs={{0,1},{1,0},{2,3},{3,2},{4,5},{5,4},{6,7},{7,6},{8,9},{9,8},{10,11... | collective-permute-start | bytes 786440 | tf_op jit(solution)/shard_map/ppermute | solution.py:22
  16.7 15.3 %all-to-all-start = ((bf16[8,8,2176]{2,1,0:T(8,128)(2,1)}), bf16[8,8,2176]{2,1,0:T(8,128)(2,1)S(1)}, u32[]{:S(2)}, u32[]{:S(2)}) async-start(bf16[8,8,2176]{2,1,0:T(8,128)(2,1)} %shard_map.138), calls=%async_computation | async-start | bytes 557056 | tf_op jit(solution)/shard_map/all_to_all | solution.py:399
  22.5 8.1 %collective-permute-start.6 = (bf16[64,2048]{1,0:T(8,128)(2,1)S(1)}, bf16[64,2048]{1,0:T(8,128)(2,1)S(1)}, u32[]{:S(2)}, u32[]{:S(2)}) collective-permute-start(bf16[64,2048]{1,0:T(8,128)(2,1)S(1)} %copy-done.9), channel_id=1, source_target_pairs={{0,2},{1,3},{2,0},{3,1},{4,6},{5,7},{6,4},{7,5},{8,10},{9,11},{10,... | collective-permute-start | bytes 786440 | tf_op jit(solution)/shard_map/ppermute | solution.py:22
  23.5 1.2 collective-permute-start.7
  23.5 1.3 %collective-permute-start.8 = (s32[64,4]{0,1:T(4,128)S(1)}, s32[64,4]{0,1:T(4,128)S(1)}, u32[]{:S(2)}, u32[]{:S(2)}) collective-permute-start(s32[64,4]{0,1:T(4,128)S(1)} %collective-permute-done.3), channel_id=1, source_target_pairs={{0,1},{1,0},{2,3},{3,2},{4,5},{5,4},{6,7},{7,6},{8,9},{9,8},{10,11... | collective-permute-start | bytes 3080 | tf_op jit(solution)/shard_map/ppermute | solution.py:22
  32.0 6.8 %collective-permute-start.9 = (bf16[8,8,2176]{2,1,0:T(8,128)(2,1)S(1)}, bf16[8,8,2176]{2,1,0:T(8,128)(2,1)S(1)}, u32[]{:S(2)}, u32[]{:S(2)}) collective-permute-start(bf16[8,8,2176]{2,1,0:T(8,128)(2,1)S(1)} %all-to-all-done.refs_0_), channel_id=1, source_target_pairs={{0,2},{1,3},{2,0},{3,1},{4,6},{5,7},{6,4},{7,5},{8,10},{9,11},{10,... | collective-permute-start | bytes 835592 | tf_op jit(solution)/shard_map/ppermute | solution.py:22
  38.8 30.1 %copy-start = (bf16[1,2048,352]{1,2,0:T(8,128)(2,1)S(1)}, bf16[1,2048,352]{1,2,0:T(8,128)(2,1)}, u32[]{:S(2)}) copy-start(bf16[1,2048,352]{1,2,0:T(8,128)(2,1)} %param.23) | copy-start | bytes 4325380
  38.8 30.1 %copy-start.1 = (bf16[1,2048,352]{1,2,0:T(8,128)(2,1)S(1)}, bf16[1,2048,352]{1,2,0:T(8,128)(2,1)}, u32[]{:S(2)}) copy-start(bf16[1,2048,352]{1,2,0:T(8,128)(2,1)} %param.24) | copy-start | bytes 4325380
  38.8 30.1 %copy-start.2 = (bf16[1,352,2048]{2,1,0:T(8,128)(2,1)S(1)}, bf16[1,352,2048]{2,1,0:T(8,128)(2,1)}, u32[]{:S(2)}) copy-start(bf16[1,352,2048]{2,1,0:T(8,128)(2,1)} %param.25) | copy-start | bytes 4325380
  39.6 2.0 %collective-permute-start.10 = (bf16[128,2048]{1,0:T(8,128)(2,1)S(1)}, bf16[128,2048]{1,0:T(8,128)(2,1)S(1)}, u32[]{:S(2)}, u32[]{:S(2)}) collective-permute-start(bf16[128,2048]{1,0:T(8,128)(2,1)S(1)} %get-tuple-element.138.refs_1_.refs_0_), channel_id=1, source_target_pairs={{0,1},{1,0},{2,3},{3,2},{4,5},{5,4},{6,7},{7,6},{8,9},{9,8},{10,11... | collective-permute-start | bytes 1572872 | tf_op jit(solution)/shard_map/ppermute | solution.py:22
  42.0 11.3 %collective-permute-start.12 = (bf16[24,2048]{1,0:T(8,128)(2,1)S(1)}, bf16[24,2048]{1,0:T(8,128)(2,1)S(1)}, u32[]{:S(2)}, u32[]{:S(2)}) collective-permute-start(bf16[24,2048]{1,0:T(8,128)(2,1)S(1)} %get-tuple-element.109), channel_id=1, source_target_pairs={{0,20},{4,16},{8,28},{12,24},{16,4},{20,0},{24,12},{28,8},{1,21},{... | collective-permute-start | bytes 294920 | tf_op jit(solution)/shard_map/ppermute | solution.py:22
  44.6 10.2 %collective-permute-start.11 = (bf16[24,2048]{1,0:T(8,128)(2,1)S(1)}, bf16[24,2048]{1,0:T(8,128)(2,1)S(1)}, u32[]{:S(2)}, u32[]{:S(2)}) collective-permute-start(bf16[24,2048]{1,0:T(8,128)(2,1)S(1)} %get-tuple-element.108), channel_id=1, source_target_pairs={{0,16},{4,20},{8,24},{12,28},{16,0},{20,4},{24,8},{28,12},{1,17},{... | collective-permute-start | bytes 294920 | tf_op jit(solution)/shard_map/ppermute | solution.py:22
  45.7 13.0 %collective-permute-start.14 = (bf16[48,2048]{1,0:T(8,128)(2,1)S(1)}, bf16[48,2048]{1,0:T(8,128)(2,1)S(1)}, u32[]{:S(2)}, u32[]{:S(2)}) collective-permute-start(bf16[48,2048]{1,0:T(8,128)(2,1)S(1)} %get-tuple-element.111), channel_id=1, source_target_pairs={{0,4},{4,0},{8,12},{12,8},{16,20},{20,16},{24,28},{28,24},{1,5},{5... | collective-permute-start | bytes 589832 | tf_op jit(solution)/shard_map/ppermute | solution.py:22
  46.5 13.5 %collective-permute-start.15 = (bf16[48,2048]{1,0:T(8,128)(2,1)S(1)}, bf16[48,2048]{1,0:T(8,128)(2,1)S(1)}, u32[]{:S(2)}, u32[]{:S(2)}) collective-permute-start(bf16[48,2048]{1,0:T(8,128)(2,1)S(1)} %get-tuple-element.112), channel_id=1, source_target_pairs={{0,8},{4,12},{8,0},{12,4},{16,24},{20,28},{24,16},{28,20},{1,9},{5... | collective-permute-start | bytes 589832 | tf_op jit(solution)/shard_map/ppermute | solution.py:22
  47.3 16.1 %collective-permute-start.16 = (bf16[48,2048]{1,0:T(8,128)(2,1)S(1)}, bf16[48,2048]{1,0:T(8,128)(2,1)S(1)}, u32[]{:S(2)}, u32[]{:S(2)}) collective-permute-start(bf16[48,2048]{1,0:T(8,128)(2,1)S(1)} %get-tuple-element.113), channel_id=1, source_target_pairs={{0,12},{4,8},{8,4},{12,0},{16,28},{20,24},{24,20},{28,16},{1,13},{... | collective-permute-start | bytes 589832 | tf_op jit(solution)/shard_map/ppermute | solution.py:22
  54.8 11.1 %collective-permute-start.13 = (bf16[48,2048]{1,0:T(8,128)(2,1)S(1)}, bf16[48,2048]{1,0:T(8,128)(2,1)S(1)}, u32[]{:S(2)}, u32[]{:S(2)}) collective-permute-start(bf16[48,2048]{1,0:T(8,128)(2,1)S(1)} %pad_maximum_fusion.1.refs_0_), channel_id=1, source_target_pairs={{0,2},{1,3},{2,0},{3,1},{4,6},{5,7},{6,4},{7,5},{8,10},{9,11},{10,... | collective-permute-start | bytes 589832 | tf_op jit(solution)/shard_map/ppermute | solution.py:22
  55.8 7.7 %collective-permute-start.17 = (bf16[24,2048]{1,0:T(8,128)(2,1)S(1)}, bf16[24,2048]{1,0:T(8,128)(2,1)S(1)}, u32[]{:S(2)}, u32[]{:S(2)}) collective-permute-start(bf16[24,2048]{1,0:T(8,128)(2,1)S(1)} %get-tuple-element.117), channel_id=1, source_target_pairs={{0,24},{4,28},{8,16},{12,20},{16,8},{20,12},{24,0},{28,4},{1,25},{... | collective-permute-start | bytes 294920 | tf_op jit(solution)/shard_map/ppermute | solution.py:22
  58.6 7.3 %collective-permute-start.18 = (bf16[24,2048]{1,0:T(8,128)(2,1)S(1)}, bf16[24,2048]{1,0:T(8,128)(2,1)S(1)}, u32[]{:S(2)}, u32[]{:S(2)}) collective-permute-start(bf16[24,2048]{1,0:T(8,128)(2,1)S(1)} %get-tuple-element.118), channel_id=1, source_target_pairs={{0,28},{4,24},{8,20},{12,16},{16,12},{20,8},{24,4},{28,0},{1,29},{... | collective-permute-start | bytes 294920 | tf_op jit(solution)/shard_map/ppermute | solution.py:22
  66.0 5.7 %collective-permute-start.19 = (bf16[48,2048]{1,0:T(8,128)(2,1)S(1)}, bf16[48,2048]{1,0:T(8,128)(2,1)S(1)}, u32[]{:S(2)}, u32[]{:S(2)}) collective-permute-start(bf16[48,2048]{1,0:T(8,128)(2,1)S(1)} %constant_dynamic-update-slice_fusion.refs_0_), channel_id=1, source_target_pairs={{0,2},{1,3},{2,0},{3,1},{4,6},{5,7},{6,4},{7,5},{8,10},{9,11},{10,... | collective-permute-start | bytes 589832 | tf_op jit(solution)/shard_map/ppermute | solution.py:22
  67.2 1.4 %collective-permute-start.20 = (bf16[48,2048]{1,0:T(8,128)(2,1)S(1)}, bf16[48,2048]{1,0:T(8,128)(2,1)S(1)}, u32[]{:S(2)}, u32[]{:S(2)}) collective-permute-start(bf16[48,2048]{1,0:T(8,128)(2,1)S(1)} %pad_maximum_fusion.1.refs_0_), channel_id=1, source_target_pairs={{0,1},{1,0},{2,3},{3,2},{4,5},{5,4},{6,7},{7,6},{8,9},{9,8},{10,11... | collective-permute-start | bytes 589832 | tf_op jit(solution)/shard_map/ppermute | solution.py:22
  67.2 1.7 %collective-permute-start.21 = (bf16[48,2048]{1,0:T(8,128)(2,1)S(1)}, bf16[48,2048]{1,0:T(8,128)(2,1)S(1)}, u32[]{:S(2)}, u32[]{:S(2)}) collective-permute-start(bf16[48,2048]{1,0:T(8,128)(2,1)S(1)} %collective-permute-done.13.refs_1_), channel_id=1, source_target_pairs={{0,1},{1,0},{2,3},{3,2},{4,5},{5,4},{6,7},{7,6},{8,9},{9,8},{10,11... | collective-permute-start | bytes 589832 | tf_op jit(solution)/shard_map/ppermute | solution.py:22
  71.7 1.7 %collective-permute-start.22 = (bf16[96,2048]{1,0:T(8,128)(2,1)S(1)}, bf16[96,2048]{1,0:T(8,128)(2,1)S(1)}, u32[]{:S(2)}, u32[]{:S(2)}) collective-permute-start(bf16[96,2048]{1,0:T(8,128)(2,1)S(1)} %get-tuple-element.126), channel_id=1, source_target_pairs={{0,1},{1,0},{2,3},{3,2},{4,5},{5,4},{6,7},{7,6},{8,9},{9,8},{10,11... | collective-permute-start | bytes 1179656 | tf_op jit(solution)/shard_map/ppermute | solution.py:22
  71.8 5.2 %collective-permute-start.24 = (bf16[192,2048]{1,0:T(8,128)(2,1)S(1)}, bf16[192,2048]{1,0:T(8,128)(2,1)S(1)}, u32[]{:S(2)}, u32[]{:S(2)}) collective-permute-start(bf16[192,2048]{1,0:T(8,128)(2,1)S(1)} %constant_dynamic-update-slice_fusion.2.refs_0_), channel_id=1, source_target_pairs={{0,1},{1,0},{2,3},{3,2},{4,5},{5,4},{6,7},{7,6},{8,9},{9,8},{10,11... | collective-permute-start | bytes 2359304 | tf_op jit(solution)/shard_map/ppermute | solution.py:22
  72.6 2.3 %collective-permute-start.25 = (bf16[48,2048]{1,0:T(8,128)(2,1)S(1)}, bf16[48,2048]{1,0:T(8,128)(2,1)S(1)}, u32[]{:S(2)}, u32[]{:S(2)}) collective-permute-start(bf16[48,2048]{1,0:T(8,128)(2,1)S(1)} %constant_dynamic-update-slice_fusion.refs_0_), channel_id=1, source_target_pairs={{0,1},{1,0},{2,3},{3,2},{4,5},{5,4},{6,7},{7,6},{8,9},{9,8},{10,11... | collective-permute-start | bytes 589832 | tf_op jit(solution)/shard_map/ppermute | solution.py:22
  72.7 2.5 %collective-permute-start.26 = (bf16[48,2048]{1,0:T(8,128)(2,1)S(1)}, bf16[48,2048]{1,0:T(8,128)(2,1)S(1)}, u32[]{:S(2)}, u32[]{:S(2)}) collective-permute-start(bf16[48,2048]{1,0:T(8,128)(2,1)S(1)} %collective-permute-done.19.refs_1_), channel_id=1, source_target_pairs={{0,1},{1,0},{2,3},{3,2},{4,5},{5,4},{6,7},{7,6},{8,9},{9,8},{10,11... | collective-permute-start | bytes 589832 | tf_op jit(solution)/shard_map/ppermute | solution.py:22
  73.6 7.0 %collective-permute-start.23 = (bf16[48,2048]{1,0:T(8,128)(2,1)S(1)}, bf16[48,2048]{1,0:T(8,128)(2,1)S(1)}, u32[]{:S(2)}, u32[]{:S(2)}) collective-permute-start(bf16[48,2048]{1,0:T(8,128)(2,1)S(1)} %slice.119), channel_id=1, source_target_pairs={{0,2},{1,3},{2,0},{3,1},{4,6},{5,7},{6,4},{7,5},{8,10},{9,11},{10,... | collective-permute-start | bytes 589832 | tf_op jit(solution)/shard_map/ppermute | solution.py:22
  76.8 3.9 %collective-permute-start.30 = (bf16[96,2048]{1,0:T(8,128)(2,1)S(1)}, bf16[96,2048]{1,0:T(8,128)(2,1)S(1)}, u32[]{:S(2)}, u32[]{:S(2)}) collective-permute-start(bf16[96,2048]{1,0:T(8,128)(2,1)S(1)} %get-tuple-element.144), channel_id=1, source_target_pairs={{0,1},{1,0},{2,3},{3,2},{4,5},{5,4},{6,7},{7,6},{8,9},{9,8},{10,11... | collective-permute-start | bytes 1179656 | tf_op jit(solution)/shard_map/ppermute | solution.py:22
  77.0 22.4 %copy-start.6 = (bf16[704,2048]{1,0:T(8,128)(2,1)S(1)}, bf16[704,2048]{1,0:T(8,128)(2,1)}, u32[]{:S(2)}) copy-start(bf16[704,2048]{1,0:T(8,128)(2,1)} %refs_4_.1) | copy-start | bytes 8650756
  80.6 4.5 %collective-permute-start.27 = (bf16[192,2048]{1,0:T(8,128)(2,1)S(1)}, bf16[192,2048]{1,0:T(8,128)(2,1)S(1)}, u32[]{:S(2)}, u32[]{:S(2)}) collective-permute-start(bf16[192,2048]{1,0:T(8,128)(2,1)S(1)} %get-tuple-element.142), channel_id=1, source_target_pairs={{0,1},{1,0},{2,3},{3,2},{4,5},{5,4},{6,7},{7,6},{8,9},{9,8},{10,11... | collective-permute-start | bytes 2359304 | tf_op jit(solution)/shard_map/ppermute | solution.py:22
  80.9 7.7 %collective-permute-start.31 = (bf16[48,2048]{1,0:T(8,128)(2,1)S(1)}, bf16[48,2048]{1,0:T(8,128)(2,1)S(1)}, u32[]{:S(2)}, u32[]{:S(2)}) collective-permute-start(bf16[48,2048]{1,0:T(8,128)(2,1)S(1)} %slice.132), channel_id=1, source_target_pairs={{0,2},{1,3},{2,0},{3,1},{4,6},{5,7},{6,4},{7,5},{8,10},{9,11},{10,... | collective-permute-start | bytes 589832 | tf_op jit(solution)/shard_map/ppermute | solution.py:22
  82.1 17.4 %copy-start.5 = (bf16[2048,704]{0,1:T(8,128)(2,1)S(1)}, bf16[2048,704]{0,1:T(8,128)(2,1)}, u32[]{:S(2)}) copy-start(bf16[2048,704]{0,1:T(8,128)(2,1)} %param.21) | copy-start | bytes 8650756
  82.1 12.9 %collective-permute-start.34 = (bf16[24,2048]{1,0:T(8,128)(2,1)S(1)}, bf16[24,2048]{1,0:T(8,128)(2,1)S(1)}, u32[]{:S(2)}, u32[]{:S(2)}) collective-permute-start(bf16[24,2048]{1,0:T(8,128)(2,1)S(1)} %get-tuple-element.161), channel_id=1, source_target_pairs={{0,16},{4,20},{8,24},{12,28},{16,0},{20,4},{24,8},{28,12},{1,17},{... | collective-permute-start | bytes 294920 | tf_op jit(solution)/shard_map/ppermute | solution.py:22
  82.9 14.4 %collective-permute-start.35 = (bf16[24,2048]{1,0:T(8,128)(2,1)S(1)}, bf16[24,2048]{1,0:T(8,128)(2,1)S(1)}, u32[]{:S(2)}, u32[]{:S(2)}) collective-permute-start(bf16[24,2048]{1,0:T(8,128)(2,1)S(1)} %get-tuple-element.160), channel_id=1, source_target_pairs={{0,20},{4,16},{8,28},{12,24},{16,4},{20,0},{24,12},{28,8},{1,21},{... | collective-permute-start | bytes 294920 | tf_op jit(solution)/shard_map/ppermute | solution.py:22
  85.5 14.0 %copy-start.4 = (bf16[2048,704]{0,1:T(8,128)(2,1)S(1)}, bf16[2048,704]{0,1:T(8,128)(2,1)}, u32[]{:S(2)}) copy-start(bf16[2048,704]{0,1:T(8,128)(2,1)} %param.20) | copy-start | bytes 8650756
  85.5 6.9 %collective-permute-start.29 = (bf16[48,2048]{1,0:T(8,128)(2,1)S(1)}, bf16[48,2048]{1,0:T(8,128)(2,1)S(1)}, u32[]{:S(2)}, u32[]{:S(2)}) collective-permute-start(bf16[48,2048]{1,0:T(8,128)(2,1)S(1)} %get-tuple-element.153), channel_id=1, source_target_pairs={{0,2},{1,3},{2,0},{3,1},{4,6},{5,7},{6,4},{7,5},{8,10},{9,11},{10,... | collective-permute-start | bytes 589832 | tf_op jit(solution)/shard_map/ppermute | solution.py:22
  88.6 13.5 %collective-permute-start.28 = (bf16[48,2048]{1,0:T(8,128)(2,1)S(1)}, bf16[48,2048]{1,0:T(8,128)(2,1)S(1)}, u32[]{:S(2)}, u32[]{:S(2)}) collective-permute-start(bf16[48,2048]{1,0:T(8,128)(2,1)S(1)} %get-tuple-element.154), channel_id=1, source_target_pairs={{0,4},{4,0},{8,12},{12,8},{16,20},{20,16},{24,28},{28,24},{1,5},{5... | collective-permute-start | bytes 589832 | tf_op jit(solution)/shard_map/ppermute | solution.py:22
  92.5 9.6 %collective-permute-start.32 = (bf16[24,2048]{1,0:T(8,128)(2,1)S(1)}, bf16[24,2048]{1,0:T(8,128)(2,1)S(1)}, u32[]{:S(2)}, u32[]{:S(2)}) collective-permute-start(bf16[24,2048]{1,0:T(8,128)(2,1)S(1)} %get-tuple-element.163), channel_id=1, source_target_pairs={{0,8},{4,12},{8,0},{12,4},{16,24},{20,28},{24,16},{28,20},{1,9},{5... | collective-permute-start | bytes 294920 | tf_op jit(solution)/shard_map/ppermute | solution.py:22
  93.6 8.5 %collective-permute-start.33 = (bf16[24,2048]{1,0:T(8,128)(2,1)S(1)}, bf16[24,2048]{1,0:T(8,128)(2,1)S(1)}, u32[]{:S(2)}, u32[]{:S(2)}) collective-permute-start(bf16[24,2048]{1,0:T(8,128)(2,1)S(1)} %get-tuple-element.162), channel_id=1, source_target_pairs={{0,12},{4,8},{8,4},{12,0},{16,28},{20,24},{24,20},{28,16},{1,13},{... | collective-permute-start | bytes 294920 | tf_op jit(solution)/shard_map/ppermute | solution.py:22
  95.0 7.3 %collective-permute-start.36 = (bf16[24,2048]{1,0:T(8,128)(2,1)S(1)}, bf16[24,2048]{1,0:T(8,128)(2,1)S(1)}, u32[]{:S(2)}, u32[]{:S(2)}) collective-permute-start(bf16[24,2048]{1,0:T(8,128)(2,1)S(1)} %get-tuple-element.159), channel_id=1, source_target_pairs={{0,24},{4,28},{8,16},{12,20},{16,8},{20,12},{24,0},{28,4},{1,25},{... | collective-permute-start | bytes 294920 | tf_op jit(solution)/shard_map/ppermute | solution.py:22
  97.3 7.4 %collective-permute-start.37 = (bf16[24,2048]{1,0:T(8,128)(2,1)S(1)}, bf16[24,2048]{1,0:T(8,128)(2,1)S(1)}, u32[]{:S(2)}, u32[]{:S(2)}) collective-permute-start(bf16[24,2048]{1,0:T(8,128)(2,1)S(1)} %get-tuple-element.158), channel_id=1, source_target_pairs={{0,28},{4,24},{8,20},{12,16},{16,12},{20,8},{24,4},{28,0},{1,29},{... | collective-permute-start | bytes 294920 | tf_op jit(solution)/shard_map/ppermute | solution.py:22
  105.4 1.6 %collective-permute-start.40 = (bf16[128,1024]{1,0:T(8,128)(2,1)S(1)}, bf16[128,1024]{1,0:T(8,128)(2,1)S(1)}, u32[]{:S(2)}, u32[]{:S(2)}) collective-permute-start(bf16[128,1024]{1,0:T(8,128)(2,1)S(1)} %get-tuple-element.152), channel_id=1, source_target_pairs={{0,1},{1,0},{2,3},{3,2},{4,5},{5,4},{6,7},{7,6},{8,9},{9,8},{10,11... | collective-permute-start | bytes 786440 | tf_op jit(solution)/shard_map/ppermute | solution.py:22
  105.5 2.8 %collective-permute-start.38 = (bf16[128,1024]{1,0:T(8,128)(2,1)S(1)}, bf16[128,1024]{1,0:T(8,128)(2,1)S(1)}, u32[]{:S(2)}, u32[]{:S(2)}) collective-permute-start(bf16[128,1024]{1,0:T(8,128)(2,1)S(1)} %get-tuple-element.150), channel_id=1, source_target_pairs={{0,1},{1,0},{2,3},{3,2},{4,5},{5,4},{6,7},{7,6},{8,9},{9,8},{10,11... | collective-permute-start | bytes 786440 | tf_op jit(solution)/shard_map/ppermute | solution.py:22
  107.1 6.4 %collective-permute-start.41 = (bf16[64,1024]{1,0:T(8,128)(2,1)S(1)}, bf16[64,1024]{1,0:T(8,128)(2,1)S(1)}, u32[]{:S(2)}, u32[]{:S(2)}) collective-permute-start(bf16[64,1024]{1,0:T(8,128)(2,1)S(1)} %slice.136), channel_id=1, source_target_pairs={{0,2},{1,3},{2,0},{3,1},{4,6},{5,7},{6,4},{7,5},{8,10},{9,11},{10,... | collective-permute-start | bytes 393224 | tf_op jit(solution)/shard_map/ppermute | solution.py:22
  108.3 7.2 %collective-permute-start.39 = (bf16[64,1024]{1,0:T(8,128)(2,1)S(1)}, bf16[64,1024]{1,0:T(8,128)(2,1)S(1)}, u32[]{:S(2)}, u32[]{:S(2)}) collective-permute-start(bf16[64,1024]{1,0:T(8,128)(2,1)S(1)} %slice.134), channel_id=1, source_target_pairs={{0,2},{1,3},{2,0},{3,1},{4,6},{5,7},{6,4},{7,5},{8,10},{9,11},{10,... | collective-permute-start | bytes 393224 | tf_op jit(solution)/shard_map/ppermute | solution.py:22
